TPU v7x, 256 devices: a whole 4x4x8 slice. The times are simulated.
256 devices in a mesh: gx: 16 (over z, core), gy: 16 (over y, x).
Axes of the slice: x: 4, y: 4, z: 8, core: 2. Of those that a mesh axis runs over, the one named last changes fastest.
Arguments:
- material: int32 [256, 256, 128], P('gx', 'gy'), may hold values from 0 to 7
- velocity: float32 [8], replicated, may hold values from 1.5 to 4.5
- density: float32 [8], replicated, may hold values from 1 to 2.2
- right_side: float32 [256, 256, 128], P('gx', 'gy'), may hold values from -24 to 24
Outputs:
- fine_solution: float32 [256, 256, 128], P('gx', 'gy')
- mid_solution: float32 [128, 128, 64], P('gx', 'gy')
- coarse_solution: float32 [64, 64, 32], P('gx', 'gy')
Inputs may be any that keep to these rules, and one draw needn't show every extreme that they name: Each cell's material selects its row of the velocity and density tables.
All inputs are finite; a program needn't handle non-finite values.
Results may differ from a plain program's by a relative error of at most 0.0003.
Values sent between devices are 32-bit elements; how exact they have to be, the bound alone decides.
No kernel may reach another device: no remote copies, remote signals or barrier semaphores. Data moves between devices by JAX's collectives and lax.ppermute only.
A program may use at most 128 MiB of HBM per device.

v0:
```python
import jax
import jax.numpy as jnp
from jax import lax
from jax.sharding import PartitionSpec as P

SWEEPS_FINE = 2
SWEEPS_MID = 2
SWEEPS_COARSE = 4


SHIFT_SCALE = 3.0
DAMPING = 0.7


def shifted(block, axis, distance):
    devices = range(lax.axis_size(axis))
    route = [(i - distance, i) for i in devices if i - distance in devices]
    return lax.ppermute(block, axis, route)


def extended(shard, sides, width):
    for axis, dim in sides:
        devices, length = (lax.axis_size(axis), shard.shape[dim])
        up = [(i, (i + 1) % devices) for i in range(devices - 1)]
        down = [(j, i) for i, j in up]
        last = lax.slice_in_dim(shard, length - width, length, axis=dim)
        first = lax.slice_in_dim(shard, 0, width, axis=dim)
        before = lax.ppermute(last, axis, up)
        after = lax.ppermute(first, axis, down)
        shard = jnp.concatenate([before, shard, after], axis=dim)
    return shard


def safe_divide(upper, lower):
    positive = lower > 0.0
    return jnp.where(positive, upper / jnp.where(positive, lower, 1.0), 0.0)


def harmonic(former, latter):
    return safe_divide(2.0 * former * latter, former + latter)


def look_up(material, table):
    picked = jnp.zeros(material.shape, table.dtype)
    for number in range(table.shape[0]):
        picked = jnp.where(material == number, table[number], picked)
    return picked


def neighbour(plane, dimension, offset):
    if dimension == 1:
        return shifted(plane, "gx", offset)
    if dimension == 2:
        return shifted(plane, "gy", offset)
    return jnp.zeros_like(plane)


def pad_depth(padded):
    return jnp.pad(padded, ((0, 0), (0, 0), (0, 0), (1, 1)))


def faces(current):
    return pad_depth(extended(current, (("gx", 1), ("gy", 2)), 1))


def rims(current):
    return pad_depth(extended(current, (("gx", 1), ("gy", 2)), 1))


def face_values(padded, shape):
    size_x, size_y, size_z = (shape[1], shape[2], shape[3])
    return [
        padded[:, 0:size_x, 1 : size_y + 1, 1 : size_z + 1],
        padded[:, 2 : size_x + 2, 1 : size_y + 1, 1 : size_z + 1],
        padded[:, 1 : size_x + 1, 0:size_y, 1 : size_z + 1],
        padded[:, 1 : size_x + 1, 2 : size_y + 2, 1 : size_z + 1],
        padded[:, 1 : size_x + 1, 1 : size_y + 1, 0:size_z],
        padded[:, 1 : size_x + 1, 1 : size_y + 1, 2 : size_z + 2],
    ]


def apply_fine(current, couplings, diagonal, padder):
    values = face_values(padder(current), current.shape)
    summed = couplings[0] * values[0]
    for number in range(1, 6):
        summed = summed + couplings[number] * values[number]
    return diagonal * current - summed


def stencil_sum(padded, stencil, shape):
    size_x, size_y, size_z = (shape[1], shape[2], shape[3])
    result = jnp.zeros(shape, jnp.float32)
    for offset in range(27):
        step_x, step_y, step_z = (offset // 9, offset // 3 % 3, offset % 3)
        result = (
            result
            + stencil[offset]
            * padded[
                :, step_x : step_x + size_x, step_y : step_y + size_y, step_z : step_z + size_z
            ]
        )
    return result


def line_weights(conductivity, dimension):
    moved = jnp.moveaxis(conductivity, dimension, 0)
    even_cells = moved[0::2]
    odd_cells = moved[1::2]
    before = neighbour(odd_cells[-1], dimension, 1)
    previous = jnp.concatenate([before[None], odd_cells[:-1]], 0)
    below = harmonic(even_cells, previous)
    above = harmonic(even_cells, odd_cells)
    summed = below + above
    return (
        jnp.moveaxis(safe_divide(below, summed), 0, dimension),
        jnp.moveaxis(safe_divide(above, summed), 0, dimension),
    )


def level_weights(conductivity):
    return [
        line_weights(conductivity[:, :, 1::2, 1::2], 1),
        line_weights(conductivity[:, :, :, 1::2], 2),
        line_weights(conductivity, 3),
    ]


def prolong(coarse, low_weight, high_weight, dimension):
    moved = jnp.moveaxis(coarse, dimension, 0)
    low_moved = jnp.moveaxis(low_weight, dimension, 0)
    high_moved = jnp.moveaxis(high_weight, dimension, 0)
    before = neighbour(moved[-1], dimension, 1)
    previous = jnp.concatenate([before[None], moved[:-1]], 0)
    between = low_moved * previous + high_moved * moved
    finer = jnp.stack([between, moved], 1).reshape((2 * moved.shape[0],) + moved.shape[1:])
    return jnp.moveaxis(finer, 0, dimension)


def restrict(finer, low_weight, high_weight, dimension):
    moved = jnp.moveaxis(finer, dimension, 0)
    low_moved = jnp.moveaxis(low_weight, dimension, 0)
    high_moved = jnp.moveaxis(high_weight, dimension, 0)
    pairs = moved.reshape((moved.shape[0] // 2, 2) + moved.shape[1:])
    between = pairs[:, 0]
    centres = pairs[:, 1]
    carried = low_moved * between
    after = neighbour(carried[0], dimension, -1)
    following = jnp.concatenate([carried[1:], after[None]], 0)
    return jnp.moveaxis(centres + high_moved * between + following, 0, dimension)


def prolong_all(coarse, weights):
    for number in range(3):
        coarse = prolong(coarse, weights[number][0], weights[number][1], number + 1)
    return coarse


def restrict_all(finer, weights):
    for number in (2, 1, 0):
        finer = restrict(finer, weights[number][0], weights[number][1], number + 1)
    return finer


def coarsen(conductivity):
    size_x, size_y, size_z = (conductivity.shape[1], conductivity.shape[2], conductivity.shape[3])
    blocks = conductivity.reshape(1, size_x // 2, 2, size_y // 2, 2, size_z // 2, 2)
    return jnp.mean(blocks, axis=(2, 4, 6))


def colour_masks(position, dtype):
    return jnp.stack(
        [
            jnp.stack([(position + offset - 1) % 3 == colour for colour in range(3)])
            for offset in range(3)
        ]
    ).astype(dtype)


def assemble(stacked, index_x, index_y, index_z):
    shape = stacked.shape[1:]
    blocks = stacked.reshape((3, 3, 3) + shape)
    mask_x = colour_masks(index_x, stacked.dtype)
    mask_y = colour_masks(index_y, stacked.dtype)
    mask_z = colour_masks(index_z, stacked.dtype)
    along_x = mask_x[:, 0][:, None, None, :, None, None] * blocks[0][None]
    for colour in (1, 2):
        along_x = along_x + mask_x[:, colour][:, None, None, :, None, None] * blocks[colour][None]
    along_y = mask_y[:, 0][None, :, None, None, :, None] * along_x[:, 0][:, None]
    for colour in (1, 2):
        along_y = (
            along_y + mask_y[:, colour][None, :, None, None, :, None] * along_x[:, colour][:, None]
        )
    along_z = mask_z[:, 0][None, None, :, None, None, :] * along_y[:, :, 0][:, :, None]
    for colour in (1, 2):
        along_z = (
            along_z
            + mask_z[:, colour][None, None, :, None, None, :] * along_y[:, :, colour][:, :, None]
        )
    return along_z.reshape((27,) + shape)


def galerkin(operate, weights, shape, first_x, first_y, limit_x, limit_y, group_size):
    index_x = first_x + jnp.arange(shape[0], dtype=jnp.int32)
    index_y = first_y + jnp.arange(shape[1], dtype=jnp.int32)
    index_z = jnp.arange(shape[2], dtype=jnp.int32)
    inside = ((index_x >= 0) & (index_x < limit_x))[:, None, None] & (
        (index_y >= 0) & (index_y < limit_y)
    )[None, :, None]

    def probe(colours):
        hits = (
            ((index_x % 3)[None, :, None, None] == (colours // 9)[:, None, None, None])
            & ((index_y % 3)[None, None, :, None] == (colours // 3 % 3)[:, None, None, None])
            & ((index_z % 3)[None, None, None, :] == (colours % 3)[:, None, None, None])
            & inside[None]
        )
        return restrict_all(operate(prolong_all(hits.astype(jnp.float32), weights)), weights)

    stacked = lax.map(probe, jnp.arange(27, dtype=jnp.int32).reshape(27 // group_size, group_size))
    return assemble(stacked.reshape((27,) + tuple(shape)), index_x, index_y, index_z)


def smooth(operate, diagonal, source, sweeps):
    current = DAMPING * (source / diagonal)
    for repeat in range(sweeps - 1):
        current = current + DAMPING * ((source - operate(current)) / diagonal)
    return current


def per_device(material, velocity, density, right_side):
    density_cell = look_up(material[None], density)
    velocity_cell = look_up(material[None], velocity)
    conductivity = 1.0 / density_cell
    shift_field = SHIFT_SCALE / (density_cell * velocity_cell * velocity_cell)
    count_x = lax.axis_size("gx")
    count_y = lax.axis_size("gy")
    row_x = lax.axis_index("gx")
    row_y = lax.axis_index("gy")
    group_mid, group_low = (3, 27)
    couplings = [
        harmonic(conductivity, other)
        for other in face_values(faces(conductivity), conductivity.shape)
    ]
    diagonal = shift_field
    for coupling in couplings:
        diagonal = diagonal + coupling
    weights_fine = level_weights(conductivity)
    conductivity_mid = coarsen(conductivity)
    weights_mid = level_weights(conductivity_mid)
    shape_mid = conductivity_mid.shape[1:]
    shape_low = (shape_mid[0] // 2, shape_mid[1] // 2, shape_mid[2] // 2)

    def probe_fine_operator(current):
        return apply_fine(current, couplings, diagonal, faces)

    stencil_mid = galerkin(
        probe_fine_operator,
        weights_fine,
        shape_mid,
        row_x * shape_mid[0],
        row_y * shape_mid[1],
        count_x * shape_mid[0],
        count_y * shape_mid[1],
        group_mid,
    )

    def probe_mid_operator(current):
        return stencil_sum(rims(current), stencil_mid, current.shape)

    stencil_low = galerkin(
        probe_mid_operator,
        weights_mid,
        shape_low,
        row_x * shape_low[0],
        row_y * shape_low[1],
        count_x * shape_low[0],
        count_y * shape_low[1],
        group_low,
    )

    def fine_operator(current):
        return apply_fine(current, couplings, diagonal, faces)

    def mid_operator(current):
        return stencil_sum(rims(current), stencil_mid, current.shape)

    source = right_side[None]
    fine_solution = smooth(fine_operator, diagonal, source, SWEEPS_FINE)
    source_mid = restrict_all(source - fine_operator(fine_solution), weights_fine)
    mid_solution = smooth(mid_operator, stencil_mid[13], source_mid, SWEEPS_MID)
    source_low = restrict_all(source_mid - mid_operator(mid_solution), weights_mid)

    def low_operator(current):
        return stencil_sum(rims(current), stencil_low, current.shape)

    coarse_solution = smooth(low_operator, stencil_low[13], source_low, SWEEPS_COARSE)
    return (fine_solution[0], mid_solution[0], coarse_solution[0])


def solution(mesh):
    return jax.shard_map(
        per_device,
        mesh=mesh,
        in_specs=(P("gx", "gy", None), P(), P(), P("gx", "gy", None)),
        out_specs=(P("gx", "gy", None), P("gx", "gy", None), P("gx", "gy", None)),
        check_vma=False,
    )
```

profile of v0, /device:TPU:1, one launch (start us, length us, event | category | flops | bytes accessed | tf_op | source)
XLA Modules:
  0.0 948.0 jit_solution(10423994270963002901)
XLA Ops:
  2.3 6.2 fusion.122
  31.0 9.7 %reshape.1430 = f32[8,2,8,2,64,2]{5,4,3,2,1,0:T(8,128)} reshape(f32[16,16,128]{2,1,0:T(8,128)S(1)} %get-tuple-element.736) | data formatting | bytes 262144 | tf_op jit(solution)/shard_map/reshape | solution.py:166
  60.4 11.6 %fusion.120 = (f32[1,16,16,128]{3,2,1,0:T(8,128)S(1)}, f32[1,16,16,128]{3,2,1,0:T(8,128)}, f32[1,16,16,128]{3,2,1,0:T(8,128)}, f32[1,16,16,128]{3,2,1,0:T(8,128)...) fusion(f32[16,16,128]{2,1,0:T(8,128)S(1)} %copy-done.3, ...), kind=kLoop, calls=%fused_computation.310 | loop fusion | flops 2359296 | bytes 2000960 | tf_op jit(solution)/shard_map/mul | solution.py:224
  132.6 564.8 %while.18 = (s32[]{:T(128)}, f32[9,3,8,8,64]{4,3,1,2,0:T(8,128)}, f32[1,16,16,128]{3,2,1,0:T(8,128)}, f32[64,1,16,16]{0,2,3,1:T(8,128)}, f32[8,1,16,64]{3,0,2,1:...) while((s32[]{:T(128)}, f32[9,3,8,8,64]{4,3,1,2,0:T(8,128)}, ...), condition=%wide.region_1.2_spmd.clone, body=%wide.region_0.1_spmd.clone.sunk | while | flops 4554826 | bytes 16401273 | solution.py:219
  177.9 5.5 collective-permute-done.6
  220.1 6.5 collective-permute-start.5
  240.2 5.8 collective-permute-done.6
  282.5 6.4 collective-permute-start.5
  302.4 5.8 collective-permute-done.6
  343.9 6.4 collective-permute-start.5
  363.8 5.8 collective-permute-done.6
  399.0 6.1 collective-permute-start.3
  407.5 6.4 collective-permute-start.5
  427.4 5.8 collective-permute-done.6
  462.6 6.1 collective-permute-start.3
  471.0 6.4 collective-permute-start.5
  490.9 5.8 collective-permute-done.6
  526.2 6.1 collective-permute-start.3
  534.6 6.4 collective-permute-start.5
  554.5 5.8 collective-permute-done.6
  589.7 6.1 collective-permute-start.3
  598.2 6.4 collective-permute-start.5
  618.1 5.8 collective-permute-done.6
  653.3 6.1 collective-permute-start.3
  661.7 6.4 collective-permute-start.5
  681.6 5.8 collective-permute-done.6
  737.7 6.1 collective-permute-start.30
  769.6 8.0 collective-permute-start.38
  851.2 20.5 %fusion.35 = f32[27,8,8,64]{0,2,1,3:T(8,128)S(1)} fusion(f32[27,10,10,66]{0,2,1,3:T(8,128)S(1)} %select_maximum_fusion.4, f32[27,10,9,64]{0,2,1,3:T(8,128)S(1)} %get-tuple-element.759, f32[27,1,8,64]{0,2,1,3:T(8,128)S(1)} %collective-permute-done.39, f32[27,8,8,64]{0,2,1,3:T(8,128)S(1)} %bitcast.806, f32[27,10,9,64]{0,2,1,3:T(8,128)S(1)} %get-tuple-element.758, ...), kind=kLoop, calls=%fused_computation.96 | loop fusion | flops 6082560 | bytes 12054528 | tf_op jit(solution)/shard_map/while/body/eval_jaxpr/add | solution.py:96
  875.9 6.1 collective-permute-done.42
  917.9 5.8 collective-permute-start.50
  937.1 5.5 collective-permute-start.54
  (1219 shorter events, 728.1 us)
Async XLA Ops:
  8.4 44.1 %collective-permute-start.8 = (f32[1,1,16,128]{3,2,1,0:T(8,128)S(1)}, f32[1,1,16,128]{3,2,1,0:T(8,128)S(1)}, u32[]{:S(2)}, u32[]{:S(2)}) collective-permute-start(f32[1,1,16,128]{3,2,1,0:T(8,128)S(1)} %get-tuple-element.836), channel_id=1, source_target_pairs={{0,16},{16,32},{32,48},{48,64},{64,80},{80,96},{96,112},{112,128},... | collective-permute-start | bytes 24584 | tf_op jit(solution)/shard_map/ppermute | solution.py:28
  13.4 39.1 %collective-permute-start.9 = (f32[1,1,16,128]{3,2,1,0:T(8,128)S(1)}, f32[1,1,16,128]{3,2,1,0:T(8,128)S(1)}, u32[]{:S(2)}, u32[]{:S(2)}) collective-permute-start(f32[1,1,16,128]{3,2,1,0:T(8,128)S(1)} %get-tuple-element.835), channel_id=1, source_target_pairs={{16,0},{32,16},{48,32},{64,48},{80,64},{96,80},{112,96},{128,112},... | collective-permute-start | bytes 24584 | tf_op jit(solution)/shard_map/ppermute | solution.py:29
  17.7 108.3 %collective-permute-start.20 = (f32[1,16,64]{2,1,0:T(8,128)S(1)}, f32[1,16,64]{2,1,0:T(8,128)S(1)}, u32[]{:S(2)}, u32[]{:S(2)}) collective-permute-start(f32[1,16,64]{2,1,0:T(8,128)S(1)} %bitcast.903), channel_id=1, source_target_pairs={{0,1},{1,2},{2,3},{3,4},{4,5},{5,6},{6,7},{7,8},{8,9},{9,10},{10,1... | collective-permute-start | bytes 12296 | tf_op jit(solution)/shard_map/ppermute | solution.py:18
  22.0 106.0 %collective-permute-start.22 = (f32[1,8,64]{2,1,0:T(8,128)S(1)}, f32[1,8,64]{2,1,0:T(8,128)S(1)}, u32[]{:S(2)}, u32[]{:S(2)}) collective-permute-start(f32[1,8,64]{2,1,0:T(8,128)S(1)} %slice_bitcast_fusion.57), channel_id=1, source_target_pairs={{0,16},{16,32},{32,48},{48,64},{64,80},{80,96},{96,112},{112,128},... | collective-permute-start | bytes 6152 | tf_op jit(solution)/shard_map/ppermute | solution.py:18
  97.7 18.4 %collective-permute-start.18 = (f32[1,18,1,128]{3,2,1,0:T(1,128)S(1)}, f32[1,18,1,128]{3,2,1,0:T(1,128)S(1)}, u32[]{:S(2)}, u32[]{:S(2)}) collective-permute-start(f32[1,18,1,128]{3,2,1,0:T(1,128)S(1)} %get-tuple-element.823), channel_id=1, source_target_pairs={{0,1},{1,2},{2,3},{3,4},{4,5},{5,6},{6,7},{7,8},{8,9},{9,10},{10,1... | collective-permute-start | bytes 27656 | tf_op jit(solution)/shard_map/ppermute | solution.py:28
  102.4 16.8 %collective-permute-start.19 = (f32[1,18,1,128]{3,2,1,0:T(1,128)S(1)}, f32[1,18,1,128]{3,2,1,0:T(1,128)S(1)}, u32[]{:S(2)}, u32[]{:S(2)}) collective-permute-start(f32[1,18,1,128]{3,2,1,0:T(1,128)S(1)} %get-tuple-element.824), channel_id=1, source_target_pairs={{1,0},{2,1},{3,2},{4,3},{5,4},{6,5},{7,6},{8,7},{9,8},{10,9},{11,1... | collective-permute-start | bytes 27656 | tf_op jit(solution)/shard_map/ppermute | solution.py:29
  111.2 633.9 %collective-permute-start.32 = (f32[1,8,32]{2,1,0:T(8,128)}, f32[1,8,32]{2,1,0:T(8,128)}, u32[]{:S(2)}, u32[]{:S(2)}) collective-permute-start(f32[1,8,32]{2,1,0:T(8,128)} %bitcast.91), channel_id=1, source_target_pairs={{0,1},{1,2},{2,3},{3,4},{4,5},{5,6},{6,7},{7,8},{8,9},{9,10},{10,1... | collective-permute-start | bytes 3080 | tf_op jit(solution)/shard_map/ppermute | solution.py:18
  116.1 634.9 %collective-permute-start.34 = (f32[1,4,32]{2,1,0:T(4,128)}, f32[1,4,32]{2,1,0:T(4,128)}, u32[]{:S(2)}, u32[]{:S(2)}) collective-permute-start(f32[1,4,32]{2,1,0:T(4,128)} %slice_bitcast_fusion.59), channel_id=1, source_target_pairs={{0,16},{16,32},{32,48},{48,64},{64,80},{80,96},{96,112},{112,128},... | collective-permute-start | bytes 1544 | tf_op jit(solution)/shard_map/ppermute | solution.py:18
  122.3 634.5 %collective-permute-start.36 = (f32[27,4,32]{2,1,0:T(4,128)}, f32[27,4,32]{2,1,0:T(4,128)}, u32[]{:S(2)}, u32[]{:S(2)}) collective-permute-start(f32[27,4,32]{2,1,0:T(4,128)} %slice_bitcast_fusion.23), channel_id=1, source_target_pairs={{0,16},{16,32},{32,48},{48,64},{64,80},{80,96},{96,112},{112,128},... | collective-permute-start | bytes 41480 | tf_op jit(solution)/shard_map/while/body/eval_jaxpr/ppermute | solution.py:18
  218.8 9.5 %collective-permute-start.4 = (f32[3,18,1,128]{3,2,1,0:T(1,128)S(1)}, f32[3,18,1,128]{3,2,1,0:T(1,128)S(1)}, u32[]{:S(2)}, u32[]{:S(2)}) collective-permute-start(f32[3,18,1,128]{3,2,1,0:T(1,128)S(1)} %get-tuple-element.1096), channel_id=1, source_target_pairs={{1,0},{2,1},{3,2},{4,3},{5,4},{6,5},{7,6},{8,7},{9,8},{10,9},{11,1... | collective-permute-start | bytes 82952 | tf_op jit(solution)/shard_map/while/body/eval_jaxpr/ppermute | solution.py:29
  220.1 8.2 collective-permute-start.5
  281.2 9.3 collective-permute-start.4
  282.5 8.1 collective-permute-start.5
  342.6 9.3 collective-permute-start.4
  343.9 8.1 collective-permute-start.5
  396.3 8.9 collective-permute-start.2
  406.2 9.3 collective-permute-start.4
  407.5 8.1 collective-permute-start.5
  459.9 8.9 collective-permute-start.2
  469.7 9.3 collective-permute-start.4
  471.0 8.1 collective-permute-start.5
  523.5 8.9 collective-permute-start.2
  533.3 9.3 collective-permute-start.4
  587.0 8.9 collective-permute-start.2
  596.9 9.3 collective-permute-start.4
  650.6 8.9 collective-permute-start.2
  660.4 9.3 collective-permute-start.4
  737.7 8.2 collective-permute-start.30
  769.6 28.5 %collective-permute-start.38 = (f32[27,1,8,64]{0,2,1,3:T(8,128)}, f32[27,1,8,64]{0,2,1,3:T(8,128)S(1)}, u32[]{:S(2)}, u32[]{:S(2)}) collective-permute-start(f32[27,1,8,64]{0,2,1,3:T(8,128)} %get-tuple-element.764), channel_id=1, source_target_pairs={{0,16},{16,32},{32,48},{48,64},{64,80},{80,96},{96,112},{112,128},... | collective-permute-start | bytes 165896 | tf_op jit(solution)/shard_map/while/body/eval_jaxpr/ppermute | solution.py:28
  777.6 20.5 %collective-permute-start.39 = (f32[27,1,8,64]{0,2,1,3:T(8,128)}, f32[27,1,8,64]{0,2,1,3:T(8,128)S(1)}, u32[]{:S(2)}, u32[]{:S(2)}) collective-permute-start(f32[27,1,8,64]{0,2,1,3:T(8,128)} %get-tuple-element.765), channel_id=1, source_target_pairs={{16,0},{32,16},{48,32},{64,48},{80,64},{96,80},{112,96},{128,112},... | collective-permute-start | bytes 165896 | tf_op jit(solution)/shard_map/while/body/eval_jaxpr/ppermute | solution.py:29
  799.4 44.9 %collective-permute-start.40 = (f32[27,10,1,64]{0,2,1,3:T(1,128)}, f32[27,10,1,64]{0,2,1,3:T(1,128)}, u32[]{:S(2)}, u32[]{:S(2)}) collective-permute-start(f32[27,10,1,64]{0,2,1,3:T(1,128)} %get-tuple-element.760), channel_id=1, source_target_pairs={{0,1},{1,2},{2,3},{3,4},{4,5},{5,6},{6,7},{7,8},{8,9},{9,10},{10,1... | collective-permute-start | bytes 207368 | tf_op jit(solution)/shard_map/while/body/eval_jaxpr/ppermute | solution.py:28
  804.2 40.1 %collective-permute-start.41 = (f32[27,10,1,64]{0,2,1,3:T(1,128)}, f32[27,10,1,64]{0,2,1,3:T(1,128)}, u32[]{:S(2)}, u32[]{:S(2)}) collective-permute-start(f32[27,10,1,64]{0,2,1,3:T(1,128)} %get-tuple-element.761), channel_id=1, source_target_pairs={{1,0},{2,1},{3,2},{4,3},{5,4},{6,5},{7,6},{8,7},{9,8},{10,9},{11,1... | collective-permute-start | bytes 207368 | tf_op jit(solution)/shard_map/while/body/eval_jaxpr/ppermute | solution.py:29
  (240 other events, 2401.4 us)
where the time goes:
time: 965 us; the launch traced here: 948 us
  starting transfers between devices  367 us (38%)
  local copies, waits for them, and re-layouts  203 us (21%)
  other arithmetic  188 us (19%)
  waiting for transfers between devices  183 us (19%)
    ppermute x36, starting transfers between devices, extended(): before = lax.ppermute(last, axis, up)  184 us
    ppermute x48, waiting for transfers between devices, shifted(): return lax.ppermute(block, axis, route)  130 us
    ppermute x48, starting transfers between devices, shifted(): return lax.ppermute(block, axis, route)  118 us
    ppermute x36, starting transfers between devices, extended(): after = lax.ppermute(first, axis, down)  65.2 us
    ppermute x36, waiting for transfers between devices, extended(): after = lax.ppermute(first, axis, down)  44.9 us
    squeeze x21, local copies, waits for them, and re-layouts, restrict(): between = pairs[:, 0]  38.2 us
    mul x28, local copies, waits for them, and re-layouts, stencil_sum(): stencil[offset]  37.4 us
    another operation x50, other arithmetic, prolong(): jnp.stack([between, moved], 1)  29.5 us
  transfers between devices with their start and end apart: 120, of which 66 were waited for; matrix products, arithmetic and copies ran while one was open for 36% of the time, Pallas kernels for 0%

commit v1 on v0

v1 whole, which is shorter than its diff:
```python
import jax
import jax.numpy as jnp
from jax import lax
from jax.experimental import pallas as pl
from jax.experimental.pallas import tpu as pltpu
from jax.sharding import PartitionSpec as P

DAMP = 0.7
F32 = jnp.float32
LOW, HIGH = 7, 10
X0 = LOW
ROWS = LOW + 16 + HIGH
HALF = ((0, 0), (0, 1), (1, -1), (1, 0), (1, 1))
FULL = tuple((dy, dz) for dy in (-1, 0, 1) for dz in (-1, 0, 1))
HI = lax.Precision.HIGHEST


def neg(s):
    return (-s[0], -s[1])


def shift(v, dy, dz, sy=1, sz=1):
    rows, lanes = v.shape
    if dy:
        v = pltpu.roll(v, (-dy * sy) % rows, 0)
    if dz:
        v = pltpu.roll(v, (-dz * sz) % lanes, 1)
    return v


def iota(shape, dim):
    return lax.broadcasted_iota(jnp.int32, shape, dim)


def depth_order(transposed):
    z = iota((128, 128), 1 if transposed else 0)
    c = iota((128, 128), 0 if transposed else 1)
    source = jnp.where(c < 64, 2 * c, 2 * c - 127)
    return jnp.where(z == source, 1.0, 0.0).astype(F32)


def pack_kernel(mat_ref, rhs_ref, mid_ref, low_ref, high_ref, fl_ref):
    fl_ref[...] = mat_ref[...].astype(F32)
    order = depth_order(False)
    for q, ref in ((0, fl_ref), (2, rhs_ref)):
        for parity in range(2):
            part = ref[:, pl.ds(parity, 8, stride=2), :].reshape(128, 128)
            part = jnp.dot(part, order, precision=HI, preferred_element_type=F32)
            part = part.reshape(16, 8, 128)
            mid_ref[:, q + parity] = part
            low_ref[:, q + parity] = part[16 - LOW :]
            high_ref[:, q + parity] = part[:HIGH]


def pick(index, table):
    b0 = (index & 1) == 1
    b1 = (index & 2) == 2
    b2 = (index & 4) == 4
    q = [jnp.where(b0, table[2 * n + 1], table[2 * n]) for n in range(4)]
    q = [jnp.where(b1, q[2 * n + 1], q[2 * n]) for n in range(2)]
    return jnp.where(b2, q[1], q[0])


def collapse_line(tm, t0, tp, l, lc, move, want):
    h, hc = 1.0 - l, 1.0 - lc
    out = {}
    hcp = move(hc, 1)
    lcm = move(lc, -1)
    if 0 in want:
        low = move(h * (hc * t0 + tp), -1)
        high = move(l * (lc * t0 + tm), 1)
        out[0] = t0 + low + high + tm * move(hc, -1) + tp * move(lc, 1)
    if 1 in want:
        out[1] = move(l * (hc * t0 + tp), 1) + tp * hcp
    if -1 in want:
        out[-1] = move(h * (lc * t0 + tm), -1) + tm * lcm
    return out


def collapse_rows(d0, d1, d2, c0, c1, c2, a0, a2, sy, sz, upper):
    h0 = 1.0 - a0
    diag, up = {}, {}
    for s in HALF:
        a2s = shift(a2, *s, sy, sz)
        h0s = 1.0 - shift(a0, *s, sy, sz)
        t10 = shift(c0[neg(s)], *s, sy, sz)
        t21 = shift(c1[neg(s)], *s, sy, sz)
        diag[s] = (
            d1[s]
            + h0 * (h0s * d0[s] + c0[s])
            + h0s * t10
            + a2 * (a2s * d2[s] + t21)
            + a2s * c1[s]
        )
    if upper:
        for s in FULL:
            h2s = 1.0 - shift(a2, *s, sy, sz)
            d2s = d2[s] if s in HALF else shift(d2[neg(s)], *s, sy, sz)
            up[s] = a2 * (h2s * d2s + c2[s]) + h2s * c1[s]
    return diag, up


def apply27(e0, e1, e1_before, u_before, u, u_after):
    total = e0[(0, 0)] * u
    back = {}
    for dy in (-1, 0, 1):
        for dz in (-1, 0, 1):
            s = (dy, dz)
            total = total + e1[s] * shift(u_after, dy, dz)
            if s in HALF and s != (0, 0):
                total = total + e0[s] * shift(u, dy, dz)
    for dy in (-1, 0, 1):
        row = None
        for dz in (-1, 0, 1):
            s = (dy, dz)
            product = e1_before[s] * u_before
            if s in HALF and s != (0, 0):
                product = product + e0[s] * u
            product = shift(product, 0, -dz)
            row = product if row is None else row + product
        total = total + shift(row, -dy, 0)
    return total


def halves(n, shape):
    return iota(shape, 1) < n


def main_kernel(tab_ref, pos_ref, *refs):
    ins = refs[:9]
    fine_ref, mid_ref, low_ref = refs[9:12]
    (D, S, B, OP, CX, CYE, CYO, CZL, CZU, WZ, WY, DG, DI, U1, U2, T, AL, SM, CM,
     WZP, WYP, C0, C1, E0, E1, UM, UN, Z0, Z1, L15, CMP) = refs[12:]
    sh = (16, 128)
    lane = iota(sh, 1)
    subl = iota(sh, 0)
    lt64 = lane < 64
    x_first = pos_ref[0] == 0
    x_last = pos_ref[1] == 1
    y_first = pos_ref[2] == 0
    y_last = pos_ref[3] == 1
    yc = jnp.where(y_first, 0, -1)
    yd = jnp.where(y_last, 8, -1)
    keep_y = jnp.where((subl == yc) | (subl == yd), 0.0, 1.0)
    keep_zl = jnp.where(lane == 0, 0.0, 1.0)
    keep_zu = jnp.where(lane == 127, 0.0, 1.0)
    keep_wz = jnp.where((lane == 0) | (lane >= 64), 0.0, 1.0)

    def keep_x(x):
        cut = (x_first & (x == 0)) | (x_last & (x == 16))
        return jnp.where(cut, 0.0, 1.0).astype(F32)

    def r64(v):
        return pltpu.roll(v, 64, 1)

    def z_lower(v):
        return jnp.where(lt64, pltpu.roll(v, 65, 1), r64(v))

    def z_upper(v):
        return jnp.where(lt64, r64(v), pltpu.roll(v, 63, 1))

    def y_next(v):
        return pltpu.roll(v, 15, 0)

    def y_prev(v):
        return pltpu.roll(v, 1, 0)

    tsh = (8, 128)
    den = [jnp.full(tsh, tab_ref[n], F32) for n in range(8)]
    vel = [jnp.full(tsh, tab_ref[8 + n], F32) for n in range(8)]
    sft = [3.0 / (d * v * v) for d, v in zip(den, vel)]
    s8 = iota(tsh, 0)

    def segment(first, count, own, above, below):
        def body(i, _):
            r = first + i
            for p in range(2):
                m0 = own[i, p].astype(jnp.int32)
                mb = below[i, p].astype(jnp.int32)
                m1 = jnp.where(s8 < 5, above[i, p].astype(jnp.int32), mb)
                d0, d1 = pick(m0, den), pick(m1, den)
                D[r, p, 0:8] = d0
                D[r, p, 8:16] = d1
                S[r, p, 0:8] = pick(m0, sft)
                S[r, p, 8:16] = pick(m1, sft)
                B[r, p, 0:8] = own[i, 2 + p]
                B[r, p, 8:16] = jnp.where(s8 < 5, above[i, 2 + p], below[i, 2 + p])
                if p == 1:
                    dd = y_prev(jnp.concatenate([d0, d1], 0))
                    OP[r, 0:8] = dd[0:8]
                    OP[r, 8:16] = jnp.where(s8 == 5, pltpu.roll(pick(mb, den), 1, 0), dd[8:16])
            return 0

        lax.fori_loop(0, count, body, 0)

    segment(0, LOW, ins[0], ins[1], ins[2])
    segment(LOW, 16, ins[3], ins[4], ins[5])
    segment(LOW + 16, HIGH, ins[6], ins[7], ins[8])

    def x_coupling(r, p):
        return keep_x(r - X0) * 2.0 / (D[r, p] + D[r - 1, p])

    for p in range(2):
        CX[1, p] = x_coupling(1, p)

    def coefficients(r, _):
        de, do, op = D[r, 0], D[r, 1], OP[r]
        sy_m, sy_p = de + op, de + do
        cye = keep_y * 2.0 / sy_m
        cyo = 2.0 / sy_p
        CYE[r] = cye
        CYO[r] = cyo
        WY[r] = keep_y * sy_p / (sy_m + sy_p)
        for p in range(2):
            d = D[r, p]
            lo, up = d + z_lower(d), d + z_upper(d)
            czl = keep_zl * 2.0 / lo
            czu = keep_zu * 2.0 / up
            CZL[r, p] = czl
            CZU[r, p] = czu
            WZ[r, p] = keep_wz * up / (lo + up)
            cxu = x_coupling(r + 1, p)
            CX[r + 1, p] = cxu
            ylo, yup = (cye, cyo) if p == 0 else (cyo, y_next(cye))
            diag = S[r, p] + CX[r, p] + cxu + ylo + yup + czl + czu
            DG[r, p] = diag
            di = DAMP / diag
            DI[r, p] = di
            U1[r, p] = di * B[r, p]
        return 0

    lax.fori_loop(1, ROWS - 1, coefficients, 0)

    def neighbours(U, r):
        e, o = U[r, 0], U[r, 1]
        cye, cyo = CYE[r], CYO[r]
        out = []
        for p in range(2):
            u = (e, o)[p]
            if p == 0:
                along_y = cye * y_prev(o) + cyo * o
            else:
                along_y = cyo * e + y_next(cye * e)
            out.append(
                CX[r, p] * U[r - 1, p]
                + CX[r + 1, p] * U[r + 1, p]
                + along_y
                + CZL[r, p] * z_lower(u)
                + CZU[r, p] * z_upper(u)
            )
        return out

    def second(r, _):
        around = neighbours(U1, r)
        for p in range(2):
            U2[r, p] = U1[r, p] + DI[r, p] * ((1.0 - DAMP) * B[r, p] + around[p])
        return 0

    lax.fori_loop(2, ROWS - 2, second, 0)
    order = depth_order(True)
    for p in range(2):
        part = U2[X0 : X0 + 16, p, 0:8].reshape(128, 128)
        part = jnp.dot(part, order, precision=HI, preferred_element_type=F32)
        fine_ref[:, pl.ds(p, 8, stride=2), :] = part.reshape(16, 8, 128)

    def residual(r, _):
        around = neighbours(U2, r)
        t = []
        for p in range(2):
            v = B[r, p] - DG[r, p] * U2[r, p] + around[p]
            wl = WZ[r, p]
            lowered = wl * v
            t.append(v + r64(v - lowered) + pltpu.roll(lowered, 63, 1))
        wy = WY[r]
        te = t[0] * wy
        T[r] = t[1] + (t[0] - te) + y_next(te)
        return 0

    lax.fori_loop(3, ROWS - 3, residual, 0)

    def x_weights(n, _):
        r = 3 + 2 * n
        d = D[r, 1]
        lo, up = d + D[r - 1, 1], d + D[r + 1, 1]
        AL[n] = keep_x(r - X0) * up / (lo + up)
        return 0

    lax.fori_loop(0, 14, x_weights, 0)

    def restrict_x(n, _):
        r = 3 + 2 * n
        SM[n] = T[r + 1] + (1.0 - AL[n]) * T[r] + AL[n + 1] * T[r + 2]
        return 0

    lax.fori_loop(0, 13, restrict_x, 0)

    def mean_mid(n, _):
        r = 3 + 2 * n
        total = 1.0 / D[r, 0] + 1.0 / D[r, 1] + 1.0 / D[r + 1, 0] + 1.0 / D[r + 1, 1]
        CM[n] = 0.125 * (total + r64(total))
        return 0

    lax.fori_loop(0, 13, mean_mid, 0)

    def even_part(qa, qb):
        return jnp.where(lt64, qa, r64(qb))

    def odd_part(qa, qb):
        return jnp.where(lt64, r64(qa), qb)

    def pair_weights(n, _):
        r = 3 + n
        for p in range(2):
            WZP[n, p] = even_part(WZ[r, p], WZ[r + 12, p])
        WYP[n] = odd_part(WY[r], WY[r + 12])
        return 0

    lax.fori_loop(0, 16, pair_weights, 0)

    def z1(v):
        return pltpu.roll(v, 127, 1)

    def z_collapse_lateral(c_e, c_o, wa, wb):
        ha, hb = 1.0 - wa, 1.0 - wb
        wc = wa * c_e
        return {
            0: c_o + ha * hb * c_e + z1(wc * wb),
            1: z1(wc * hb),
            -1: (c_e - wc) * wb,
        }

    def build(n, _):
        r = 3 + n
        q = r + 12
        cen, xup = [], []
        for p in range(2):
            wl = WZP[n, p]
            wh = 1.0 - wl
            dge, dgo = even_part(DG[r, p], DG[q, p]), odd_part(DG[r, p], DG[q, p])
            cze, czo = -even_part(CZL[r, p], CZL[q, p]), -odd_part(CZL[r, p], CZL[q, p])
            wd = wl * dge
            c = dgo + wh * (wh * dge + 2.0 * czo) + z1(wl * (wd + 2.0 * cze))
            m = wh * (wd + cze) + wl * czo
            cen.append({-1: m, 0: c, 1: z1(m)})
            cxe = -even_part(CX[r + 1, p], CX[q + 1, p])
            cxo = -odd_part(CX[r + 1, p], CX[q + 1, p])
            xup.append(z_collapse_lateral(cxe, cxo, wl, WZP[n + 1, p]))
        we, wo = WZP[n, 0], WZP[n, 1]
        F = z_collapse_lateral(-even_part(CYO[r], CYO[q]), -odd_part(CYO[r], CYO[q]), we, wo)
        H = z_collapse_lateral(-even_part(CYE[r], CYE[q]), -odd_part(CYE[r], CYE[q]), we, y_prev(wo))
        vl = WYP[n]
        vh = 1.0 - vl
        ul = WYP[n + 1]
        be, bo = cen
        vls = {d: shift(vl, 0, d) for d in (-1, 0, 1)}
        vhs = {d: 1.0 - vls[d] for d in (-1, 0, 1)}
        uls = {d: shift(ul, 0, d) for d in (-1, 0, 1)}
        uhs = {d: 1.0 - uls[d] for d in (-1, 0, 1)}
        Ht = {d: shift(H[-d], 0, d) for d in (-1, 0, 1)}
        Ft = {d: shift(F[-d], 0, d) for d in (0, 1)}
        for d in (0, 1):
            C0[n, HALF.index((0, d))] = (
                bo[d]
                + vh * (vhs[d] * be[d] + F[d])
                + vhs[d] * Ft[d]
                + y_next(vl * (vls[d] * be[d] + H[d]) + vls[d] * Ht[d])
            )
        for d in (-1, 0, 1):
            C0[n, HALF.index((1, d))] = y_next(vl * (vhs[d] * be[d] + F[d]) + vhs[d] * Ht[d])
        xe, xo = xup
        for d in (-1, 0, 1):
            lx = vl * xe[d]
            hx = xe[d] - lx
            C1[n, FULL.index((0, d))] = xo[d] + hx * uhs[d] + y_next(lx * uls[d])
            C1[n, FULL.index((1, d))] = y_next(lx * uhs[d])
            C1[n, FULL.index((-1, d))] = hx * uls[d]
        return 0

    lax.fori_loop(0, 15, build, 0)

    def half_of(ref, n):
        return {s: ref[n, j] for j, s in enumerate(HALF)}

    def full_of(ref, n):
        return {s: ref[n, j] for j, s in enumerate(FULL)}

    def join6(n, ref):
        return odd_part(ref[n], ref[n + 6])

    def first_dim(a, _):
        n = 2 * a
        diag, up = collapse_rows(
            half_of(C0, n), half_of(C0, n + 1), half_of(C0, n + 2),
            full_of(C1, n), full_of(C1, n + 1), full_of(C1, n + 2),
            join6(a, AL), join6(a + 1, AL), 1, 1, True,
        )
        for j, s in enumerate(HALF):
            E0[a, j] = diag[s]
        for j, s in enumerate(FULL):
            E1[a + 1, j] = up[s]
        return 0

    for j in range(9):
        C1[15, j] = jnp.zeros(sh, F32)
        C1[14, j] = jnp.zeros(sh, F32)
    lax.fori_loop(0, 7, first_dim, 0)
    for j in range(9):
        E1[0, j] = r64(E1[6, j])
        E1[7, j] = r64(E1[1, j])

    def mid_first(a, _):
        UM[a + 1] = DAMP * join6(a, SM) / E0[a, 0]
        return 0

    lax.fori_loop(0, 7, mid_first, 0)
    UM[0] = r64(UM[6])
    UM[8] = r64(UM[2])

    def a1(U, a):
        return apply27(half_of(E0, a), full_of(E1, a + 1), full_of(E1, a), U[a], U[a + 1], U[a + 2])

    def mid_second(a, _):
        UN[a + 1] = UM[a + 1] + DAMP * ((join6(a, SM) - a1(UM, a)) / E0[a, 0])
        return 0

    lax.fori_loop(0, 7, mid_second, 0)
    UN[0] = r64(UN[6])
    UN[8] = r64(UN[2])
    for i in range(4):
        mid_ref[i] = UN[i + 3, 0:8, 0:64]
        mid_ref[i + 4] = r64(UN[i + 1])[0:8, 0:64]

    def mid_residual(a, _):
        UM[a + 1] = join6(a, SM) - a1(UN, a)
        return 0

    lax.fori_loop(0, 7, mid_residual, 0)

    def at(b, ref, j=None):
        if j is None:
            return jnp.where(lt64, ref[b + 2], ref[b])
        return jnp.where(lt64, ref[b + 2, j], ref[b, j])

    def at1(b, j=None):
        if j is None:
            return jnp.where(lt64, UM[b + 3], UM[b + 1])
        return jnp.where(lt64, E1[b + 3, j], E1[b + 1, j])

    def cm(b):
        return jnp.where(lt64, CM[b + 2], CM[b + 6])

    edge_z = jnp.where((lane == 0) | (lane == 64), 0.0, 1.0)

    def weight(g, before, after, keep):
        lo, up = before * (g + after), after * (g + before)
        return keep * lo / (lo + up)

    def mid_z(b):
        g = cm(b)
        return weight(g, pltpu.roll(g, 1, 1), pltpu.roll(g, 127, 1), edge_z)

    def mid_y(b):
        g = cm(b)
        return weight(g, y_prev(g), y_next(g), keep_y)

    def mid_x(b):
        ka = jnp.where(x_first & (b == 0), 0.0, 1.0).astype(F32)
        kb = jnp.where(x_last & (b == 4), 0.0, 1.0).astype(F32)
        return weight(cm(b), cm(b - 1), cm(b + 1), jnp.where(lt64, ka, kb))

    def move_z(v, n):
        return shift(v, 0, n)

    def move_y(v, n):
        return shift(v, n, 0)

    def build_low(b, _):
        e0 = {s: at(b, E0, j) for j, s in enumerate(HALF)}
        e1 = {s: at1(b, j) for j, s in enumerate(FULL)}
        lz = (mid_z(b), mid_z(b + 1))
        z0, zz1 = {}, {}
        for dx in (0, 1):
            source, out = ((e0, z0), (e1, zz1))[dx]
            for dy in (-1, 0, 1):
                if dx == 0 and dy == -1:
                    continue
                lc = move_y(lz[dx], dy)
                if dx == 0 and dy == 0:
                    t0, tp = source[(0, 0)], source[(0, 1)]
                    tm = move_z(tp, -1)
                    want = (0, 1)
                else:
                    tm, t0, tp = (source[(dy, d)] for d in (-1, 0, 1))
                    want = (-1, 0, 1)
                for d, v in collapse_line(tm, t0, tp, lz[0], lc, move_z, want).items():
                    out[(dy, d)] = v
        ly = (mid_y(b), mid_y(b + 1))
        for d in (-1, 0, 1):
            lc = shift(ly[0], 0, d, 1, 2)
            want = (0, 1) if d >= 0 else (1,)
            t0 = z0[(0, d)] if d >= 0 else shift(z0[(0, 1)], 0, -1, 1, 2)
            tp = z0[(1, d)]
            tm = shift(z0[(1, -d)], -1, d, 1, 2)
            for dy, v in collapse_line(tm, t0, tp, ly[0], lc, move_y, want).items():
                Z0[b, HALF.index((dy, d))] = v
            lc = shift(ly[1], 0, d, 1, 2)
            tm, t0, tp = (zz1[(dy, d)] for dy in (-1, 0, 1))
            for dy, v in collapse_line(tm, t0, tp, ly[0], lc, move_y, (-1, 0, 1)).items():
                Z1[b, FULL.index((dy, d))] = v
        v = at1(b)
        lv = lz[0] * v
        v = v + move_z(v - lv, -1) + move_z(lv, 1)
        lv = ly[0] * v
        UN[b] = v + move_y(v - lv, -1) + move_y(lv, 1)
        return 0

    lax.fori_loop(0, 5, build_low, 0)

    def low_rows(i, _):
        b = 2 * i
        w0, w2 = mid_x(b), mid_x(b + 2)
        diag, up = collapse_rows(
            half_of(Z0, b), half_of(Z0, b + 1), half_of(Z0, b + 2),
            full_of(Z1, b), full_of(Z1, b + 1), full_of(Z1, b + 2),
            w0, w2, 1, 2, True,
        )
        del diag, up
        return 0

    for i in range(2):
        b = 2 * i
        w0, w2 = mid_x(b), mid_x(b + 2)
        diag, up = collapse_rows(
            half_of(Z0, b), half_of(Z0, b + 1), half_of(Z0, b + 2),
            full_of(Z1, b), full_of(Z1, b + 1), full_of(Z1, b + 2),
            w0, w2, 2, 2, True,
        )
        for j, s in enumerate(HALF):
            L15[i, j] = diag[s][0:8]
        for j, s in enumerate(FULL):
            L15[i, 5 + j] = up[s][0:8]
        L15[i, 14] = (UN[b + 1] + (1.0 - w0) * UN[b] + w2 * UN[b + 2])[0:8]
    src, dst = iota((128, 128), 0), iota((128, 128), 1)
    total = None
    for i in range(2):
        row, z = dst // 32, dst % 32
        hit = (src // 64 == row // 2) & (row % 2 == i) & (src % 64 == 2 * z + 1)
        part = jnp.dot(L15[i].reshape(120, 128), jnp.where(hit, 1.0, 0.0).astype(F32),
                       precision=HI, preferred_element_type=F32)
        total = part if total is None else total + part
    CMP[...] = total
    low_ref[0:60] = CMP[pl.ds(1, 60, stride=2), :]
    low_ref[60:64] = jnp.zeros((4, 128), F32)


def low_kernel(*refs):
    ins, out_ref, E, SRC, UA, UB = refs[:9], refs[9], refs[10], refs[11], refs[12], refs[13]
    for b in range(3):
        own, above, below = ins[3 * b : 3 * b + 3]
        for j in range(15):
            rows = pl.ds(4 * j, 4)
            mine = own[rows, :]
            v = jnp.concatenate([mine, above[rows, :], mine, below[rows, :]], 0)
            if j < 14:
                E[b, j] = v
            else:
                SRC[b] = v
    lane = iota((16, 128), 1)
    last = lane >= 96
    first = lane < 32

    def after(get, b):
        here = pltpu.roll(get(b), 96, 1)
        there = pltpu.roll(get(min(b + 1, 2)), 96, 1)
        return jnp.where(last, there, here)

    def before(get, b):
        here = pltpu.roll(get(b), 32, 1)
        there = pltpu.roll(get(max(b - 1, 0)), 32, 1)
        return jnp.where(first, there, here)

    zlane = lane % 32
    keep = {-1: jnp.where(zlane == 0, 0.0, 1.0), 1: jnp.where(zlane == 31, 0.0, 1.0)}
    del keep
    for b in range(3):
        UA[b] = DAMP * SRC[b] / E[b, 0]
    cur, nxt = UA, UB
    for sweep in range(3):
        blocks = (0, 1, 2) if sweep < 2 else (1,)
        for b in blocks:
            u_after = after(lambda c: cur[c], b)
            e0 = {s: E[b, j] for j, s in enumerate(HALF)}
            u = cur[b]
            total = e0[(0, 0)] * u
            for s in FULL:
                total = total + E[b, 5 + FULL.index(s)] * shift(u_after, *s)
                if s in HALF and s != (0, 0):
                    total = total + e0[s] * shift(u, *s)
            for dy in (-1, 0, 1):
                row = None
                for dz in (-1, 0, 1):
                    s = (dy, dz)
                    j = 5 + FULL.index(s)
                    product = before(lambda c: E[c, j] * cur[c], b)
                    if s in HALF and s != (0, 0):
                        product = product + e0[s] * u
                    product = shift(product, 0, -dz)
                    row = product if row is None else row + product
                total = total + shift(row, -dy, 0)
            nxt[b] = u + DAMP * ((SRC[b] - total) / e0[(0, 0)])
        if sweep < 2:
            cur, nxt = nxt, cur
    result = nxt[1]
    for i in range(4):
        out_ref[i] = pltpu.roll(result, (128 - 32 * i) % 128, 1)[0:4, 0:32] if i else result[0:4, 0:32]


def around(pieces):
    nx, ny = lax.axis_size("gx"), lax.axis_size("gy")

    def fetch(value, fx, fy):
        if fx == 0 and fy == 0:
            return value
        route = [
            (((i + fx) % nx) * ny + (j + fy) % ny, i * ny + j) for i in range(nx) for j in range(ny)
        ]
        return lax.ppermute(value, ("gx", "gy"), route)

    return [fetch(pieces[fx], fx, fy) for fx in (-1, 0, 1) for fy in (0, 1, -1)]


def per_device(material, velocity, density, right_side):
    shape = jax.ShapeDtypeStruct
    params = pltpu.CompilerParams(vmem_limit_bytes=48 * 1024 * 1024)
    own, low, high = pl.pallas_call(
        pack_kernel,
        out_shape=(
            shape((16, 4, 8, 128), F32),
            shape((LOW, 4, 8, 128), F32),
            shape((HIGH, 4, 8, 128), F32),
        ),
        scratch_shapes=[pltpu.VMEM((16, 16, 128), F32)],
        compiler_params=params,
        name="pack",
    )(material, right_side)
    row_x, row_y = lax.axis_index("gx"), lax.axis_index("gy")
    position = jnp.stack(
        [
            row_x,
            (row_x == lax.axis_size("gx") - 1).astype(jnp.int32),
            row_y,
            (row_y == lax.axis_size("gy") - 1).astype(jnp.int32),
        ]
    ).astype(jnp.int32)
    tables = jnp.concatenate([density, velocity])
    blocks = around({-1: low, 0: own, 1: high})
    vm = lambda *s: pltpu.VMEM(s, F32)
    smem, vmem = pl.BlockSpec(memory_space=pltpu.SMEM), pl.BlockSpec(memory_space=pltpu.VMEM)
    two, one = (ROWS, 2, 16, 128), (ROWS, 16, 128)
    fine, mid, sent = pl.pallas_call(
        main_kernel,
        in_specs=[smem, smem] + [vmem] * 9,
        out_specs=[vmem] * 3,
        out_shape=(
            shape((16, 16, 128), F32),
            shape((8, 8, 64), F32),
            shape((64, 128), F32),
        ),
        scratch_shapes=[
            vm(*two), vm(*two), vm(*two), vm(*one), vm(*two), vm(*one), vm(*one), vm(*two), vm(*two),
            vm(*two), vm(*one), vm(*two), vm(*two), vm(*two), vm(*two), vm(*one),
            vm(14, 16, 128), vm(13, 16, 128), vm(13, 16, 128),
            vm(16, 2, 16, 128), vm(16, 16, 128), vm(16, 5, 16, 128), vm(16, 9, 16, 128),
            vm(7, 5, 16, 128), vm(8, 9, 16, 128), vm(9, 16, 128), vm(9, 16, 128),
            vm(5, 5, 16, 128), vm(5, 9, 16, 128), vm(2, 15, 8, 128), vm(120, 128),
        ],
        compiler_params=params,
        name="levels",
    )(tables, position, *blocks)
    lows = around({-1: sent, 0: sent, 1: sent})
    coarse = pl.pallas_call(
        low_kernel,
        in_specs=[vmem] * 9,
        out_specs=vmem,
        out_shape=shape((4, 4, 32), F32),
        scratch_shapes=[vm(3, 14, 16, 128), vm(3, 16, 128), vm(3, 16, 128), vm(3, 16, 128)],
        compiler_params=params,
        name="coarse",
    )(*lows)
    return fine, mid, coarse


def solution(mesh):
    return jax.shard_map(
        per_device,
        mesh=mesh,
        in_specs=(P("gx", "gy", None), P(), P(), P("gx", "gy", None)),
        out_specs=(P("gx", "gy", None), P("gx", "gy", None), P("gx", "gy", None)),
        check_vma=False,
    )
```

time: 965 us -> 75.1 us (0.08); the launches traced: 948 us -> 74.4 us
  starting transfers between devices: 367 us -> 40.2 us
  local copies, waits for them, and re-layouts: 203 us -> 1.81 us
  other arithmetic: 188 us -> 0.15 us
  waiting for transfers between devices: 183 us -> 6.52 us
  Pallas kernels: 0 us -> 25 us
    ppermute x120 -> x16, starting transfers between devices: 367 us -> 40.2 us  [fetch(): return lax.ppermute(value, ('gx', 'gy'), route)]
    ppermute x120 -> x16, waiting for transfers between devices: 183 us -> 6.52 us  [fetch(): return lax.ppermute(value, ('gx', 'gy'), route)]
    add x44 -> x0, other arithmetic: 52.2 us -> none  [the longest x1 20.5 us: stencil_sum(): result + stencil[offset] * padded[:, step_x:step_x + size_x, step_y:step_...]
    mul x53 -> x0, local copies, waits for them, and re-layouts: 47.9 us -> none  [the longest x28 37.4 us: stencil_sum(): stencil[offset]]
    squeeze x46 -> x0, local copies, waits for them, and re-layouts: 39.5 us -> none  [the longest x21 38.2 us: restrict(): between = pairs[:, 0]]
    mul x42 -> x0, other arithmetic: 33.9 us -> none  [the longest x36 19.2 us: restrict(): carried = low_moved * between]
    slice x127 -> x0, local copies, waits for them, and re-layouts: 32.5 us -> none  [the longest x33 16.7 us: restrict(): following = jnp.concatenate([carried[1:], after[None]], 0)]
    another operation x68 -> x1, other arithmetic: 31.3 us -> 0.08 us  [per_device(): jnp.stack([row_x, (row_x == lax.axis_size('gx') - 1).astype(jnp.int32), r...]
  transfers between devices with their start and end apart: 120 -> 16, of which waited for: 66 -> 5; matrix products, arithmetic and copies ran while one was open for 36% -> 0% of each run, Pallas kernels for 0% -> 0%
where the time goes in v1:
time: 75.1 us; the launch traced here: 74.4 us
  starting transfers between devices  40.2 us (54%)
  Pallas kernels  25 us (33%)
  waiting for transfers between devices  6.52 us (9%)
  local copies, waits for them, and re-layouts  1.81 us (2%)
    ppermute x16, starting transfers between devices, fetch(): return lax.ppermute(value, ('gx', 'gy'), route)  40.2 us
    pallas_call x1, Pallas kernels, per_device(): pl.pallas_call(main_kernel, in_specs=[smem, smem] + [vmem] * 9, out_specs...  22.5 us
    ppermute x16, waiting for transfers between devices, fetch(): return lax.ppermute(value, ('gx', 'gy'), route)  6.52 us
    pallas_call x1, Pallas kernels, per_device(): pl.pallas_call(low_kernel, in_specs=[vmem] * 9, out_specs=vmem, out_shape...  2.09 us
    unnamed x8, local copies, waits for them, and re-layouts  1.81 us
  transfers between devices with their start and end apart: 16, of which 5 were waited for; matrix products, arithmetic and copies ran while one was open for 0% of the time, Pallas kernels for 0%

profile of v1, /device:TPU:1, one launch (start us, length us, event | category | flops | bytes accessed | tf_op | source)
XLA Modules:
  0.0 74.4 jit_solution(5434708934457317038)
XLA Ops:
  0.6 0.9 %copy-done = s32[16,16,128]{2,1,0:T(8,128)S(1)} copy-done((s32[16,16,128]{2,1,0:T(8,128)S(1)}, s32[16,16,128]{2,1,0:T(8,128)}, u32[]{:S(2)}) %copy-start) | copy-done | bytes 131096
  1.5 0.9 %copy-done.1 = f32[16,16,128]{2,1,0:T(8,128)S(1)} copy-done((f32[16,16,128]{2,1,0:T(8,128)S(1)}, f32[16,16,128]{2,1,0:T(8,128)}, u32[]{:S(2)}) %copy-start.1) | copy-done | bytes 131096
  2.4 0.4 pack.1
  2.8 4.0 %collective-permute-start.2 = (f32[7,4,8,128]{3,2,1,0:T(8,128)S(1)}, f32[7,4,8,128]{3,2,1,0:T(8,128)S(1)}, u32[]{:S(2)}, u32[]{:S(2)}) collective-permute-start(f32[7,4,8,128]{3,2,1,0:T(8,128)S(1)} %get-tuple-element.9), channel_id=1, source_target_pairs={{255,0},{240,1},{241,2},{242,3},{243,4},{244,5},{245,6},{246,7},{2... | collective-permute-start | bytes 344072 | tf_op jit(solution)/shard_map/ppermute | solution.py:627
  6.9 3.8 %collective-permute-start.1 = (f32[7,4,8,128]{3,2,1,0:T(8,128)S(1)}, f32[7,4,8,128]{3,2,1,0:T(8,128)S(1)}, u32[]{:S(2)}, u32[]{:S(2)}) collective-permute-start(f32[7,4,8,128]{3,2,1,0:T(8,128)S(1)} %get-tuple-element.9), channel_id=1, source_target_pairs={{241,0},{242,1},{243,2},{244,3},{245,4},{246,5},{247,6},{248,7},{2... | collective-permute-start | bytes 344072 | tf_op jit(solution)/shard_map/ppermute | solution.py:627
  10.7 1.7 %collective-permute-start = (f32[7,4,8,128]{3,2,1,0:T(8,128)S(1)}, f32[7,4,8,128]{3,2,1,0:T(8,128)S(1)}, u32[]{:S(2)}, u32[]{:S(2)}) collective-permute-start(f32[7,4,8,128]{3,2,1,0:T(8,128)S(1)} %get-tuple-element.9), channel_id=1, source_target_pairs={{240,0},{241,1},{242,2},{243,3},{244,4},{245,5},{246,6},{247,7},{2... | collective-permute-start | bytes 344072 | tf_op jit(solution)/shard_map/ppermute | solution.py:627
  12.4 0.0 collective-permute-start.4
  12.4 4.8 %collective-permute-start.3 = (f32[16,4,8,128]{3,2,1,0:T(8,128)S(1)}, f32[16,4,8,128]{3,2,1,0:T(8,128)S(1)}, u32[]{:S(2)}, u32[]{:S(2)}) collective-permute-start(f32[16,4,8,128]{3,2,1,0:T(8,128)S(1)} %get-tuple-element.10.refs_3_), channel_id=1, source_target_pairs={{1,0},{2,1},{3,2},{4,3},{5,4},{6,5},{7,6},{8,7},{9,8},{10,9},{11,1... | collective-permute-start | bytes 786440 | tf_op jit(solution)/shard_map/ppermute | solution.py:627
  17.1 0.0 collective-permute-done.2.refs_2_
  17.2 0.0 collective-permute-start.7
  17.2 0.0 collective-permute-done.1.refs_1_
  17.2 6.1 %collective-permute-start.6 = (f32[10,4,8,128]{3,2,1,0:T(8,128)S(1)}, f32[10,4,8,128]{3,2,1,0:T(8,128)S(1)}, u32[]{:S(2)}, u32[]{:S(2)}) collective-permute-start(f32[10,4,8,128]{3,2,1,0:T(8,128)S(1)} %get-tuple-element.11), channel_id=1, source_target_pairs={{17,0},{18,1},{19,2},{20,3},{21,4},{22,5},{23,6},{24,7},{25,8},{26... | collective-permute-start | bytes 491528 | tf_op jit(solution)/shard_map/ppermute | solution.py:627
  23.3 0.0 collective-permute-done.refs_0_
  23.3 1.6 %collective-permute-start.5 = (f32[10,4,8,128]{3,2,1,0:T(8,128)S(1)}, f32[10,4,8,128]{3,2,1,0:T(8,128)S(1)}, u32[]{:S(2)}, u32[]{:S(2)}) collective-permute-start(f32[10,4,8,128]{3,2,1,0:T(8,128)S(1)} %get-tuple-element.11), channel_id=1, source_target_pairs={{16,0},{17,1},{18,2},{19,3},{20,4},{21,5},{22,6},{23,7},{24,8},{25... | collective-permute-start | bytes 491528 | tf_op jit(solution)/shard_map/ppermute | solution.py:627
  24.9 0.1 pad_maximum_fusion.tab_ref
  25.0 0.1 pad_add_fusion.pos_ref
  25.0 1.2 %collective-permute-done.7.refs_8_ = f32[10,4,8,128]{3,2,1,0:T(8,128)S(1)} collective-permute-done((f32[10,4,8,128]{3,2,1,0:T(8,128)S(1)}, f32[10,4,8,128]{3,2,1,0:T(8,128)S(1)}, u32[]{:S(2)}, u32[]{:S(2)}) %collective-permute-start.7) | collective-permute-done | bytes 163872 | tf_op jit(solution)/shard_map/ppermute | solution.py:627
  26.2 0.8 %collective-permute-done.6.refs_7_ = f32[10,4,8,128]{3,2,1,0:T(8,128)S(1)} collective-permute-done((f32[10,4,8,128]{3,2,1,0:T(8,128)S(1)}, f32[10,4,8,128]{3,2,1,0:T(8,128)S(1)}, u32[]{:S(2)}, u32[]{:S(2)}) %collective-permute-start.6) | collective-permute-done | bytes 163872 | tf_op jit(solution)/shard_map/ppermute | solution.py:627
  27.0 1.0 %collective-permute-done.5.refs_6_ = f32[10,4,8,128]{3,2,1,0:T(8,128)S(1)} collective-permute-done((f32[10,4,8,128]{3,2,1,0:T(8,128)S(1)}, f32[10,4,8,128]{3,2,1,0:T(8,128)S(1)}, u32[]{:S(2)}, u32[]{:S(2)}) %collective-permute-start.5) | collective-permute-done | bytes 163872 | tf_op jit(solution)/shard_map/ppermute | solution.py:627
  28.0 0.0 collective-permute-done.4.refs_5_
  28.0 0.0 collective-permute-done.3.refs_4_
  28.1 22.5 %levels.1 = (f32[16,16,128]{2,1,0:T(8,128)}, f32[8,8,64]{2,1,0:T(8,128)}, f32[64,128]{1,0:T(8,128)S(1)}) custom-call(f32[16]{0:T(128)S(1)} %pad_maximum_fusion.tab_ref, s32[4]{0:T(128)S(1)} %pad_add_fusion.pos_ref, f32[7,4,8,128]{3,2,1,0:T(8,128)S(1)} %collective-permute-done.refs_0_, f32[7,4,8,128]{3,2,1,0:T(8,128)S(1)} %collective-permute-done.1.refs_1_, ...), custom_call_target="tpu_custom_call" | custom-call | tf_op jit(solution)/shard_map/levels/pallas_call | solution.py:660
  50.6 0.1 collective-permute-start.15
  50.7 8.9 %collective-permute-start.14 = (f32[64,128]{1,0:T(8,128)S(1)}, f32[64,128]{1,0:T(8,128)S(1)}, u32[]{:S(2)}, u32[]{:S(2)}) collective-permute-start(f32[64,128]{1,0:T(8,128)S(1)} %get-tuple-element.14.refs_3_), channel_id=1, source_target_pairs={{17,0},{18,1},{19,2},{20,3},{21,4},{22,5},{23,6},{24,7},{25,8},{26... | collective-permute-start | bytes 98312 | tf_op jit(solution)/shard_map/ppermute | solution.py:627
  59.6 0.0 collective-permute-start.13
  59.6 0.0 collective-permute-start.12
  59.6 4.8 %collective-permute-start.11 = (f32[64,128]{1,0:T(8,128)S(1)}, f32[64,128]{1,0:T(8,128)S(1)}, u32[]{:S(2)}, u32[]{:S(2)}) collective-permute-start(f32[64,128]{1,0:T(8,128)S(1)} %get-tuple-element.14.refs_3_), channel_id=1, source_target_pairs={{1,0},{2,1},{3,2},{4,3},{5,4},{6,5},{7,6},{8,7},{9,8},{10,9},{11,1... | collective-permute-start | bytes 98312 | tf_op jit(solution)/shard_map/ppermute | solution.py:627
  64.4 3.5 %collective-permute-start.9 = (f32[64,128]{1,0:T(8,128)S(1)}, f32[64,128]{1,0:T(8,128)S(1)}, u32[]{:S(2)}, u32[]{:S(2)}) collective-permute-start(f32[64,128]{1,0:T(8,128)S(1)} %get-tuple-element.14.refs_3_), channel_id=1, source_target_pairs={{241,0},{242,1},{243,2},{244,3},{245,4},{246,5},{247,6},{248,7},{2... | collective-permute-start | bytes 98312 | tf_op jit(solution)/shard_map/ppermute | solution.py:627
  67.9 0.9 %collective-permute-start.8 = (f32[64,128]{1,0:T(8,128)S(1)}, f32[64,128]{1,0:T(8,128)S(1)}, u32[]{:S(2)}, u32[]{:S(2)}) collective-permute-start(f32[64,128]{1,0:T(8,128)S(1)} %get-tuple-element.14.refs_3_), channel_id=1, source_target_pairs={{240,0},{241,1},{242,2},{243,3},{244,4},{245,5},{246,6},{247,7},{2... | collective-permute-start | bytes 98312 | tf_op jit(solution)/shard_map/ppermute | solution.py:627
  68.8 2.2 %collective-permute-done.10.refs_2_ = f32[64,128]{1,0:T(8,128)S(1)} collective-permute-done((f32[64,128]{1,0:T(8,128)S(1)}, f32[64,128]{1,0:T(8,128)S(1)}, u32[]{:S(2)}, u32[]{:S(2)}) %collective-permute-start.10) | collective-permute-done | bytes 32800 | tf_op jit(solution)/shard_map/ppermute | solution.py:627
  71.0 1.2 %collective-permute-done.8.refs_0_ = f32[64,128]{1,0:T(8,128)S(1)} collective-permute-done((f32[64,128]{1,0:T(8,128)S(1)}, f32[64,128]{1,0:T(8,128)S(1)}, u32[]{:S(2)}, u32[]{:S(2)}) %collective-permute-start.8) | collective-permute-done | bytes 32800 | tf_op jit(solution)/shard_map/ppermute | solution.py:627
  72.3 2.1 %coarse.1 = f32[4,4,32]{2,1,0:T(4,128)} custom-call(f32[64,128]{1,0:T(8,128)S(1)} %collective-permute-done.8.refs_0_, f32[64,128]{1,0:T(8,128)S(1)} %collective-permute-done.9.refs_1_, f32[64,128]{1,0:T(8,128)S(1)} %collective-permute-done.10.refs_2_, f32[64,128]{1,0:T(8,128)S(1)} %get-tuple-element.14.refs_3_, ...), custom_call_target="tpu_custom_call" | custom-call | tf_op jit(solution)/shard_map/coarse/pallas_call | solution.py:681
  (13 shorter events, 0.0 us)
Async XLA Ops:
  0.6 0.9 %copy-start = (s32[16,16,128]{2,1,0:T(8,128)S(1)}, s32[16,16,128]{2,1,0:T(8,128)}, u32[]{:S(2)}) copy-start(s32[16,16,128]{2,1,0:T(8,128)} %mat_ref.1) | copy-start | bytes 393220
  1.5 0.9 %copy-start.1 = (f32[16,16,128]{2,1,0:T(8,128)S(1)}, f32[16,16,128]{2,1,0:T(8,128)}, u32[]{:S(2)}) copy-start(f32[16,16,128]{2,1,0:T(8,128)} %rhs_ref.1) | copy-start | bytes 393220
  2.8 14.3 %collective-permute-start.2 = (f32[7,4,8,128]{3,2,1,0:T(8,128)S(1)}, f32[7,4,8,128]{3,2,1,0:T(8,128)S(1)}, u32[]{:S(2)}, u32[]{:S(2)}) collective-permute-start(f32[7,4,8,128]{3,2,1,0:T(8,128)S(1)} %get-tuple-element.9), channel_id=1, source_target_pairs={{255,0},{240,1},{241,2},{242,3},{243,4},{244,5},{245,6},{246,7},{2... | collective-permute-start | bytes 344072 | tf_op jit(solution)/shard_map/ppermute | solution.py:627
  6.9 10.3 %collective-permute-start.1 = (f32[7,4,8,128]{3,2,1,0:T(8,128)S(1)}, f32[7,4,8,128]{3,2,1,0:T(8,128)S(1)}, u32[]{:S(2)}, u32[]{:S(2)}) collective-permute-start(f32[7,4,8,128]{3,2,1,0:T(8,128)S(1)} %get-tuple-element.9), channel_id=1, source_target_pairs={{241,0},{242,1},{243,2},{244,3},{245,4},{246,5},{247,6},{248,7},{2... | collective-permute-start | bytes 344072 | tf_op jit(solution)/shard_map/ppermute | solution.py:627
  10.7 12.6 %collective-permute-start = (f32[7,4,8,128]{3,2,1,0:T(8,128)S(1)}, f32[7,4,8,128]{3,2,1,0:T(8,128)S(1)}, u32[]{:S(2)}, u32[]{:S(2)}) collective-permute-start(f32[7,4,8,128]{3,2,1,0:T(8,128)S(1)} %get-tuple-element.9), channel_id=1, source_target_pairs={{240,0},{241,1},{242,2},{243,3},{244,4},{245,5},{246,6},{247,7},{2... | collective-permute-start | bytes 344072 | tf_op jit(solution)/shard_map/ppermute | solution.py:627
  12.4 12.5 %copy-start.2 = (f32[8]{0:T(128)S(1)}, f32[8]{0:T(128)}, u32[]{:S(2)}) copy-start(f32[8]{0:T(128)} %param.5) | copy-start | bytes 100
  12.4 12.5 %copy-start.3 = (f32[8]{0:T(128)S(1)}, f32[8]{0:T(128)}, u32[]{:S(2)}) copy-start(f32[8]{0:T(128)} %param.6) | copy-start | bytes 100
  12.4 15.7 %collective-permute-start.4 = (f32[16,4,8,128]{3,2,1,0:T(8,128)S(1)}, f32[16,4,8,128]{3,2,1,0:T(8,128)S(1)}, u32[]{:S(2)}, u32[]{:S(2)}) collective-permute-start(f32[16,4,8,128]{3,2,1,0:T(8,128)S(1)} %get-tuple-element.10.refs_3_), channel_id=1, source_target_pairs={{15,0},{0,1},{1,2},{2,3},{3,4},{4,5},{5,6},{6,7},{7,8},{8,9},{9,10... | collective-permute-start | bytes 786440 | tf_op jit(solution)/shard_map/ppermute | solution.py:627
  12.4 15.7 %collective-permute-start.3 = (f32[16,4,8,128]{3,2,1,0:T(8,128)S(1)}, f32[16,4,8,128]{3,2,1,0:T(8,128)S(1)}, u32[]{:S(2)}, u32[]{:S(2)}) collective-permute-start(f32[16,4,8,128]{3,2,1,0:T(8,128)S(1)} %get-tuple-element.10.refs_3_), channel_id=1, source_target_pairs={{1,0},{2,1},{3,2},{4,3},{5,4},{6,5},{7,6},{8,7},{9,8},{10,9},{11,1... | collective-permute-start | bytes 786440 | tf_op jit(solution)/shard_map/ppermute | solution.py:627
  17.2 9.1 %collective-permute-start.7 = (f32[10,4,8,128]{3,2,1,0:T(8,128)S(1)}, f32[10,4,8,128]{3,2,1,0:T(8,128)S(1)}, u32[]{:S(2)}, u32[]{:S(2)}) collective-permute-start(f32[10,4,8,128]{3,2,1,0:T(8,128)S(1)} %get-tuple-element.11), channel_id=1, source_target_pairs={{31,0},{16,1},{17,2},{18,3},{19,4},{20,5},{21,6},{22,7},{23,8},{24... | collective-permute-start | bytes 491528 | tf_op jit(solution)/shard_map/ppermute | solution.py:627
  17.2 9.8 %collective-permute-start.6 = (f32[10,4,8,128]{3,2,1,0:T(8,128)S(1)}, f32[10,4,8,128]{3,2,1,0:T(8,128)S(1)}, u32[]{:S(2)}, u32[]{:S(2)}) collective-permute-start(f32[10,4,8,128]{3,2,1,0:T(8,128)S(1)} %get-tuple-element.11), channel_id=1, source_target_pairs={{17,0},{18,1},{19,2},{20,3},{21,4},{22,5},{23,6},{24,7},{25,8},{26... | collective-permute-start | bytes 491528 | tf_op jit(solution)/shard_map/ppermute | solution.py:627
  23.3 4.7 %collective-permute-start.5 = (f32[10,4,8,128]{3,2,1,0:T(8,128)S(1)}, f32[10,4,8,128]{3,2,1,0:T(8,128)S(1)}, u32[]{:S(2)}, u32[]{:S(2)}) collective-permute-start(f32[10,4,8,128]{3,2,1,0:T(8,128)S(1)} %get-tuple-element.11), channel_id=1, source_target_pairs={{16,0},{17,1},{18,2},{19,3},{20,4},{21,5},{22,6},{23,7},{24,8},{25... | collective-permute-start | bytes 491528 | tf_op jit(solution)/shard_map/ppermute | solution.py:627
  50.6 13.8 %collective-permute-start.15 = (f32[64,128]{1,0:T(8,128)S(1)}, f32[64,128]{1,0:T(8,128)S(1)}, u32[]{:S(2)}, u32[]{:S(2)}) collective-permute-start(f32[64,128]{1,0:T(8,128)S(1)} %get-tuple-element.14.refs_3_), channel_id=1, source_target_pairs={{31,0},{16,1},{17,2},{18,3},{19,4},{20,5},{21,6},{22,7},{23,8},{24... | collective-permute-start | bytes 98312 | tf_op jit(solution)/shard_map/ppermute | solution.py:627
  50.7 13.7 %collective-permute-start.14 = (f32[64,128]{1,0:T(8,128)S(1)}, f32[64,128]{1,0:T(8,128)S(1)}, u32[]{:S(2)}, u32[]{:S(2)}) collective-permute-start(f32[64,128]{1,0:T(8,128)S(1)} %get-tuple-element.14.refs_3_), channel_id=1, source_target_pairs={{17,0},{18,1},{19,2},{20,3},{21,4},{22,5},{23,6},{24,7},{25,8},{26... | collective-permute-start | bytes 98312 | tf_op jit(solution)/shard_map/ppermute | solution.py:627
  59.6 8.3 %collective-permute-start.13 = (f32[64,128]{1,0:T(8,128)S(1)}, f32[64,128]{1,0:T(8,128)S(1)}, u32[]{:S(2)}, u32[]{:S(2)}) collective-permute-start(f32[64,128]{1,0:T(8,128)S(1)} %get-tuple-element.14.refs_3_), channel_id=1, source_target_pairs={{16,0},{17,1},{18,2},{19,3},{20,4},{21,5},{22,6},{23,7},{24,8},{25... | collective-permute-start | bytes 98312 | tf_op jit(solution)/shard_map/ppermute | solution.py:627
  59.6 9.2 %collective-permute-start.12 = (f32[64,128]{1,0:T(8,128)S(1)}, f32[64,128]{1,0:T(8,128)S(1)}, u32[]{:S(2)}, u32[]{:S(2)}) collective-permute-start(f32[64,128]{1,0:T(8,128)S(1)} %get-tuple-element.14.refs_3_), channel_id=1, source_target_pairs={{15,0},{0,1},{1,2},{2,3},{3,4},{4,5},{5,6},{6,7},{7,8},{8,9},{9,10... | collective-permute-start | bytes 98312 | tf_op jit(solution)/shard_map/ppermute | solution.py:627
  59.6 9.2 %collective-permute-start.11 = (f32[64,128]{1,0:T(8,128)S(1)}, f32[64,128]{1,0:T(8,128)S(1)}, u32[]{:S(2)}, u32[]{:S(2)}) collective-permute-start(f32[64,128]{1,0:T(8,128)S(1)} %get-tuple-element.14.refs_3_), channel_id=1, source_target_pairs={{1,0},{2,1},{3,2},{4,3},{5,4},{6,5},{7,6},{8,7},{9,8},{10,9},{11,1... | collective-permute-start | bytes 98312 | tf_op jit(solution)/shard_map/ppermute | solution.py:627
  64.4 6.7 %collective-permute-start.10 = (f32[64,128]{1,0:T(8,128)S(1)}, f32[64,128]{1,0:T(8,128)S(1)}, u32[]{:S(2)}, u32[]{:S(2)}) collective-permute-start(f32[64,128]{1,0:T(8,128)S(1)} %get-tuple-element.14.refs_3_), channel_id=1, source_target_pairs={{255,0},{240,1},{241,2},{242,3},{243,4},{244,5},{245,6},{246,7},{2... | collective-permute-start | bytes 98312 | tf_op jit(solution)/shard_map/ppermute | solution.py:627
  64.4 6.7 %collective-permute-start.9 = (f32[64,128]{1,0:T(8,128)S(1)}, f32[64,128]{1,0:T(8,128)S(1)}, u32[]{:S(2)}, u32[]{:S(2)}) collective-permute-start(f32[64,128]{1,0:T(8,128)S(1)} %get-tuple-element.14.refs_3_), channel_id=1, source_target_pairs={{241,0},{242,1},{243,2},{244,3},{245,4},{246,5},{247,6},{248,7},{2... | collective-permute-start | bytes 98312 | tf_op jit(solution)/shard_map/ppermute | solution.py:627
  67.9 4.4 %collective-permute-start.8 = (f32[64,128]{1,0:T(8,128)S(1)}, f32[64,128]{1,0:T(8,128)S(1)}, u32[]{:S(2)}, u32[]{:S(2)}) collective-permute-start(f32[64,128]{1,0:T(8,128)S(1)} %get-tuple-element.14.refs_3_), channel_id=1, source_target_pairs={{240,0},{241,1},{242,2},{243,3},{244,4},{245,5},{246,6},{247,7},{2... | collective-permute-start | bytes 98312 | tf_op jit(solution)/shard_map/ppermute | solution.py:627

commit v2 on v1

--- a/solution.py
+++ b/solution.py
@@ -13,6 +13,7 @@
 HALF = ((0, 0), (0, 1), (1, -1), (1, 0), (1, 1))
 FULL = tuple((dy, dz) for dy in (-1, 0, 1) for dz in (-1, 0, 1))
 HI = lax.Precision.HIGHEST
+BY = (4, 2, 4, 4, 1, 1, 1, 1)
 
 
 def neg(s):
@@ -28,6 +29,33 @@
     return v
 
 
+def rows_loop(first, last, body, by):
+    def group(start, count):
+        stores = []
+        for k in range(count):
+            stores += body(start + k)
+        for ref, index, value in stores:
+            ref[index] = value
+
+    count = last - first
+    whole = count // by
+    if whole == 1:
+        group(first, by)
+    elif whole > 1:
+
+        def step(n, _):
+            group(first + n * by, by)
+            return 0
+
+        lax.fori_loop(0, whole, step, 0)
+    if count % by:
+        group(first + whole * by, count % by)
+
+
+def inverse(v):
+    return pl.reciprocal(v, approx=True)
+
+
 def iota(shape, dim):
     return lax.broadcasted_iota(jnp.int32, shape, dim)
 
@@ -39,17 +67,36 @@
     return jnp.where(z == source, 1.0, 0.0).astype(F32)
 
 
-def pack_kernel(mat_ref, rhs_ref, mid_ref, low_ref, high_ref, fl_ref):
+def pack_kernel(mat_ref, rhs_ref, own_ref, fl_ref):
     fl_ref[...] = mat_ref[...].astype(F32)
     order = depth_order(False)
     for q, ref in ((0, fl_ref), (2, rhs_ref)):
         for parity in range(2):
             part = ref[:, pl.ds(parity, 8, stride=2), :].reshape(128, 128)
             part = jnp.dot(part, order, precision=HI, preferred_element_type=F32)
-            part = part.reshape(16, 8, 128)
-            mid_ref[:, q + parity] = part
-            low_ref[:, q + parity] = part[16 - LOW :]
-            high_ref[:, q + parity] = part[:HIGH]
+            own_ref[:, q + parity] = part.reshape(16, 8, 128)
+
+
+def widen_kernel(pos_ref, own_ref, swap_ref, other_ref, wide_ref, to_swap_ref, to_other_ref):
+    even_x, even_y = pos_ref[4] == 0, pos_ref[5] == 0
+    row = iota((16, 8, 128), 1)
+    for q in range(4):
+        above = jnp.where(even_y, swap_ref[:, q], other_ref[:, q])
+        below = jnp.where(even_y, other_ref[:, q], swap_ref[:, q])
+        extra = jnp.where(row < 5, above, below)
+        if q == 3:
+            below_odd = jnp.where(even_y, other_ref[:, 1], swap_ref[:, 1])
+            extra = jnp.where(row == 4, below_odd, extra)
+        wide_ref[:, q, 0:8] = own_ref[:, q]
+        wide_ref[:, q, 8:16] = extra
+    start = jnp.where(even_x, 16 - HIGH, 0)
+
+    def copy(i, _):
+        to_swap_ref[i] = wide_ref[start + i]
+        to_other_ref[i] = wide_ref[(16 - HIGH) - start + i]
+        return 0
+
+    lax.fori_loop(0, HIGH, copy, 0)
 
 
 def pick(index, table):
@@ -127,10 +174,10 @@
 
 
 def main_kernel(tab_ref, pos_ref, *refs):
-    ins = refs[:9]
-    fine_ref, mid_ref, low_ref = refs[9:12]
+    ins = refs[:3]
+    fine_ref, mid_ref, low_ref = refs[3:6]
     (D, S, B, OP, CX, CYE, CYO, CZL, CZU, WZ, WY, DG, DI, U1, U2, T, AL, SM, CM,
-     WZP, WYP, C0, C1, E0, E1, UM, UN, Z0, Z1, L15, CMP) = refs[12:]
+     WZP, WYP, C0, C1, E0, E1, UM, UN, Z0, Z1, L15, CMP, MD, MS) = refs[6:]
     sh = (16, 128)
     lane = iota(sh, 1)
     subl = iota(sh, 0)
@@ -144,6 +191,7 @@
     keep_y = jnp.where((subl == yc) | (subl == yd), 0.0, 1.0)
     keep_zl = jnp.where(lane == 0, 0.0, 1.0)
     keep_zu = jnp.where(lane == 127, 0.0, 1.0)
+    two_y, two_zl, two_zu = 2.0 * keep_y, 2.0 * keep_zl, 2.0 * keep_zu
     keep_wz = jnp.where((lane == 0) | (lane >= 64), 0.0, 1.0)
 
     def keep_x(x):
@@ -171,65 +219,70 @@
     sft = [3.0 / (d * v * v) for d, v in zip(den, vel)]
     s8 = iota(tsh, 0)
 
-    def segment(first, count, own, above, below):
-        def body(i, _):
+    even_x = pos_ref[4] == 0
+
+    def segment(first, count, get, by):
+        def body(i):
             r = first + i
+            v = get(i)
+            stores = []
             for p in range(2):
-                m0 = own[i, p].astype(jnp.int32)
-                mb = below[i, p].astype(jnp.int32)
-                m1 = jnp.where(s8 < 5, above[i, p].astype(jnp.int32), mb)
-                d0, d1 = pick(m0, den), pick(m1, den)
-                D[r, p, 0:8] = d0
-                D[r, p, 8:16] = d1
-                S[r, p, 0:8] = pick(m0, sft)
-                S[r, p, 8:16] = pick(m1, sft)
-                B[r, p, 0:8] = own[i, 2 + p]
-                B[r, p, 8:16] = jnp.where(s8 < 5, above[i, 2 + p], below[i, 2 + p])
+                half = []
+                for t in range(2):
+                    rows = slice(8 * t, 8 * t + 8)
+                    m = v[p][rows].astype(jnp.int32)
+                    d = pick(m, den)
+                    half.append(d)
+                    stores.append((S, (r, p, rows), pick(m, sft)))
+                dd = jnp.concatenate(half, 0)
+                stores.append((D, (r, p), dd))
+                stores.append((B, (r, p), v[2 + p]))
                 if p == 1:
-                    dd = y_prev(jnp.concatenate([d0, d1], 0))
-                    OP[r, 0:8] = dd[0:8]
-                    OP[r, 8:16] = jnp.where(s8 == 5, pltpu.roll(pick(mb, den), 1, 0), dd[8:16])
-            return 0
-
-        lax.fori_loop(0, count, body, 0)
-
-    segment(0, LOW, ins[0], ins[1], ins[2])
-    segment(LOW, 16, ins[3], ins[4], ins[5])
-    segment(LOW + 16, HIGH, ins[6], ins[7], ins[8])
+                    dd = y_prev(dd)
+                    special = pick(v[3][8:16].astype(jnp.int32), den)
+                    stores.append((OP, (r, slice(0, 8)), dd[0:8]))
+                    extra = jnp.where(s8 == 5, pltpu.roll(special, 1, 0), dd[8:16])
+                    stores.append((OP, (r, slice(8, 16)), extra))
+            return stores
+
+        rows_loop(0, count, body, by)
+
+    wide_ref, swap_ref, other_ref = ins
+    skip = HIGH - LOW
+    segment(0, LOW, lambda i: jnp.where(even_x, other_ref[i + skip], swap_ref[i + skip]), BY[0])
+    segment(LOW, 16, lambda i: wide_ref[i], BY[0])
+    segment(LOW + 16, HIGH, lambda i: jnp.where(even_x, swap_ref[i], other_ref[i]), BY[0])
 
     def x_coupling(r, p):
-        return keep_x(r - X0) * 2.0 / (D[r, p] + D[r - 1, p])
+        return (2.0 * keep_x(r - X0)) * inverse(D[r, p] + D[r - 1, p])
 
     for p in range(2):
         CX[1, p] = x_coupling(1, p)
 
-    def coefficients(r, _):
+    def coefficients(r):
         de, do, op = D[r, 0], D[r, 1], OP[r]
         sy_m, sy_p = de + op, de + do
-        cye = keep_y * 2.0 / sy_m
-        cyo = 2.0 / sy_p
-        CYE[r] = cye
-        CYO[r] = cyo
-        WY[r] = keep_y * sy_p / (sy_m + sy_p)
+        cye = two_y * inverse(sy_m)
+        cyo = 2.0 * inverse(sy_p)
+        stores = [
+            (CYE, r, cye), (CYO, r, cyo), (WY, r, keep_y * sy_p * inverse(sy_m + sy_p)),
+        ]
         for p in range(2):
             d = D[r, p]
             lo, up = d + z_lower(d), d + z_upper(d)
-            czl = keep_zl * 2.0 / lo
-            czu = keep_zu * 2.0 / up
-            CZL[r, p] = czl
-            CZU[r, p] = czu
-            WZ[r, p] = keep_wz * up / (lo + up)
-            cxu = x_coupling(r + 1, p)
-            CX[r + 1, p] = cxu
+            czl = two_zl * inverse(lo)
+            czu = two_zu * inverse(up)
+            cxl, cxu = x_coupling(r, p), x_coupling(r + 1, p)
             ylo, yup = (cye, cyo) if p == 0 else (cyo, y_next(cye))
-            diag = S[r, p] + CX[r, p] + cxu + ylo + yup + czl + czu
-            DG[r, p] = diag
-            di = DAMP / diag
-            DI[r, p] = di
-            U1[r, p] = di * B[r, p]
-        return 0
-
-    lax.fori_loop(1, ROWS - 1, coefficients, 0)
+            diag = S[r, p] + cxl + cxu + ylo + yup + czl + czu
+            di = DAMP * inverse(diag)
+            stores += [
+                (CZL, (r, p), czl), (CZU, (r, p), czu), (WZ, (r, p), keep_wz * up * inverse(lo + up)),
+                (CX, (r + 1, p), cxu), (DG, (r, p), diag), (DI, (r, p), di), (U1, (r, p), di * B[r, p]),
+            ]
+        return stores
+
+    rows_loop(1, ROWS - 1, coefficients, BY[1])
 
     def neighbours(U, r):
         e, o = U[r, 0], U[r, 1]
@@ -250,57 +303,51 @@
             )
         return out
 
-    def second(r, _):
+    def second(r):
         around = neighbours(U1, r)
-        for p in range(2):
-            U2[r, p] = U1[r, p] + DI[r, p] * ((1.0 - DAMP) * B[r, p] + around[p])
-        return 0
-
-    lax.fori_loop(2, ROWS - 2, second, 0)
+        return [
+            (U2, (r, p), U1[r, p] + DI[r, p] * ((1.0 - DAMP) * B[r, p] + around[p])) for p in range(2)
+        ]
+
+    rows_loop(2, ROWS - 2, second, BY[2])
     order = depth_order(True)
     for p in range(2):
         part = U2[X0 : X0 + 16, p, 0:8].reshape(128, 128)
         part = jnp.dot(part, order, precision=HI, preferred_element_type=F32)
         fine_ref[:, pl.ds(p, 8, stride=2), :] = part.reshape(16, 8, 128)
 
-    def residual(r, _):
+    def residual(r):
         around = neighbours(U2, r)
         t = []
         for p in range(2):
             v = B[r, p] - DG[r, p] * U2[r, p] + around[p]
-            wl = WZ[r, p]
-            lowered = wl * v
+            lowered = WZ[r, p] * v
             t.append(v + r64(v - lowered) + pltpu.roll(lowered, 63, 1))
-        wy = WY[r]
-        te = t[0] * wy
-        T[r] = t[1] + (t[0] - te) + y_next(te)
-        return 0
-
-    lax.fori_loop(3, ROWS - 3, residual, 0)
-
-    def x_weights(n, _):
+        te = t[0] * WY[r]
+        return [(T, r, t[1] + (t[0] - te) + y_next(te))]
+
+    rows_loop(3, ROWS - 3, residual, BY[3])
+
+    def x_weights(n):
         r = 3 + 2 * n
         d = D[r, 1]
         lo, up = d + D[r - 1, 1], d + D[r + 1, 1]
-        AL[n] = keep_x(r - X0) * up / (lo + up)
-        return 0
-
-    lax.fori_loop(0, 14, x_weights, 0)
-
-    def restrict_x(n, _):
+        return [(AL, n, keep_x(r - X0) * up * inverse(lo + up))]
+
+    rows_loop(0, 14, x_weights, 7)
+
+    def restrict_x(n):
         r = 3 + 2 * n
-        SM[n] = T[r + 1] + (1.0 - AL[n]) * T[r] + AL[n + 1] * T[r + 2]
-        return 0
-
-    lax.fori_loop(0, 13, restrict_x, 0)
-
-    def mean_mid(n, _):
+        return [(SM, n, T[r + 1] + (1.0 - AL[n]) * T[r] + AL[n + 1] * T[r + 2])]
+
+    rows_loop(0, 13, restrict_x, 7)
+
+    def mean_mid(n):
         r = 3 + 2 * n
-        total = 1.0 / D[r, 0] + 1.0 / D[r, 1] + 1.0 / D[r + 1, 0] + 1.0 / D[r + 1, 1]
-        CM[n] = 0.125 * (total + r64(total))
-        return 0
-
-    lax.fori_loop(0, 13, mean_mid, 0)
+        total = inverse(D[r, 0]) + inverse(D[r, 1]) + inverse(D[r + 1, 0]) + inverse(D[r + 1, 1])
+        return [(CM, n, 0.125 * (total + r64(total)))]
+
+    rows_loop(0, 13, mean_mid, 7)
 
     def even_part(qa, qb):
         return jnp.where(lt64, qa, r64(qb))
@@ -308,14 +355,13 @@
     def odd_part(qa, qb):
         return jnp.where(lt64, r64(qa), qb)
 
-    def pair_weights(n, _):
+    def pair_weights(n):
         r = 3 + n
-        for p in range(2):
-            WZP[n, p] = even_part(WZ[r, p], WZ[r + 12, p])
-        WYP[n] = odd_part(WY[r], WY[r + 12])
-        return 0
-
-    lax.fori_loop(0, 16, pair_weights, 0)
+        return [(WZP, (n, p), even_part(WZ[r, p], WZ[r + 12, p])) for p in range(2)] + [
+            (WYP, n, odd_part(WY[r], WY[r + 12]))
+        ]
+
+    rows_loop(0, 16, pair_weights, 4)
 
     def z1(v):
         return pltpu.roll(v, 127, 1)
@@ -329,7 +375,8 @@
             -1: (c_e - wc) * wb,
         }
 
-    def build(n, _):
+    def build(n):
+        stores = []
         r = 3 + n
         q = r + 12
         cen, xup = [], []
@@ -359,24 +406,28 @@
         Ht = {d: shift(H[-d], 0, d) for d in (-1, 0, 1)}
         Ft = {d: shift(F[-d], 0, d) for d in (0, 1)}
         for d in (0, 1):
-            C0[n, HALF.index((0, d))] = (
+            v = (
                 bo[d]
                 + vh * (vhs[d] * be[d] + F[d])
                 + vhs[d] * Ft[d]
                 + y_next(vl * (vls[d] * be[d] + H[d]) + vls[d] * Ht[d])
             )
+            stores.append((C0, (n, HALF.index((0, d))), v))
         for d in (-1, 0, 1):
-            C0[n, HALF.index((1, d))] = y_next(vl * (vhs[d] * be[d] + F[d]) + vhs[d] * Ht[d])
+            v = y_next(vl * (vhs[d] * be[d] + F[d]) + vhs[d] * Ht[d])
+            stores.append((C0, (n, HALF.index((1, d))), v))
         xe, xo = xup
         for d in (-1, 0, 1):
             lx = vl * xe[d]
             hx = xe[d] - lx
-            C1[n, FULL.index((0, d))] = xo[d] + hx * uhs[d] + y_next(lx * uls[d])
-            C1[n, FULL.index((1, d))] = y_next(lx * uhs[d])
-            C1[n, FULL.index((-1, d))] = hx * uls[d]
-        return 0
-
-    lax.fori_loop(0, 15, build, 0)
+            stores += [
+                (C1, (n, FULL.index((0, d))), xo[d] + hx * uhs[d] + y_next(lx * uls[d])),
+                (C1, (n, FULL.index((1, d))), y_next(lx * uhs[d])),
+                (C1, (n, FULL.index((-1, d))), hx * uls[d]),
+            ]
+        return stores
+
+    rows_loop(0, 15, build, BY[4])
 
     def half_of(ref, n):
         return {s: ref[n, j] for j, s in enumerate(HALF)}
@@ -387,54 +438,48 @@
     def join6(n, ref):
         return odd_part(ref[n], ref[n + 6])
 
-    def first_dim(a, _):
+    def first_dim(a):
         n = 2 * a
         diag, up = collapse_rows(
             half_of(C0, n), half_of(C0, n + 1), half_of(C0, n + 2),
             full_of(C1, n), full_of(C1, n + 1), full_of(C1, n + 2),
             join6(a, AL), join6(a + 1, AL), 1, 1, True,
         )
-        for j, s in enumerate(HALF):
-            E0[a, j] = diag[s]
-        for j, s in enumerate(FULL):
-            E1[a + 1, j] = up[s]
-        return 0
-
-    for j in range(9):
-        C1[15, j] = jnp.zeros(sh, F32)
-        C1[14, j] = jnp.zeros(sh, F32)
-    lax.fori_loop(0, 7, first_dim, 0)
+        return [(E0, (a, j), diag[s]) for j, s in enumerate(HALF)] + [
+            (E1, (a + 1, j), up[s]) for j, s in enumerate(FULL)
+        ]
+
+    rows_loop(0, 7, first_dim, BY[5])
     for j in range(9):
         E1[0, j] = r64(E1[6, j])
         E1[7, j] = r64(E1[1, j])
 
-    def mid_first(a, _):
-        UM[a + 1] = DAMP * join6(a, SM) / E0[a, 0]
-        return 0
-
-    lax.fori_loop(0, 7, mid_first, 0)
+    def mid_first(a):
+        di = DAMP * inverse(E0[a, 0])
+        source = join6(a, SM)
+        return [(MD, a, di), (MS, a, source), (UM, a + 1, di * source)]
+
+    rows_loop(0, 7, mid_first, 7)
     UM[0] = r64(UM[6])
     UM[8] = r64(UM[2])
 
     def a1(U, a):
         return apply27(half_of(E0, a), full_of(E1, a + 1), full_of(E1, a), U[a], U[a + 1], U[a + 2])
 
-    def mid_second(a, _):
-        UN[a + 1] = UM[a + 1] + DAMP * ((join6(a, SM) - a1(UM, a)) / E0[a, 0])
-        return 0
-
-    lax.fori_loop(0, 7, mid_second, 0)
+    def mid_second(a):
+        return [(UN, a + 1, UM[a + 1] + MD[a] * (MS[a] - a1(UM, a)))]
+
+    rows_loop(0, 7, mid_second, BY[6])
     UN[0] = r64(UN[6])
     UN[8] = r64(UN[2])
     for i in range(4):
         mid_ref[i] = UN[i + 3, 0:8, 0:64]
         mid_ref[i + 4] = r64(UN[i + 1])[0:8, 0:64]
 
-    def mid_residual(a, _):
-        UM[a + 1] = join6(a, SM) - a1(UN, a)
-        return 0
-
-    lax.fori_loop(0, 7, mid_residual, 0)
+    def mid_residual(a):
+        return [(UM, a + 1, MS[a] - a1(UN, a))]
+
+    rows_loop(0, 7, mid_residual, BY[6])
 
     def at(b, ref, j=None):
         if j is None:
@@ -453,7 +498,7 @@
 
     def weight(g, before, after, keep):
         lo, up = before * (g + after), after * (g + before)
-        return keep * lo / (lo + up)
+        return keep * lo * inverse(lo + up)
 
     def mid_z(b):
         g = cm(b)
@@ -474,7 +519,8 @@
     def move_y(v, n):
         return shift(v, n, 0)
 
-    def build_low(b, _):
+    def build_low(b):
+        stores = []
         e0 = {s: at(b, E0, j) for j, s in enumerate(HALF)}
         e1 = {s: at1(b, j) for j, s in enumerate(FULL)}
         lz = (mid_z(b), mid_z(b + 1))
@@ -502,30 +548,18 @@
             tp = z0[(1, d)]
             tm = shift(z0[(1, -d)], -1, d, 1, 2)
             for dy, v in collapse_line(tm, t0, tp, ly[0], lc, move_y, want).items():
-                Z0[b, HALF.index((dy, d))] = v
+                stores.append((Z0, (b, HALF.index((dy, d))), v))
             lc = shift(ly[1], 0, d, 1, 2)
             tm, t0, tp = (zz1[(dy, d)] for dy in (-1, 0, 1))
             for dy, v in collapse_line(tm, t0, tp, ly[0], lc, move_y, (-1, 0, 1)).items():
-                Z1[b, FULL.index((dy, d))] = v
+                stores.append((Z1, (b, FULL.index((dy, d))), v))
         v = at1(b)
         lv = lz[0] * v
         v = v + move_z(v - lv, -1) + move_z(lv, 1)
         lv = ly[0] * v
-        UN[b] = v + move_y(v - lv, -1) + move_y(lv, 1)
-        return 0
-
-    lax.fori_loop(0, 5, build_low, 0)
-
-    def low_rows(i, _):
-        b = 2 * i
-        w0, w2 = mid_x(b), mid_x(b + 2)
-        diag, up = collapse_rows(
-            half_of(Z0, b), half_of(Z0, b + 1), half_of(Z0, b + 2),
-            full_of(Z1, b), full_of(Z1, b + 1), full_of(Z1, b + 2),
-            w0, w2, 1, 2, True,
-        )
-        del diag, up
-        return 0
+        return stores + [(UN, b, v + move_y(v - lv, -1) + move_y(lv, 1))]
+
+    rows_loop(0, 5, build_low, BY[7])
 
     for i in range(2):
         b = 2 * i
@@ -553,14 +587,20 @@
     low_ref[60:64] = jnp.zeros((4, 128), F32)
 
 
-def low_kernel(*refs):
-    ins, out_ref, E, SRC, UA, UB = refs[:9], refs[9], refs[10], refs[11], refs[12], refs[13]
-    for b in range(3):
-        own, above, below = ins[3 * b : 3 * b + 3]
-        for j in range(15):
-            rows = pl.ds(4 * j, 4)
-            mine = own[rows, :]
-            v = jnp.concatenate([mine, above[rows, :], mine, below[rows, :]], 0)
+def low_widen_kernel(pos_ref, own_ref, swap_ref, other_ref, wide_ref):
+    even = pos_ref[5] == 0
+    for j in range(15):
+        rows = slice(4 * j, 4 * j + 4)
+        own, one, two = own_ref[rows], swap_ref[rows], other_ref[rows]
+        above, below = jnp.where(even, one, two), jnp.where(even, two, one)
+        wide_ref[j] = jnp.concatenate([own, above, own, below], 0)
+
+
+def low_kernel(pos_ref, own_ref, swap_ref, other_ref, out_ref, E, SRC, UA, UB):
+    even = pos_ref[4] == 0
+    for j in range(15):
+        own, one, two = own_ref[j], swap_ref[j], other_ref[j]
+        for b, v in enumerate((jnp.where(even, two, one), own, jnp.where(even, one, two))):
             if j < 14:
                 E[b, j] = v
             else:
@@ -579,9 +619,6 @@
         there = pltpu.roll(get(max(b - 1, 0)), 32, 1)
         return jnp.where(first, there, here)
 
-    zlane = lane % 32
-    keep = {-1: jnp.where(zlane == 0, 0.0, 1.0), 1: jnp.where(zlane == 31, 0.0, 1.0)}
-    del keep
     for b in range(3):
         UA[b] = DAMP * SRC[b] / E[b, 0]
     cur, nxt = UA, UB
@@ -615,34 +652,17 @@
         out_ref[i] = pltpu.roll(result, (128 - 32 * i) % 128, 1)[0:4, 0:32] if i else result[0:4, 0:32]
 
 
-def around(pieces):
-    nx, ny = lax.axis_size("gx"), lax.axis_size("gy")
-
-    def fetch(value, fx, fy):
-        if fx == 0 and fy == 0:
-            return value
-        route = [
-            (((i + fx) % nx) * ny + (j + fy) % ny, i * ny + j) for i in range(nx) for j in range(ny)
-        ]
-        return lax.ppermute(value, ("gx", "gy"), route)
-
-    return [fetch(pieces[fx], fx, fy) for fx in (-1, 0, 1) for fy in (0, 1, -1)]
+def partners(axis, to_swap, to_other):
+    n = lax.axis_size(axis)
+    swap = [(i, i ^ 1) for i in range(n)]
+    other = [(i, (i - 1 if i % 2 == 0 else i + 1) % n) for i in range(n)]
+    return lax.ppermute(to_swap, axis, swap), lax.ppermute(to_other, axis, other)
 
 
 def per_device(material, velocity, density, right_side):
     shape = jax.ShapeDtypeStruct
     params = pltpu.CompilerParams(vmem_limit_bytes=48 * 1024 * 1024)
-    own, low, high = pl.pallas_call(
-        pack_kernel,
-        out_shape=(
-            shape((16, 4, 8, 128), F32),
-            shape((LOW, 4, 8, 128), F32),
-            shape((HIGH, 4, 8, 128), F32),
-        ),
-        scratch_shapes=[pltpu.VMEM((16, 16, 128), F32)],
-        compiler_params=params,
-        name="pack",
-    )(material, right_side)
+    smem, vmem = pl.BlockSpec(memory_space=pltpu.SMEM), pl.BlockSpec(memory_space=pltpu.VMEM)
     row_x, row_y = lax.axis_index("gx"), lax.axis_index("gy")
     position = jnp.stack(
         [
@@ -650,16 +670,37 @@
             (row_x == lax.axis_size("gx") - 1).astype(jnp.int32),
             row_y,
             (row_y == lax.axis_size("gy") - 1).astype(jnp.int32),
+            row_x % 2,
+            row_y % 2,
         ]
     ).astype(jnp.int32)
     tables = jnp.concatenate([density, velocity])
-    blocks = around({-1: low, 0: own, 1: high})
+    own = pl.pallas_call(
+        pack_kernel,
+        out_shape=shape((16, 4, 8, 128), F32),
+        scratch_shapes=[pltpu.VMEM((16, 16, 128), F32)],
+        compiler_params=params,
+        name="pack",
+    )(material, right_side)
+    near = partners("gy", own, own)
+    wide, to_swap, to_other = pl.pallas_call(
+        widen_kernel,
+        in_specs=[smem] + [vmem] * 3,
+        out_specs=[vmem] * 3,
+        out_shape=(
+            shape((16, 4, 16, 128), F32),
+            shape((HIGH, 4, 16, 128), F32),
+            shape((HIGH, 4, 16, 128), F32),
+        ),
+        compiler_params=params,
+        name="widen",
+    )(position, own, *near)
+    near = partners("gx", to_swap, to_other)
     vm = lambda *s: pltpu.VMEM(s, F32)
-    smem, vmem = pl.BlockSpec(memory_space=pltpu.SMEM), pl.BlockSpec(memory_space=pltpu.VMEM)
     two, one = (ROWS, 2, 16, 128), (ROWS, 16, 128)
     fine, mid, sent = pl.pallas_call(
         main_kernel,
-        in_specs=[smem, smem] + [vmem] * 9,
+        in_specs=[smem, smem] + [vmem] * 3,
         out_specs=[vmem] * 3,
         out_shape=(
             shape((16, 16, 128), F32),
@@ -670,23 +711,32 @@
             vm(*two), vm(*two), vm(*two), vm(*one), vm(*two), vm(*one), vm(*one), vm(*two), vm(*two),
             vm(*two), vm(*one), vm(*two), vm(*two), vm(*two), vm(*two), vm(*one),
             vm(14, 16, 128), vm(13, 16, 128), vm(13, 16, 128),
-            vm(16, 2, 16, 128), vm(16, 16, 128), vm(16, 5, 16, 128), vm(16, 9, 16, 128),
+            vm(16, 2, 16, 128), vm(16, 16, 128), vm(15, 5, 16, 128), vm(15, 9, 16, 128),
             vm(7, 5, 16, 128), vm(8, 9, 16, 128), vm(9, 16, 128), vm(9, 16, 128),
-            vm(5, 5, 16, 128), vm(5, 9, 16, 128), vm(2, 15, 8, 128), vm(120, 128),
+            vm(5, 5, 16, 128), vm(5, 9, 16, 128), vm(2, 15, 8, 128), vm(120, 128), vm(7, 16, 128), vm(7, 16, 128),
         ],
         compiler_params=params,
         name="levels",
-    )(tables, position, *blocks)
-    lows = around({-1: sent, 0: sent, 1: sent})
+    )(tables, position, wide, *near)
+    near = partners("gy", sent, sent)
+    low = pl.pallas_call(
+        low_widen_kernel,
+        in_specs=[smem] + [vmem] * 3,
+        out_specs=vmem,
+        out_shape=shape((15, 16, 128), F32),
+        compiler_params=params,
+        name="low_widen",
+    )(position, sent, *near)
+    near = partners("gx", low, low)
     coarse = pl.pallas_call(
         low_kernel,
-        in_specs=[vmem] * 9,
+        in_specs=[smem] + [vmem] * 3,
         out_specs=vmem,
         out_shape=shape((4, 4, 32), F32),
         scratch_shapes=[vm(3, 14, 16, 128), vm(3, 16, 128), vm(3, 16, 128), vm(3, 16, 128)],
         compiler_params=params,
         name="coarse",
-    )(*lows)
+    )(position, low, *near)
     return fine, mid, coarse
 
 

time: 75.1 us -> 57.9 us (0.77)
  starting transfers between devices: 40.2 us -> 20.2 us
  waiting for transfers between devices: 6.52 us -> 16.7 us
  Pallas kernels: 25 us -> 18.2 us
    ppermute x16 -> x8, starting transfers between devices: 40.2 us -> 20.2 us  [the longest x4 10.2 us: partners(): lax.ppermute(to_other, axis, other)]
    ppermute x16 -> x8, waiting for transfers between devices: 6.52 us -> 16.7 us  [the longest x4 15.4 us: partners(): lax.ppermute(to_other, axis, other)]
    pallas_call x3 -> x5, Pallas kernels: 25 us -> 18.2 us  [the longest x1 14 us: per_device(): pl.pallas_call(main_kernel, in_specs=[smem, smem] + [vmem] * 3, out_specs...]
  transfers between devices with their start and end apart: 16 -> 8, of which waited for: 5 -> 6; matrix products, arithmetic and copies ran while one was open for 0% -> 0% of each run, Pallas kernels for 0% -> 0%
where the time goes in v2:
time: 57.9 us; the launch traced here: 57.8 us
  starting transfers between devices  20.2 us (35%)
  Pallas kernels  18.2 us (31%)
  waiting for transfers between devices  16.7 us (29%)
  local copies, waits for them, and re-layouts  1.9 us (3%)
  between operations  0.7 us (1%)
    ppermute x4, waiting for transfers between devices, partners(): lax.ppermute(to_other, axis, other)  15.4 us
    pallas_call x1, Pallas kernels, per_device(): pl.pallas_call(main_kernel, in_specs=[smem, smem] + [vmem] * 3, out_specs...  14 us
    ppermute x4, starting transfers between devices, partners(): lax.ppermute(to_other, axis, other)  10.2 us
    ppermute x4, starting transfers between devices, partners(): lax.ppermute(to_swap, axis, swap)  9.99 us
    pallas_call x1, Pallas kernels, per_device(): pl.pallas_call(low_kernel, in_specs=[smem] + [vmem] * 3, out_specs=vmem,...  2.57 us
    unnamed x8, local copies, waits for them, and re-layouts  1.81 us
    ppermute x4, waiting for transfers between devices, partners(): lax.ppermute(to_swap, axis, swap)  1.32 us
  transfers between devices with their start and end apart: 8, of which 6 were waited for; matrix products, arithmetic and copies ran while one was open for 0% of the time, Pallas kernels for 0%

profile of v2, /device:TPU:1, one launch (start us, length us, event | category | flops | bytes accessed | tf_op | source)
XLA Modules:
  0.0 57.8 jit_solution(5265015505339312253)
XLA Ops:
  0.6 0.0 copy-start
  0.6 0.9 %copy-done = s32[16,16,128]{2,1,0:T(8,128)S(1)} copy-done((s32[16,16,128]{2,1,0:T(8,128)S(1)}, s32[16,16,128]{2,1,0:T(8,128)}, u32[]{:S(2)}) %copy-start) | copy-done | bytes 131096
  1.5 0.0 copy-start.1
  1.5 0.9 %copy-done.1 = f32[16,16,128]{2,1,0:T(8,128)S(1)} copy-done((f32[16,16,128]{2,1,0:T(8,128)S(1)}, f32[16,16,128]{2,1,0:T(8,128)}, u32[]{:S(2)}) %copy-start.1) | copy-done | bytes 131096
  2.4 0.4 pack.1.own_ref
  2.8 2.1 %collective-permute-start = (f32[16,4,8,128]{3,2,1,0:T(8,128)S(1)}, f32[16,4,8,128]{3,2,1,0:T(8,128)S(1)}, u32[]{:S(2)}, u32[]{:S(2)}) collective-permute-start(f32[16,4,8,128]{3,2,1,0:T(8,128)S(1)} %pack.1.own_ref), channel_id=1, source_target_pairs={{0,1},{1,0},{2,3},{3,2},{4,5},{5,4},{6,7},{7,6},{8,9},{9,8},{10,11... | collective-permute-start | bytes 786440 | tf_op jit(solution)/shard_map/ppermute | solution.py:659
  5.0 4.3 %collective-permute-start.1 = (f32[16,4,8,128]{3,2,1,0:T(8,128)S(1)}, f32[16,4,8,128]{3,2,1,0:T(8,128)S(1)}, u32[]{:S(2)}, u32[]{:S(2)}) collective-permute-start(f32[16,4,8,128]{3,2,1,0:T(8,128)S(1)} %pack.1.own_ref), channel_id=1, source_target_pairs={{0,15},{1,2},{2,1},{3,4},{4,3},{5,6},{6,5},{7,8},{8,7},{9,10},{10,... | collective-permute-start | bytes 786440 | tf_op jit(solution)/shard_map/ppermute | solution.py:659
  9.2 0.1 stack.35.pos_ref
  9.3 0.3 collective-permute-done.swap_ref
  9.6 5.1 %collective-permute-done.1.other_ref = f32[16,4,8,128]{3,2,1,0:T(8,128)S(1)} collective-permute-done((f32[16,4,8,128]{3,2,1,0:T(8,128)S(1)}, f32[16,4,8,128]{3,2,1,0:T(8,128)S(1)}, u32[]{:S(2)}, u32[]{:S(2)}) %collective-permute-start.1) | collective-permute-done | bytes 262176 | tf_op jit(solution)/shard_map/ppermute | solution.py:659
  14.8 0.7 %widen.1 = (f32[16,4,16,128]{3,2,1,0:T(8,128)S(1)}, f32[10,4,16,128]{3,2,1,0:T(8,128)S(1)}, f32[10,4,16,128]{3,2,1,0:T(8,128)S(1)}) custom-call(s32[6]{0:T(128)S(1)} %stack.35.pos_ref, f32[16,4,8,128]{3,2,1,0:T(8,128)S(1)} %pack.1.own_ref, f32[16,4,8,128]{3,2,1,0:T(8,128)S(1)} %collective-permute-done.swap_ref, ...), custom_call_target="tpu_custom_call" | custom-call | tf_op jit(solution)/shard_map/widen/pallas_call | solution.py:686
  15.5 0.0 copy-start.2
  15.5 0.0 copy-start.3
  15.5 2.3 %collective-permute-start.2 = (f32[10,4,16,128]{3,2,1,0:T(8,128)S(1)}, f32[10,4,16,128]{3,2,1,0:T(8,128)S(1)}, u32[]{:S(2)}, u32[]{:S(2)}) collective-permute-start(f32[10,4,16,128]{3,2,1,0:T(8,128)S(1)} %get-tuple-element.10), channel_id=1, source_target_pairs={{0,16},{16,0},{32,48},{48,32},{64,80},{80,64},{96,112},{112,96},{1... | collective-permute-start | bytes 983048 | tf_op jit(solution)/shard_map/ppermute | solution.py:659
  17.8 1.6 %collective-permute-start.3 = (f32[10,4,16,128]{3,2,1,0:T(8,128)S(1)}, f32[10,4,16,128]{3,2,1,0:T(8,128)S(1)}, u32[]{:S(2)}, u32[]{:S(2)}) collective-permute-start(f32[10,4,16,128]{3,2,1,0:T(8,128)S(1)} %get-tuple-element.11), channel_id=1, source_target_pairs={{0,240},{16,32},{32,16},{48,64},{64,48},{80,96},{96,80},{112,128},... | collective-permute-start | bytes 983048 | tf_op jit(solution)/shard_map/ppermute | solution.py:659
  19.4 0.0 copy-done.2
  19.4 0.0 copy-done.3
  19.4 0.1 pad_maximum_fusion.tab_ref
  19.5 0.0 collective-permute-done.2.refs_1_
  19.5 4.8 %collective-permute-done.3.refs_2_ = f32[10,4,16,128]{3,2,1,0:T(8,128)S(1)} collective-permute-done((f32[10,4,16,128]{3,2,1,0:T(8,128)S(1)}, f32[10,4,16,128]{3,2,1,0:T(8,128)S(1)}, u32[]{:S(2)}, u32[]{:S(2)}) %collective-permute-start.3) | collective-permute-done | bytes 327712 | tf_op jit(solution)/shard_map/ppermute | solution.py:659
  24.3 14.0 %levels.1 = (f32[16,16,128]{2,1,0:T(8,128)}, f32[8,8,64]{2,1,0:T(8,128)}, f32[64,128]{1,0:T(8,128)S(1)}) custom-call(f32[16]{0:T(128)S(1)} %pad_maximum_fusion.tab_ref, s32[6]{0:T(128)S(1)} %stack.35.pos_ref, f32[16,4,16,128]{3,2,1,0:T(8,128)S(1)} %get-tuple-element.9.refs_0_, f32[10,4,16,128]{3,2,1,0:T(8,128)S(1)} %collective-permute-done.2.refs_1_, ...), custom_call_target="tpu_custom_call" | custom-call | tf_op jit(solution)/shard_map/levels/pallas_call | solution.py:701
  38.3 0.1 collective-permute-start.4
  38.4 4.4 %collective-permute-start.5 = (f32[64,128]{1,0:T(8,128)S(1)}, f32[64,128]{1,0:T(8,128)S(1)}, u32[]{:S(2)}, u32[]{:S(2)}) collective-permute-start(f32[64,128]{1,0:T(8,128)S(1)} %get-tuple-element.14.own_ref), channel_id=1, source_target_pairs={{0,15},{1,2},{2,1},{3,4},{4,3},{5,6},{6,5},{7,8},{8,7},{9,10},{10,... | collective-permute-start | bytes 98312 | tf_op jit(solution)/shard_map/ppermute | solution.py:659
  42.8 0.0 collective-permute-done.4.swap_ref
  42.8 1.8 %collective-permute-done.5.other_ref = f32[64,128]{1,0:T(8,128)S(1)} collective-permute-done((f32[64,128]{1,0:T(8,128)S(1)}, f32[64,128]{1,0:T(8,128)S(1)}, u32[]{:S(2)}, u32[]{:S(2)}) %collective-permute-start.5) | collective-permute-done | bytes 32800 | tf_op jit(solution)/shard_map/ppermute | solution.py:659
  44.6 0.6 low_widen.1.own_ref
  45.2 5.5 %collective-permute-start.6 = (f32[15,16,128]{2,1,0:T(8,128)S(1)}, f32[15,16,128]{2,1,0:T(8,128)S(1)}, u32[]{:S(2)}, u32[]{:S(2)}) collective-permute-start(f32[15,16,128]{2,1,0:T(8,128)S(1)} %low_widen.1.own_ref), channel_id=1, source_target_pairs={{0,16},{16,0},{32,48},{48,32},{64,80},{80,64},{96,112},{112,96},{1... | collective-permute-start | bytes 368648 | tf_op jit(solution)/shard_map/ppermute | solution.py:659
  50.6 0.0 collective-permute-start.7
  50.6 1.0 %collective-permute-done.6.swap_ref = f32[15,16,128]{2,1,0:T(8,128)S(1)} collective-permute-done((f32[15,16,128]{2,1,0:T(8,128)S(1)}, f32[15,16,128]{2,1,0:T(8,128)S(1)}, u32[]{:S(2)}, u32[]{:S(2)}) %collective-permute-start.6) | collective-permute-done | bytes 122912 | tf_op jit(solution)/shard_map/ppermute | solution.py:659
  51.6 3.6 %collective-permute-done.7.other_ref = f32[15,16,128]{2,1,0:T(8,128)S(1)} collective-permute-done((f32[15,16,128]{2,1,0:T(8,128)S(1)}, f32[15,16,128]{2,1,0:T(8,128)S(1)}, u32[]{:S(2)}, u32[]{:S(2)}) %collective-permute-start.7) | collective-permute-done | bytes 122912 | tf_op jit(solution)/shard_map/ppermute | solution.py:659
  55.2 2.6 %coarse.1 = f32[4,4,32]{2,1,0:T(4,128)} custom-call(s32[6]{0:T(128)S(1)} %stack.35.pos_ref, f32[15,16,128]{2,1,0:T(8,128)S(1)} %low_widen.1.own_ref, f32[15,16,128]{2,1,0:T(8,128)S(1)} %collective-permute-done.6.swap_ref, f32[15,16,128]{2,1,0:T(8,128)S(1)} %collective-permute-done.7.other_ref), custom_call_target="tpu_custom_call" | custom-call | tf_op jit(solution)/shard_map/coarse/pallas_call | solution.py:731
Async XLA Ops:
  0.6 0.9 %copy-start = (s32[16,16,128]{2,1,0:T(8,128)S(1)}, s32[16,16,128]{2,1,0:T(8,128)}, u32[]{:S(2)}) copy-start(s32[16,16,128]{2,1,0:T(8,128)} %mat_ref.1) | copy-start | bytes 393220
  1.5 0.9 %copy-start.1 = (f32[16,16,128]{2,1,0:T(8,128)S(1)}, f32[16,16,128]{2,1,0:T(8,128)}, u32[]{:S(2)}) copy-start(f32[16,16,128]{2,1,0:T(8,128)} %rhs_ref.1) | copy-start | bytes 393220
  2.8 6.8 %collective-permute-start = (f32[16,4,8,128]{3,2,1,0:T(8,128)S(1)}, f32[16,4,8,128]{3,2,1,0:T(8,128)S(1)}, u32[]{:S(2)}, u32[]{:S(2)}) collective-permute-start(f32[16,4,8,128]{3,2,1,0:T(8,128)S(1)} %pack.1.own_ref), channel_id=1, source_target_pairs={{0,1},{1,0},{2,3},{3,2},{4,5},{5,4},{6,7},{7,6},{8,9},{9,8},{10,11... | collective-permute-start | bytes 786440 | tf_op jit(solution)/shard_map/ppermute | solution.py:659
  5.0 9.8 %collective-permute-start.1 = (f32[16,4,8,128]{3,2,1,0:T(8,128)S(1)}, f32[16,4,8,128]{3,2,1,0:T(8,128)S(1)}, u32[]{:S(2)}, u32[]{:S(2)}) collective-permute-start(f32[16,4,8,128]{3,2,1,0:T(8,128)S(1)} %pack.1.own_ref), channel_id=1, source_target_pairs={{0,15},{1,2},{2,1},{3,4},{4,3},{5,6},{6,5},{7,8},{8,7},{9,10},{10,... | collective-permute-start | bytes 786440 | tf_op jit(solution)/shard_map/ppermute | solution.py:659
  15.5 4.0 %copy-start.2 = (f32[8]{0:T(128)S(1)}, f32[8]{0:T(128)}, u32[]{:S(2)}) copy-start(f32[8]{0:T(128)} %param.5) | copy-start | bytes 100
  15.5 4.0 %copy-start.3 = (f32[8]{0:T(128)S(1)}, f32[8]{0:T(128)}, u32[]{:S(2)}) copy-start(f32[8]{0:T(128)} %param.6) | copy-start | bytes 100
  15.5 4.0 %collective-permute-start.2 = (f32[10,4,16,128]{3,2,1,0:T(8,128)S(1)}, f32[10,4,16,128]{3,2,1,0:T(8,128)S(1)}, u32[]{:S(2)}, u32[]{:S(2)}) collective-permute-start(f32[10,4,16,128]{3,2,1,0:T(8,128)S(1)} %get-tuple-element.10), channel_id=1, source_target_pairs={{0,16},{16,0},{32,48},{48,32},{64,80},{80,64},{96,112},{112,96},{1... | collective-permute-start | bytes 983048 | tf_op jit(solution)/shard_map/ppermute | solution.py:659
  17.8 6.5 %collective-permute-start.3 = (f32[10,4,16,128]{3,2,1,0:T(8,128)S(1)}, f32[10,4,16,128]{3,2,1,0:T(8,128)S(1)}, u32[]{:S(2)}, u32[]{:S(2)}) collective-permute-start(f32[10,4,16,128]{3,2,1,0:T(8,128)S(1)} %get-tuple-element.11), channel_id=1, source_target_pairs={{0,240},{16,32},{32,16},{48,64},{64,48},{80,96},{96,80},{112,128},... | collective-permute-start | bytes 983048 | tf_op jit(solution)/shard_map/ppermute | solution.py:659
  38.3 4.5 %collective-permute-start.4 = (f32[64,128]{1,0:T(8,128)S(1)}, f32[64,128]{1,0:T(8,128)S(1)}, u32[]{:S(2)}, u32[]{:S(2)}) collective-permute-start(f32[64,128]{1,0:T(8,128)S(1)} %get-tuple-element.14.own_ref), channel_id=1, source_target_pairs={{0,1},{1,0},{2,3},{3,2},{4,5},{5,4},{6,7},{7,6},{8,9},{9,8},{10,11... | collective-permute-start | bytes 98312 | tf_op jit(solution)/shard_map/ppermute | solution.py:659
  38.4 6.2 %collective-permute-start.5 = (f32[64,128]{1,0:T(8,128)S(1)}, f32[64,128]{1,0:T(8,128)S(1)}, u32[]{:S(2)}, u32[]{:S(2)}) collective-permute-start(f32[64,128]{1,0:T(8,128)S(1)} %get-tuple-element.14.own_ref), channel_id=1, source_target_pairs={{0,15},{1,2},{2,1},{3,4},{4,3},{5,6},{6,5},{7,8},{8,7},{9,10},{10,... | collective-permute-start | bytes 98312 | tf_op jit(solution)/shard_map/ppermute | solution.py:659
  45.2 6.4 %collective-permute-start.6 = (f32[15,16,128]{2,1,0:T(8,128)S(1)}, f32[15,16,128]{2,1,0:T(8,128)S(1)}, u32[]{:S(2)}, u32[]{:S(2)}) collective-permute-start(f32[15,16,128]{2,1,0:T(8,128)S(1)} %low_widen.1.own_ref), channel_id=1, source_target_pairs={{0,16},{16,0},{32,48},{48,32},{64,80},{80,64},{96,112},{112,96},{1... | collective-permute-start | bytes 368648 | tf_op jit(solution)/shard_map/ppermute | solution.py:659
  50.6 4.6 %collective-permute-start.7 = (f32[15,16,128]{2,1,0:T(8,128)S(1)}, f32[15,16,128]{2,1,0:T(8,128)S(1)}, u32[]{:S(2)}, u32[]{:S(2)}) collective-permute-start(f32[15,16,128]{2,1,0:T(8,128)S(1)} %low_widen.1.own_ref), channel_id=1, source_target_pairs={{0,240},{16,32},{32,16},{48,64},{64,48},{80,96},{96,80},{112,128},... | collective-permute-start | bytes 368648 | tf_op jit(solution)/shard_map/ppermute | solution.py:659

commit v3 on v2

--- a/solution.py
+++ b/solution.py
@@ -13,7 +13,7 @@
 HALF = ((0, 0), (0, 1), (1, -1), (1, 0), (1, 1))
 FULL = tuple((dy, dz) for dy in (-1, 0, 1) for dz in (-1, 0, 1))
 HI = lax.Precision.HIGHEST
-BY = (4, 2, 4, 4, 1, 1, 1, 1)
+BY = (4, 3, 8, 6, 2, 2, 7, 5)
 
 
 def neg(s):
@@ -67,28 +67,48 @@
     return jnp.where(z == source, 1.0, 0.0).astype(F32)
 
 
-def pack_kernel(mat_ref, rhs_ref, own_ref, fl_ref):
+def pack_kernel(pos_ref, mat_ref, rhs_ref, own_ref, to_swap_ref, to_other_ref, fl_ref):
+    order = depth_order(False)
     fl_ref[...] = mat_ref[...].astype(F32)
-    order = depth_order(False)
     for q, ref in ((0, fl_ref), (2, rhs_ref)):
         for parity in range(2):
             part = ref[:, pl.ds(parity, 8, stride=2), :].reshape(128, 128)
-            part = jnp.dot(part, order, precision=HI, preferred_element_type=F32)
+            precision = HI if q else None
+            part = jnp.dot(part, order, precision=precision, preferred_element_type=F32)
             own_ref[:, q + parity] = part.reshape(16, 8, 128)
+    even_y = pos_ref[5] == 0
+
+    def send(i, _):
+        for n in range(2):
+            for q in range(4):
+                up, down = own_ref[2 * i + n, q, 3:8], own_ref[2 * i + n, q, 0:5]
+                at = slice(20 * n + 5 * q, 20 * n + 5 * q + 5)
+                to_swap_ref[i, at] = jnp.where(even_y, up, down)
+                to_other_ref[i, at] = jnp.where(even_y, down, up)
+        return 0
+
+    lax.fori_loop(0, 8, send, 0, unroll=True)
 
 
 def widen_kernel(pos_ref, own_ref, swap_ref, other_ref, wide_ref, to_swap_ref, to_other_ref):
     even_x, even_y = pos_ref[4] == 0, pos_ref[5] == 0
-    row = iota((16, 8, 128), 1)
-    for q in range(4):
-        above = jnp.where(even_y, swap_ref[:, q], other_ref[:, q])
-        below = jnp.where(even_y, other_ref[:, q], swap_ref[:, q])
-        extra = jnp.where(row < 5, above, below)
-        if q == 3:
-            below_odd = jnp.where(even_y, other_ref[:, 1], swap_ref[:, 1])
-            extra = jnp.where(row == 4, below_odd, extra)
-        wide_ref[:, q, 0:8] = own_ref[:, q]
-        wide_ref[:, q, 8:16] = extra
+    wide_ref[:, :, 0:8] = own_ref[...]
+
+    def receive(i, _):
+        for n in range(2):
+            for q in range(4):
+                at = slice(20 * n + 5 * q, 20 * n + 5 * q + 5)
+                one, two = swap_ref[i, at], other_ref[i, at]
+                above, below = jnp.where(even_y, one, two), jnp.where(even_y, two, one)
+                wide_ref[2 * i + n, q, 8:13] = above
+                wide_ref[2 * i + n, q, 13:16] = below[2:5]
+                if q == 1:
+                    special = below[1:2]
+                if q == 3:
+                    wide_ref[2 * i + n, q, 12:13] = special
+        return 0
+
+    lax.fori_loop(0, 8, receive, 0, unroll=True)
     start = jnp.where(even_x, 16 - HIGH, 0)
 
     def copy(i, _):
@@ -96,7 +116,7 @@
         to_other_ref[i] = wide_ref[(16 - HIGH) - start + i]
         return 0
 
-    lax.fori_loop(0, HIGH, copy, 0)
+    lax.fori_loop(0, HIGH, copy, 0, unroll=True)
 
 
 def pick(index, table):
@@ -596,7 +616,7 @@
         wide_ref[j] = jnp.concatenate([own, above, own, below], 0)
 
 
-def low_kernel(pos_ref, own_ref, swap_ref, other_ref, out_ref, E, SRC, UA, UB):
+def low_kernel(pos_ref, own_ref, swap_ref, other_ref, out_ref, E, SRC):
     even = pos_ref[4] == 0
     for j in range(15):
         own, one, two = own_ref[j], swap_ref[j], other_ref[j]
@@ -609,45 +629,46 @@
     last = lane >= 96
     first = lane < 32
 
-    def after(get, b):
-        here = pltpu.roll(get(b), 96, 1)
-        there = pltpu.roll(get(min(b + 1, 2)), 96, 1)
-        return jnp.where(last, there, here)
-
-    def before(get, b):
-        here = pltpu.roll(get(b), 32, 1)
-        there = pltpu.roll(get(max(b - 1, 0)), 32, 1)
-        return jnp.where(first, there, here)
-
-    for b in range(3):
-        UA[b] = DAMP * SRC[b] / E[b, 0]
-    cur, nxt = UA, UB
+    def after(rows, b):
+        return pltpu.roll(jnp.where(first, rows[min(b + 1, 2)], rows[b]), 96, 1)
+
+    def before(rows, b):
+        return pltpu.roll(jnp.where(last, rows[max(b - 1, 0)], rows[b]), 32, 1)
+
+    di = [DAMP * inverse(E[b, 0]) for b in range(3)]
+    source = [SRC[b] for b in range(3)]
+    cur = [di[b] * source[b] for b in range(3)]
+
+    def lagged(products):
+        return {
+            dy: products[(dy, 0)] + shift(products[(dy, -1)], 0, 1) + shift(products[(dy, 1)], 0, -1)
+            for dy in (-1, 0, 1)
+        }
+
     for sweep in range(3):
         blocks = (0, 1, 2) if sweep < 2 else (1,)
+        moved = [lagged({s: E[b, 5 + j] * cur[b] for j, s in enumerate(FULL)}) for b in range(3)]
+        nxt = [None] * 3
         for b in blocks:
-            u_after = after(lambda c: cur[c], b)
+            u, u_after = cur[b], after(cur, b)
+            total = E[b, 0] * u
             e0 = {s: E[b, j] for j, s in enumerate(HALF)}
-            u = cur[b]
-            total = e0[(0, 0)] * u
-            for s in FULL:
-                total = total + E[b, 5 + FULL.index(s)] * shift(u_after, *s)
-                if s in HALF and s != (0, 0):
-                    total = total + e0[s] * shift(u, *s)
             for dy in (-1, 0, 1):
-                row = None
+                u_row, after_row = shift(u, dy, 0), shift(u_after, dy, 0)
                 for dz in (-1, 0, 1):
                     s = (dy, dz)
-                    j = 5 + FULL.index(s)
-                    product = before(lambda c: E[c, j] * cur[c], b)
+                    total = total + E[b, 5 + FULL.index(s)] * shift(after_row, 0, dz)
                     if s in HALF and s != (0, 0):
-                        product = product + e0[s] * u
-                    product = shift(product, 0, -dz)
-                    row = product if row is None else row + product
+                        total = total + e0[s] * shift(u_row, 0, dz)
+                row = before([m[dy] for m in moved], b)
+                if dy == 0:
+                    row = row + shift(e0[(0, 1)] * u, 0, -1)
+                if dy == 1:
+                    row = row + e0[(1, 0)] * u + shift(e0[(1, -1)] * u, 0, 1) + shift(e0[(1, 1)] * u, 0, -1)
                 total = total + shift(row, -dy, 0)
-            nxt[b] = u + DAMP * ((SRC[b] - total) / e0[(0, 0)])
-        if sweep < 2:
-            cur, nxt = nxt, cur
-    result = nxt[1]
+            nxt[b] = u + di[b] * (source[b] - total)
+        cur = nxt
+    result = cur[1]
     for i in range(4):
         out_ref[i] = pltpu.roll(result, (128 - 32 * i) % 128, 1)[0:4, 0:32] if i else result[0:4, 0:32]
 
@@ -675,14 +696,18 @@
         ]
     ).astype(jnp.int32)
     tables = jnp.concatenate([density, velocity])
-    own = pl.pallas_call(
+    own, to_swap, to_other = pl.pallas_call(
         pack_kernel,
-        out_shape=shape((16, 4, 8, 128), F32),
-        scratch_shapes=[pltpu.VMEM((16, 16, 128), F32)],
+        in_specs=[smem, vmem, vmem],
+        out_specs=[vmem] * 3,
+        out_shape=(shape((16, 4, 8, 128), F32), shape((8, 40, 128), F32), shape((8, 40, 128), F32)),
+        scratch_shapes=[
+            pltpu.VMEM((16, 16, 128), F32),
+        ],
         compiler_params=params,
         name="pack",
-    )(material, right_side)
-    near = partners("gy", own, own)
+    )(position, material, right_side)
+    near = partners("gy", to_swap, to_other)
     wide, to_swap, to_other = pl.pallas_call(
         widen_kernel,
         in_specs=[smem] + [vmem] * 3,
@@ -733,7 +758,7 @@
         in_specs=[smem] + [vmem] * 3,
         out_specs=vmem,
         out_shape=shape((4, 4, 32), F32),
-        scratch_shapes=[vm(3, 14, 16, 128), vm(3, 16, 128), vm(3, 16, 128), vm(3, 16, 128)],
+        scratch_shapes=[vm(3, 14, 16, 128), vm(3, 16, 128)],
         compiler_params=params,
         name="coarse",
     )(position, low, *near)

time: 57.9 us -> 51.3 us (0.89)
  Pallas kernels: 18.2 us -> 13.8 us
  waiting for transfers between devices: 16.7 us -> 14.4 us
    pallas_call x1, Pallas kernels: 14 us -> 9.87 us  [per_device(): pl.pallas_call(main_kernel, in_specs=[smem, smem] + [vmem] * 3, out_specs...]
    ppermute x4, waiting for transfers between devices: 15.4 us -> 13.5 us  [partners(): lax.ppermute(to_other, axis, other)]
    pallas_call x1, Pallas kernels: 2.57 us -> 1.85 us  [per_device(): pl.pallas_call(low_kernel, in_specs=[smem] + [vmem] * 3, out_specs=vmem,...]
  transfers between devices with their start and end apart: 8 -> 8, of which waited for: 6 -> 5; matrix products, arithmetic and copies ran while one was open for 0% -> 0% of each run, Pallas kernels for 0% -> 0%
where the time goes in v3:
time: 51.3 us; the launch traced here: 51.2 us
  starting transfers between devices  20.3 us (40%)
  waiting for transfers between devices  14.4 us (28%)
  Pallas kernels  13.8 us (27%)
  local copies, waits for them, and re-layouts  1.91 us (4%)
  between operations  0.7 us (1%)
    ppermute x4, waiting for transfers between devices, partners(): lax.ppermute(to_other, axis, other)  13.5 us
    ppermute x4, starting transfers between devices, partners(): lax.ppermute(to_other, axis, other)  10.2 us
    ppermute x4, starting transfers between devices, partners(): lax.ppermute(to_swap, axis, swap)  10.1 us
    pallas_call x1, Pallas kernels, per_device(): pl.pallas_call(main_kernel, in_specs=[smem, smem] + [vmem] * 3, out_specs...  9.87 us
    pallas_call x1, Pallas kernels, per_device(): pl.pallas_call(low_kernel, in_specs=[smem] + [vmem] * 3, out_specs=vmem,...  1.85 us
    unnamed x8, local copies, waits for them, and re-layouts  1.82 us
  transfers between devices with their start and end apart: 8, of which 5 were waited for; matrix products, arithmetic and copies ran while one was open for 0% of the time, Pallas kernels for 0%

profile of v3, /device:TPU:1, one launch (start us, length us, event | category | flops | bytes accessed | tf_op | source)
XLA Modules:
  0.0 51.2 jit_solution(9109470086496684256)
XLA Ops:
  0.7 0.1 stack.35.pos_ref
  0.7 0.0 copy-start
  0.7 0.9 %copy-done = s32[16,16,128]{2,1,0:T(8,128)S(1)} copy-done((s32[16,16,128]{2,1,0:T(8,128)S(1)}, s32[16,16,128]{2,1,0:T(8,128)}, u32[]{:S(2)}) %copy-start) | copy-done | bytes 131096
  1.6 0.0 copy-start.1
  1.6 0.9 %copy-done.1 = f32[16,16,128]{2,1,0:T(8,128)S(1)} copy-done((f32[16,16,128]{2,1,0:T(8,128)S(1)}, f32[16,16,128]{2,1,0:T(8,128)}, u32[]{:S(2)}) %copy-start.1) | copy-done | bytes 131096
  2.5 0.8 %pack.1 = (f32[16,4,8,128]{3,2,1,0:T(8,128)S(1)}, f32[8,40,128]{2,1,0:T(8,128)S(1)}, f32[8,40,128]{2,1,0:T(8,128)S(1)}) custom-call(s32[6]{0:T(128)S(1)} %stack.35.pos_ref, s32[16,16,128]{2,1,0:T(8,128)S(1)} %copy-done, f32[16,16,128]{2,1,0:T(8,128)S(1)} %copy-done.1), custom_call_target="tpu_custom_call" | custom-call | tf_op jit(solution)/shard_map/pack/pallas_call | solution.py:699
  3.4 2.1 %collective-permute-start = (f32[8,40,128]{2,1,0:T(8,128)S(1)}, f32[8,40,128]{2,1,0:T(8,128)S(1)}, u32[]{:S(2)}, u32[]{:S(2)}) collective-permute-start(f32[8,40,128]{2,1,0:T(8,128)S(1)} %get-tuple-element.13), channel_id=1, source_target_pairs={{0,1},{1,0},{2,3},{3,2},{4,5},{5,4},{6,7},{7,6},{8,9},{9,8},{10,11... | collective-permute-start | bytes 491528 | tf_op jit(solution)/shard_map/ppermute | solution.py:680
  5.5 4.3 %collective-permute-start.1 = (f32[8,40,128]{2,1,0:T(8,128)S(1)}, f32[8,40,128]{2,1,0:T(8,128)S(1)}, u32[]{:S(2)}, u32[]{:S(2)}) collective-permute-start(f32[8,40,128]{2,1,0:T(8,128)S(1)} %get-tuple-element.14), channel_id=1, source_target_pairs={{0,15},{1,2},{2,1},{3,4},{4,3},{5,6},{6,5},{7,8},{8,7},{9,10},{10,... | collective-permute-start | bytes 491528 | tf_op jit(solution)/shard_map/ppermute | solution.py:680
  9.8 0.0 collective-permute-done.swap_ref
  9.8 3.2 %collective-permute-done.1.other_ref = f32[8,40,128]{2,1,0:T(8,128)S(1)} collective-permute-done((f32[8,40,128]{2,1,0:T(8,128)S(1)}, f32[8,40,128]{2,1,0:T(8,128)S(1)}, u32[]{:S(2)}, u32[]{:S(2)}) %collective-permute-start.1) | collective-permute-done | bytes 163872 | tf_op jit(solution)/shard_map/ppermute | solution.py:680
  13.0 0.7 %widen.1 = (f32[16,4,16,128]{3,2,1,0:T(8,128)S(1)}, f32[10,4,16,128]{3,2,1,0:T(8,128)S(1)}, f32[10,4,16,128]{3,2,1,0:T(8,128)S(1)}) custom-call(s32[6]{0:T(128)S(1)} %stack.35.pos_ref, f32[16,4,8,128]{3,2,1,0:T(8,128)S(1)} %get-tuple-element.12.own_ref, f32[8,40,128]{2,1,0:T(8,128)S(1)} %collective-permute-done.swap_ref, ...), custom_call_target="tpu_custom_call" | custom-call | tf_op jit(solution)/shard_map/widen/pallas_call | solution.py:711
  13.7 0.0 copy-start.2
  13.7 0.0 copy-start.3
  13.7 2.5 %collective-permute-start.2 = (f32[10,4,16,128]{3,2,1,0:T(8,128)S(1)}, f32[10,4,16,128]{3,2,1,0:T(8,128)S(1)}, u32[]{:S(2)}, u32[]{:S(2)}) collective-permute-start(f32[10,4,16,128]{3,2,1,0:T(8,128)S(1)} %get-tuple-element.16), channel_id=1, source_target_pairs={{0,16},{16,0},{32,48},{48,32},{64,80},{80,64},{96,112},{112,96},{1... | collective-permute-start | bytes 983048 | tf_op jit(solution)/shard_map/ppermute | solution.py:680
  16.2 1.6 %collective-permute-start.3 = (f32[10,4,16,128]{3,2,1,0:T(8,128)S(1)}, f32[10,4,16,128]{3,2,1,0:T(8,128)S(1)}, u32[]{:S(2)}, u32[]{:S(2)}) collective-permute-start(f32[10,4,16,128]{3,2,1,0:T(8,128)S(1)} %get-tuple-element.17), channel_id=1, source_target_pairs={{0,240},{16,32},{32,16},{48,64},{64,48},{80,96},{96,80},{112,128},... | collective-permute-start | bytes 983048 | tf_op jit(solution)/shard_map/ppermute | solution.py:680
  17.8 0.0 copy-done.2
  17.8 0.0 copy-done.3
  17.8 0.1 pad_maximum_fusion.tab_ref
  17.9 0.0 collective-permute-done.2.refs_1_
  17.9 4.8 %collective-permute-done.3.refs_2_ = f32[10,4,16,128]{3,2,1,0:T(8,128)S(1)} collective-permute-done((f32[10,4,16,128]{3,2,1,0:T(8,128)S(1)}, f32[10,4,16,128]{3,2,1,0:T(8,128)S(1)}, u32[]{:S(2)}, u32[]{:S(2)}) %collective-permute-start.3) | collective-permute-done | bytes 327712 | tf_op jit(solution)/shard_map/ppermute | solution.py:680
  22.7 9.9 %levels.1 = (f32[16,16,128]{2,1,0:T(8,128)}, f32[8,8,64]{2,1,0:T(8,128)}, f32[64,128]{1,0:T(8,128)S(1)}) custom-call(f32[16]{0:T(128)S(1)} %pad_maximum_fusion.tab_ref, s32[6]{0:T(128)S(1)} %stack.35.pos_ref, f32[16,4,16,128]{3,2,1,0:T(8,128)S(1)} %get-tuple-element.15.refs_0_, f32[10,4,16,128]{3,2,1,0:T(8,128)S(1)} %collective-permute-done.2.refs_1_, ...), custom_call_target="tpu_custom_call" | custom-call | tf_op jit(solution)/shard_map/levels/pallas_call | solution.py:726
  32.6 0.0 collective-permute-start.4
  32.6 4.3 %collective-permute-start.5 = (f32[64,128]{1,0:T(8,128)S(1)}, f32[64,128]{1,0:T(8,128)S(1)}, u32[]{:S(2)}, u32[]{:S(2)}) collective-permute-start(f32[64,128]{1,0:T(8,128)S(1)} %get-tuple-element.20.own_ref), channel_id=1, source_target_pairs={{0,15},{1,2},{2,1},{3,4},{4,3},{5,6},{6,5},{7,8},{8,7},{9,10},{10,... | collective-permute-start | bytes 98312 | tf_op jit(solution)/shard_map/ppermute | solution.py:680
  36.9 0.0 collective-permute-done.4.swap_ref
  36.9 1.8 %collective-permute-done.5.other_ref = f32[64,128]{1,0:T(8,128)S(1)} collective-permute-done((f32[64,128]{1,0:T(8,128)S(1)}, f32[64,128]{1,0:T(8,128)S(1)}, u32[]{:S(2)}, u32[]{:S(2)}) %collective-permute-start.5) | collective-permute-done | bytes 32800 | tf_op jit(solution)/shard_map/ppermute | solution.py:680
  38.7 0.6 %low_widen.1.own_ref = f32[15,16,128]{2,1,0:T(8,128)S(1)} custom-call(s32[6]{0:T(128)S(1)} %stack.35.pos_ref, f32[64,128]{1,0:T(8,128)S(1)} %get-tuple-element.20.own_ref, f32[64,128]{1,0:T(8,128)S(1)} %collective-permute-done.4.swap_ref, f32[64,128]{1,0:T(8,128)S(1)} %collective-permute-done.5.other_ref), custom_call_target="tpu_custom_call" | custom-call | tf_op jit(solution)/shard_map/low_widen/pallas_call | solution.py:747
  39.2 5.5 %collective-permute-start.6 = (f32[15,16,128]{2,1,0:T(8,128)S(1)}, f32[15,16,128]{2,1,0:T(8,128)S(1)}, u32[]{:S(2)}, u32[]{:S(2)}) collective-permute-start(f32[15,16,128]{2,1,0:T(8,128)S(1)} %low_widen.1.own_ref), channel_id=1, source_target_pairs={{0,16},{16,0},{32,48},{48,32},{64,80},{80,64},{96,112},{112,96},{1... | collective-permute-start | bytes 368648 | tf_op jit(solution)/shard_map/ppermute | solution.py:680
  44.7 0.0 collective-permute-start.7
  44.7 1.0 %collective-permute-done.6.swap_ref = f32[15,16,128]{2,1,0:T(8,128)S(1)} collective-permute-done((f32[15,16,128]{2,1,0:T(8,128)S(1)}, f32[15,16,128]{2,1,0:T(8,128)S(1)}, u32[]{:S(2)}, u32[]{:S(2)}) %collective-permute-start.6) | collective-permute-done | bytes 122912 | tf_op jit(solution)/shard_map/ppermute | solution.py:680
  45.7 3.6 %collective-permute-done.7.other_ref = f32[15,16,128]{2,1,0:T(8,128)S(1)} collective-permute-done((f32[15,16,128]{2,1,0:T(8,128)S(1)}, f32[15,16,128]{2,1,0:T(8,128)S(1)}, u32[]{:S(2)}, u32[]{:S(2)}) %collective-permute-start.7) | collective-permute-done | bytes 122912 | tf_op jit(solution)/shard_map/ppermute | solution.py:680
  49.3 1.9 %coarse.1 = f32[4,4,32]{2,1,0:T(4,128)} custom-call(s32[6]{0:T(128)S(1)} %stack.35.pos_ref, f32[15,16,128]{2,1,0:T(8,128)S(1)} %low_widen.1.own_ref, f32[15,16,128]{2,1,0:T(8,128)S(1)} %collective-permute-done.6.swap_ref, f32[15,16,128]{2,1,0:T(8,128)S(1)} %collective-permute-done.7.other_ref), custom_call_target="tpu_custom_call" | custom-call | tf_op jit(solution)/shard_map/coarse/pallas_call | solution.py:756
Async XLA Ops:
  0.7 0.9 %copy-start = (s32[16,16,128]{2,1,0:T(8,128)S(1)}, s32[16,16,128]{2,1,0:T(8,128)}, u32[]{:S(2)}) copy-start(s32[16,16,128]{2,1,0:T(8,128)} %mat_ref.1) | copy-start | bytes 393220
  1.6 0.9 %copy-start.1 = (f32[16,16,128]{2,1,0:T(8,128)S(1)}, f32[16,16,128]{2,1,0:T(8,128)}, u32[]{:S(2)}) copy-start(f32[16,16,128]{2,1,0:T(8,128)} %rhs_ref.1) | copy-start | bytes 393220
  3.4 6.4 %collective-permute-start = (f32[8,40,128]{2,1,0:T(8,128)S(1)}, f32[8,40,128]{2,1,0:T(8,128)S(1)}, u32[]{:S(2)}, u32[]{:S(2)}) collective-permute-start(f32[8,40,128]{2,1,0:T(8,128)S(1)} %get-tuple-element.13), channel_id=1, source_target_pairs={{0,1},{1,0},{2,3},{3,2},{4,5},{5,4},{6,7},{7,6},{8,9},{9,8},{10,11... | collective-permute-start | bytes 491528 | tf_op jit(solution)/shard_map/ppermute | solution.py:680
  5.5 7.5 %collective-permute-start.1 = (f32[8,40,128]{2,1,0:T(8,128)S(1)}, f32[8,40,128]{2,1,0:T(8,128)S(1)}, u32[]{:S(2)}, u32[]{:S(2)}) collective-permute-start(f32[8,40,128]{2,1,0:T(8,128)S(1)} %get-tuple-element.14), channel_id=1, source_target_pairs={{0,15},{1,2},{2,1},{3,4},{4,3},{5,6},{6,5},{7,8},{8,7},{9,10},{10,... | collective-permute-start | bytes 491528 | tf_op jit(solution)/shard_map/ppermute | solution.py:680
  13.7 4.2 %copy-start.2 = (f32[8]{0:T(128)S(1)}, f32[8]{0:T(128)}, u32[]{:S(2)}) copy-start(f32[8]{0:T(128)} %param.5) | copy-start | bytes 100
  13.7 4.2 %copy-start.3 = (f32[8]{0:T(128)S(1)}, f32[8]{0:T(128)}, u32[]{:S(2)}) copy-start(f32[8]{0:T(128)} %param.6) | copy-start | bytes 100
  13.7 4.2 %collective-permute-start.2 = (f32[10,4,16,128]{3,2,1,0:T(8,128)S(1)}, f32[10,4,16,128]{3,2,1,0:T(8,128)S(1)}, u32[]{:S(2)}, u32[]{:S(2)}) collective-permute-start(f32[10,4,16,128]{3,2,1,0:T(8,128)S(1)} %get-tuple-element.16), channel_id=1, source_target_pairs={{0,16},{16,0},{32,48},{48,32},{64,80},{80,64},{96,112},{112,96},{1... | collective-permute-start | bytes 983048 | tf_op jit(solution)/shard_map/ppermute | solution.py:680
  16.2 6.5 %collective-permute-start.3 = (f32[10,4,16,128]{3,2,1,0:T(8,128)S(1)}, f32[10,4,16,128]{3,2,1,0:T(8,128)S(1)}, u32[]{:S(2)}, u32[]{:S(2)}) collective-permute-start(f32[10,4,16,128]{3,2,1,0:T(8,128)S(1)} %get-tuple-element.17), channel_id=1, source_target_pairs={{0,240},{16,32},{32,16},{48,64},{64,48},{80,96},{96,80},{112,128},... | collective-permute-start | bytes 983048 | tf_op jit(solution)/shard_map/ppermute | solution.py:680
  32.6 4.3 %collective-permute-start.4 = (f32[64,128]{1,0:T(8,128)S(1)}, f32[64,128]{1,0:T(8,128)S(1)}, u32[]{:S(2)}, u32[]{:S(2)}) collective-permute-start(f32[64,128]{1,0:T(8,128)S(1)} %get-tuple-element.20.own_ref), channel_id=1, source_target_pairs={{0,1},{1,0},{2,3},{3,2},{4,5},{5,4},{6,7},{7,6},{8,9},{9,8},{10,11... | collective-permute-start | bytes 98312 | tf_op jit(solution)/shard_map/ppermute | solution.py:680
  32.6 6.1 %collective-permute-start.5 = (f32[64,128]{1,0:T(8,128)S(1)}, f32[64,128]{1,0:T(8,128)S(1)}, u32[]{:S(2)}, u32[]{:S(2)}) collective-permute-start(f32[64,128]{1,0:T(8,128)S(1)} %get-tuple-element.20.own_ref), channel_id=1, source_target_pairs={{0,15},{1,2},{2,1},{3,4},{4,3},{5,6},{6,5},{7,8},{8,7},{9,10},{10,... | collective-permute-start | bytes 98312 | tf_op jit(solution)/shard_map/ppermute | solution.py:680
  39.2 6.4 %collective-permute-start.6 = (f32[15,16,128]{2,1,0:T(8,128)S(1)}, f32[15,16,128]{2,1,0:T(8,128)S(1)}, u32[]{:S(2)}, u32[]{:S(2)}) collective-permute-start(f32[15,16,128]{2,1,0:T(8,128)S(1)} %low_widen.1.own_ref), channel_id=1, source_target_pairs={{0,16},{16,0},{32,48},{48,32},{64,80},{80,64},{96,112},{112,96},{1... | collective-permute-start | bytes 368648 | tf_op jit(solution)/shard_map/ppermute | solution.py:680
  44.7 4.6 %collective-permute-start.7 = (f32[15,16,128]{2,1,0:T(8,128)S(1)}, f32[15,16,128]{2,1,0:T(8,128)S(1)}, u32[]{:S(2)}, u32[]{:S(2)}) collective-permute-start(f32[15,16,128]{2,1,0:T(8,128)S(1)} %low_widen.1.own_ref), channel_id=1, source_target_pairs={{0,240},{16,32},{32,16},{48,64},{64,48},{80,96},{96,80},{112,128},... | collective-permute-start | bytes 368648 | tf_op jit(solution)/shard_map/ppermute | solution.py:680

commit v4 on v3

--- a/solution.py
+++ b/solution.py
@@ -67,10 +67,9 @@
     return jnp.where(z == source, 1.0, 0.0).astype(F32)
 
 
-def pack_kernel(pos_ref, mat_ref, rhs_ref, own_ref, to_swap_ref, to_other_ref, fl_ref):
+def pack_kernel(pos_ref, mat_ref, rhs_ref, own_ref, to_swap_ref, to_other_ref):
     order = depth_order(False)
-    fl_ref[...] = mat_ref[...].astype(F32)
-    for q, ref in ((0, fl_ref), (2, rhs_ref)):
+    for q, ref in ((0, mat_ref), (2, rhs_ref)):
         for parity in range(2):
             part = ref[:, pl.ds(parity, 8, stride=2), :].reshape(128, 128)
             precision = HI if q else None
@@ -193,11 +192,16 @@
     return iota(shape, 1) < n
 
 
-def main_kernel(tab_ref, pos_ref, *refs):
-    ins = refs[:3]
-    fine_ref, mid_ref, low_ref = refs[3:6]
-    (D, S, B, OP, CX, CYE, CYO, CZL, CZU, WZ, WY, DG, DI, U1, U2, T, AL, SM, CM,
-     WZP, WYP, C0, C1, E0, E1, UM, UN, Z0, Z1, L15, CMP, MD, MS) = refs[6:]
+CARRIED = ("D", "B", "CX", "CYE", "CYO", "CZL", "CZU", "WZ", "WY", "DG", "DI", "U1", "S", "OP", "CA0", "CA1", "CB0", "CB1")
+
+
+class Fine:
+    def __init__(self, tab_ref, pos_ref, arrays):
+        for name, value in fine_work(tab_ref, pos_ref, **arrays).items():
+            setattr(self, name, value)
+
+
+def fine_work(tab_ref, pos_ref, D, S, B, OP, CX, CYE, CYO, CZL, CZU, WZ, WY, DG, DI, U1, CA0, CA1, CB0, CB1):
     sh = (16, 128)
     lane = iota(sh, 1)
     subl = iota(sh, 0)
@@ -267,17 +271,8 @@
 
         rows_loop(0, count, body, by)
 
-    wide_ref, swap_ref, other_ref = ins
-    skip = HIGH - LOW
-    segment(0, LOW, lambda i: jnp.where(even_x, other_ref[i + skip], swap_ref[i + skip]), BY[0])
-    segment(LOW, 16, lambda i: wide_ref[i], BY[0])
-    segment(LOW + 16, HIGH, lambda i: jnp.where(even_x, swap_ref[i], other_ref[i]), BY[0])
-
     def x_coupling(r, p):
         return (2.0 * keep_x(r - X0)) * inverse(D[r, p] + D[r - 1, p])
-
-    for p in range(2):
-        CX[1, p] = x_coupling(1, p)
 
     def coefficients(r):
         de, do, op = D[r, 0], D[r, 1], OP[r]
@@ -302,7 +297,110 @@
             ]
         return stores
 
-    rows_loop(1, ROWS - 1, coefficients, BY[1])
+    def even_part(qa, qb):
+        return jnp.where(lt64, qa, r64(qb))
+
+    def odd_part(qa, qb):
+        return jnp.where(lt64, r64(qa), qb)
+
+    def z1(v):
+        return pltpu.roll(v, 127, 1)
+
+    def z_collapse_lateral(c_e, c_o, wa, wb):
+        ha, hb = 1.0 - wa, 1.0 - wb
+        wc = wa * c_e
+        return {
+            0: c_o + ha * hb * c_e + z1(wc * wb),
+            1: z1(wc * hb),
+            -1: (c_e - wc) * wb,
+        }
+
+    def build(xa, xb):
+        stores = []
+        r, q = xa + X0, xb + X0
+        wz = [even_part(WZ[r, p], WZ[q, p]) for p in range(2)]
+        wz_next = [even_part(WZ[r + 1, p], WZ[q + 1, p]) for p in range(2)]
+
+        def put(refs, j, v):
+            stores.extend(((refs[0], (xa + 4, j), v), (refs[1], (xb - 8, j), v)))
+
+        cen, xup = [], []
+        for p in range(2):
+            wl = wz[p]
+            wh = 1.0 - wl
+            dge, dgo = even_part(DG[r, p], DG[q, p]), odd_part(DG[r, p], DG[q, p])
+            cze, czo = -even_part(CZL[r, p], CZL[q, p]), -odd_part(CZL[r, p], CZL[q, p])
+            wd = wl * dge
+            c = dgo + wh * (wh * dge + 2.0 * czo) + z1(wl * (wd + 2.0 * cze))
+            m = wh * (wd + cze) + wl * czo
+            cen.append({-1: m, 0: c, 1: z1(m)})
+            cxe = -even_part(CX[r + 1, p], CX[q + 1, p])
+            cxo = -odd_part(CX[r + 1, p], CX[q + 1, p])
+            xup.append(z_collapse_lateral(cxe, cxo, wl, wz_next[p]))
+        we, wo = wz
+        F = z_collapse_lateral(-even_part(CYO[r], CYO[q]), -odd_part(CYO[r], CYO[q]), we, wo)
+        H = z_collapse_lateral(-even_part(CYE[r], CYE[q]), -odd_part(CYE[r], CYE[q]), we, y_prev(wo))
+        vl = odd_part(WY[r], WY[q])
+        vh = 1.0 - vl
+        ul = odd_part(WY[r + 1], WY[q + 1])
+        be, bo = cen
+        vls = {d: shift(vl, 0, d) for d in (-1, 0, 1)}
+        vhs = {d: 1.0 - vls[d] for d in (-1, 0, 1)}
+        uls = {d: shift(ul, 0, d) for d in (-1, 0, 1)}
+        uhs = {d: 1.0 - uls[d] for d in (-1, 0, 1)}
+        Ht = {d: shift(H[-d], 0, d) for d in (-1, 0, 1)}
+        Ft = {d: shift(F[-d], 0, d) for d in (0, 1)}
+        for d in (0, 1):
+            v = (
+                bo[d]
+                + vh * (vhs[d] * be[d] + F[d])
+                + vhs[d] * Ft[d]
+                + y_next(vl * (vls[d] * be[d] + H[d]) + vls[d] * Ht[d])
+            )
+            put((CA0, CB0), HALF.index((0, d)), v)
+        for d in (-1, 0, 1):
+            v = y_next(vl * (vhs[d] * be[d] + F[d]) + vhs[d] * Ht[d])
+            put((CA0, CB0), HALF.index((1, d)), v)
+        xe, xo = xup
+        for d in (-1, 0, 1):
+            lx = vl * xe[d]
+            hx = xe[d] - lx
+            put((CA1, CB1), FULL.index((0, d)), xo[d] + hx * uhs[d] + y_next(lx * uls[d]))
+            put((CA1, CB1), FULL.index((1, d)), y_next(lx * uhs[d]))
+            put((CA1, CB1), FULL.index((-1, d)), hx * uls[d])
+        return stores
+
+    return locals()
+
+
+def inner_kernel(tab_ref, pos_ref, wide_ref, *refs):
+    arrays = dict(zip(CARRIED, refs))
+    f = Fine(tab_ref, pos_ref, arrays)
+    f.segment(LOW, 16, lambda i: wide_ref[i], BY[0])
+    rows_loop(X0 + 1, X0 + 15, f.coefficients, BY[1])
+    rows_loop(1, 7, lambda x: f.build(x, x + 7), BY[4])
+
+
+def main_kernel(tab_ref, pos_ref, swap_ref, other_ref, *refs):
+    refs = refs[len(CARRIED) :]
+    fine_ref, mid_ref, low_ref = refs[:3]
+    arrays = dict(zip(CARRIED, refs[3 : 3 + len(CARRIED)]))
+    (U2, T, AL, SM, CM,
+     E0, E1, UM, UN, Z0, Z1, L15, CMP, MD, MS) = refs[3 + len(CARRIED) :]
+    D, B, CX, CYE, CYO, CZL, CZU, WZ, WY, DG, DI, U1, _, _, CA0, CA1, CB0, CB1 = (
+        arrays[n] for n in CARRIED
+    )
+    f = Fine(tab_ref, pos_ref, arrays)
+    sh, lane, lt64, even_x = f.sh, f.lane, f.lt64, f.even_x
+    r64, y_next, y_prev, z_lower, z_upper = f.r64, f.y_next, f.y_prev, f.z_lower, f.z_upper
+    keep_x, keep_y, odd_part, x_first, x_last = f.keep_x, f.keep_y, f.odd_part, f.x_first, f.x_last
+    skip = HIGH - LOW
+    f.segment(0, LOW, lambda i: jnp.where(even_x, other_ref[i + skip], swap_ref[i + skip]), BY[0])
+    f.segment(LOW + 16, HIGH, lambda i: jnp.where(even_x, swap_ref[i], other_ref[i]), BY[0])
+    for p in range(2):
+        CX[1, p] = f.x_coupling(1, p)
+    rows_loop(1, X0 + 1, f.coefficients, BY[1])
+    rows_loop(X0 + 15, ROWS - 1, f.coefficients, BY[1])
 
     def neighbours(U, r):
         e, o = U[r, 0], U[r, 1]
@@ -369,85 +467,11 @@
 
     rows_loop(0, 13, mean_mid, 7)
 
-    def even_part(qa, qb):
-        return jnp.where(lt64, qa, r64(qb))
-
-    def odd_part(qa, qb):
-        return jnp.where(lt64, r64(qa), qb)
-
-    def pair_weights(n):
-        r = 3 + n
-        return [(WZP, (n, p), even_part(WZ[r, p], WZ[r + 12, p])) for p in range(2)] + [
-            (WYP, n, odd_part(WY[r], WY[r + 12]))
-        ]
-
-    rows_loop(0, 16, pair_weights, 4)
-
-    def z1(v):
-        return pltpu.roll(v, 127, 1)
-
-    def z_collapse_lateral(c_e, c_o, wa, wb):
-        ha, hb = 1.0 - wa, 1.0 - wb
-        wc = wa * c_e
-        return {
-            0: c_o + ha * hb * c_e + z1(wc * wb),
-            1: z1(wc * hb),
-            -1: (c_e - wc) * wb,
-        }
-
-    def build(n):
-        stores = []
-        r = 3 + n
-        q = r + 12
-        cen, xup = [], []
-        for p in range(2):
-            wl = WZP[n, p]
-            wh = 1.0 - wl
-            dge, dgo = even_part(DG[r, p], DG[q, p]), odd_part(DG[r, p], DG[q, p])
-            cze, czo = -even_part(CZL[r, p], CZL[q, p]), -odd_part(CZL[r, p], CZL[q, p])
-            wd = wl * dge
-            c = dgo + wh * (wh * dge + 2.0 * czo) + z1(wl * (wd + 2.0 * cze))
-            m = wh * (wd + cze) + wl * czo
-            cen.append({-1: m, 0: c, 1: z1(m)})
-            cxe = -even_part(CX[r + 1, p], CX[q + 1, p])
-            cxo = -odd_part(CX[r + 1, p], CX[q + 1, p])
-            xup.append(z_collapse_lateral(cxe, cxo, wl, WZP[n + 1, p]))
-        we, wo = WZP[n, 0], WZP[n, 1]
-        F = z_collapse_lateral(-even_part(CYO[r], CYO[q]), -odd_part(CYO[r], CYO[q]), we, wo)
-        H = z_collapse_lateral(-even_part(CYE[r], CYE[q]), -odd_part(CYE[r], CYE[q]), we, y_prev(wo))
-        vl = WYP[n]
-        vh = 1.0 - vl
-        ul = WYP[n + 1]
-        be, bo = cen
-        vls = {d: shift(vl, 0, d) for d in (-1, 0, 1)}
-        vhs = {d: 1.0 - vls[d] for d in (-1, 0, 1)}
-        uls = {d: shift(ul, 0, d) for d in (-1, 0, 1)}
-        uhs = {d: 1.0 - uls[d] for d in (-1, 0, 1)}
-        Ht = {d: shift(H[-d], 0, d) for d in (-1, 0, 1)}
-        Ft = {d: shift(F[-d], 0, d) for d in (0, 1)}
-        for d in (0, 1):
-            v = (
-                bo[d]
-                + vh * (vhs[d] * be[d] + F[d])
-                + vhs[d] * Ft[d]
-                + y_next(vl * (vls[d] * be[d] + H[d]) + vls[d] * Ht[d])
-            )
-            stores.append((C0, (n, HALF.index((0, d))), v))
-        for d in (-1, 0, 1):
-            v = y_next(vl * (vhs[d] * be[d] + F[d]) + vhs[d] * Ht[d])
-            stores.append((C0, (n, HALF.index((1, d))), v))
-        xe, xo = xup
-        for d in (-1, 0, 1):
-            lx = vl * xe[d]
-            hx = xe[d] - lx
-            stores += [
-                (C1, (n, FULL.index((0, d))), xo[d] + hx * uhs[d] + y_next(lx * uls[d])),
-                (C1, (n, FULL.index((1, d))), y_next(lx * uhs[d])),
-                (C1, (n, FULL.index((-1, d))), hx * uls[d]),
-            ]
-        return stores
-
-    rows_loop(0, 15, build, BY[4])
+    rows_loop(-4, 1, lambda x: f.build(x, x + 18), BY[4])
+    rows_loop(7, 11, lambda x: f.build(x, x + 12), BY[4])
+
+    def both(first, second, n, j):
+        return jnp.where(lt64, first[n, j], second[n, j])
 
     def half_of(ref, n):
         return {s: ref[n, j] for j, s in enumerate(HALF)}
@@ -461,8 +485,8 @@
     def first_dim(a):
         n = 2 * a
         diag, up = collapse_rows(
-            half_of(C0, n), half_of(C0, n + 1), half_of(C0, n + 2),
-            full_of(C1, n), full_of(C1, n + 1), full_of(C1, n + 2),
+            *({s: both(CA0, CB0, n + k, j) for j, s in enumerate(HALF)} for k in range(3)),
+            *({s: both(CA1, CB1, n + k, j) for j, s in enumerate(FULL)} for k in range(3)),
             join6(a, AL), join6(a + 1, AL), 1, 1, True,
         )
         return [(E0, (a, j), diag[s]) for j, s in enumerate(HALF)] + [
@@ -701,12 +725,9 @@
         in_specs=[smem, vmem, vmem],
         out_specs=[vmem] * 3,
         out_shape=(shape((16, 4, 8, 128), F32), shape((8, 40, 128), F32), shape((8, 40, 128), F32)),
-        scratch_shapes=[
-            pltpu.VMEM((16, 16, 128), F32),
-        ],
         compiler_params=params,
         name="pack",
-    )(position, material, right_side)
+    )(position, material.astype(F32), right_side)
     near = partners("gy", to_swap, to_other)
     wide, to_swap, to_other = pl.pallas_call(
         widen_kernel,
@@ -720,29 +741,42 @@
         compiler_params=params,
         name="widen",
     )(position, own, *near)
-    near = partners("gx", to_swap, to_other)
     vm = lambda *s: pltpu.VMEM(s, F32)
     two, one = (ROWS, 2, 16, 128), (ROWS, 16, 128)
+    carried = [two, two, two, one, one, two, two, two, one, two, two, two, two, one]
+    carried += [(15, n, 16, 128) for n in (5, 9, 5, 9)]
+    carried = [shape(c, F32) for c in carried]
+    count = len(carried)
+    inner = pl.pallas_call(
+        inner_kernel,
+        in_specs=[smem, smem, vmem],
+        out_specs=[vmem] * count,
+        out_shape=carried,
+        compiler_params=pltpu.CompilerParams(vmem_limit_bytes=24 * 1024 * 1024),
+        cost_estimate=pl.CostEstimate(flops=20_000_000, bytes_accessed=8_000_000, transcendentals=0),
+        name="inner",
+    )(tables, position, wide)
+    to_swap, *inner = lax.optimization_barrier((to_swap, *inner))
+    near = partners("gx", to_swap, to_other)
     fine, mid, sent = pl.pallas_call(
         main_kernel,
-        in_specs=[smem, smem] + [vmem] * 3,
-        out_specs=[vmem] * 3,
-        out_shape=(
+        in_specs=[smem, smem] + [vmem] * (2 + count),
+        out_specs=[vmem] * (3 + count),
+        out_shape=[
             shape((16, 16, 128), F32),
             shape((8, 8, 64), F32),
             shape((64, 128), F32),
-        ),
+        ] + carried,
+        input_output_aliases={4 + n: 3 + n for n in range(count)},
         scratch_shapes=[
-            vm(*two), vm(*two), vm(*two), vm(*one), vm(*two), vm(*one), vm(*one), vm(*two), vm(*two),
-            vm(*two), vm(*one), vm(*two), vm(*two), vm(*two), vm(*two), vm(*one),
+            vm(*two), vm(*one),
             vm(14, 16, 128), vm(13, 16, 128), vm(13, 16, 128),
-            vm(16, 2, 16, 128), vm(16, 16, 128), vm(15, 5, 16, 128), vm(15, 9, 16, 128),
             vm(7, 5, 16, 128), vm(8, 9, 16, 128), vm(9, 16, 128), vm(9, 16, 128),
             vm(5, 5, 16, 128), vm(5, 9, 16, 128), vm(2, 15, 8, 128), vm(120, 128), vm(7, 16, 128), vm(7, 16, 128),
         ],
-        compiler_params=params,
+        compiler_params=pltpu.CompilerParams(vmem_limit_bytes=24 * 1024 * 1024),
         name="levels",
-    )(tables, position, wide, *near)
+    )(tables, position, *near, *inner)[:3]
     near = partners("gy", sent, sent)
     low = pl.pallas_call(
         low_widen_kernel,

time: 51.3 us -> 47.7 us (0.930); the launches traced: 51.2 us -> 47 us
  waiting for transfers between devices: 14.4 us -> 7.76 us
  other arithmetic: 0.07 us -> 1.66 us
  starting transfers between devices: 20.3 us -> 21.4 us
  local copies, waits for them, and re-layouts: 1.91 us -> 0.99 us
  Pallas kernels: 13.8 us -> 14.5 us
    ppermute x4, waiting for transfers between devices: 13.5 us -> 4.68 us  [partners(): lax.ppermute(to_other, axis, other)]
    ppermute x4, starting transfers between devices: 10.2 us -> 13.9 us  [partners(): lax.ppermute(to_other, axis, other)]
    ppermute x4, starting transfers between devices: 10.1 us -> 7.44 us  [partners(): lax.ppermute(to_swap, axis, swap)]
    ppermute x4, waiting for transfers between devices: 0.98 us -> 3.08 us  [partners(): lax.ppermute(to_swap, axis, swap)]
    unnamed x8 -> x2, local copies, waits for them, and re-layouts: 1.82 us -> 0.91 us
    convert_element_type x0 -> x1, other arithmetic: none -> 0.92 us  [per_device(): material.astype(F32)]
    pallas_call x1 -> x2, Pallas kernels: 9.87 us -> 10.6 us  [the longest x1 8.15 us: per_device(): pl.pallas_call(main_kernel, in_specs=[smem, smem] + [vmem] * (2 + count),...]
    concatenate x1, other arithmetic: 0.07 us -> 0.75 us  [per_device(): tables = jnp.concatenate([density, velocity])]
  transfers between devices with their start and end apart: 8 -> 8, of which waited for: 5 -> 6; matrix products, arithmetic and copies ran while one was open for 0% -> 2% of each run, Pallas kernels for 0% -> 5%
where the time goes in v4:
time: 47.7 us; the launch traced here: 47 us
  starting transfers between devices  21.4 us (45%)
  Pallas kernels  14.5 us (30%)
  waiting for transfers between devices  7.76 us (16%)
  other arithmetic  1.66 us (3%)
  local copies, waits for them, and re-layouts  0.99 us (2%)
  between operations  0.71 us (1%)
    ppermute x4, starting transfers between devices, partners(): lax.ppermute(to_other, axis, other)  13.9 us
    pallas_call x1, Pallas kernels, per_device(): pl.pallas_call(main_kernel, in_specs=[smem, smem] + [vmem] * (2 + count),...  8.15 us
    ppermute x4, starting transfers between devices, partners(): lax.ppermute(to_swap, axis, swap)  7.44 us
    ppermute x4, waiting for transfers between devices, partners(): lax.ppermute(to_other, axis, other)  4.68 us
    ppermute x4, waiting for transfers between devices, partners(): lax.ppermute(to_swap, axis, swap)  3.08 us
    pallas_call x1, Pallas kernels, per_device(): pl.pallas_call(inner_kernel, in_specs=[smem, smem, vmem], out_specs=[vmem...  2.45 us
    pallas_call x1, Pallas kernels, per_device(): pl.pallas_call(low_kernel, in_specs=[smem] + [vmem] * 3, out_specs=vmem,...  1.85 us
  transfers between devices with their start and end apart: 8, of which 6 were waited for; matrix products, arithmetic and copies ran while one was open for 2% of the time, Pallas kernels for 5%

profile of v4, /device:TPU:1, one launch (start us, length us, event | category | flops | bytes accessed | tf_op | source)
XLA Modules:
  0.0 47.0 jit_solution(17503026170650225191)
XLA Ops:
  0.7 0.9 %convert_element_type.2.mat_ref = f32[16,16,128]{2,1,0:T(8,128)S(1)} convert(s32[16,16,128]{2,1,0:T(8,128)} %param.4) | non-fusion elementwise | flops 32768 | bytes 262144 | tf_op jit(solution)/shard_map/convert_element_type | solution.py:730
  1.6 0.1 stack.35.pos_ref
  1.7 0.0 copy-start
  1.7 0.9 %copy-done = f32[16,16,128]{2,1,0:T(8,128)S(1)} copy-done((f32[16,16,128]{2,1,0:T(8,128)S(1)}, f32[16,16,128]{2,1,0:T(8,128)}, u32[]{:S(2)}) %copy-start) | copy-done | bytes 131096
  2.6 0.8 %pack.1 = (f32[16,4,8,128]{3,2,1,0:T(8,128)S(1)}, f32[8,40,128]{2,1,0:T(8,128)S(1)}, f32[8,40,128]{2,1,0:T(8,128)S(1)}) custom-call(s32[6]{0:T(128)S(1)} %stack.35.pos_ref, f32[16,16,128]{2,1,0:T(8,128)S(1)} %convert_element_type.2.mat_ref, f32[16,16,128]{2,1,0:T(8,128)S(1)} %copy-done), custom_call_target="tpu_custom_call" | custom-call | tf_op jit(solution)/shard_map/pack/pallas_call | solution.py:723
  3.4 2.1 %collective-permute-start = (f32[8,40,128]{2,1,0:T(8,128)S(1)}, f32[8,40,128]{2,1,0:T(8,128)S(1)}, u32[]{:S(2)}, u32[]{:S(2)}) collective-permute-start(f32[8,40,128]{2,1,0:T(8,128)S(1)} %get-tuple-element.50), channel_id=1, source_target_pairs={{0,1},{1,0},{2,3},{3,2},{4,5},{5,4},{6,7},{7,6},{8,9},{9,8},{10,11... | collective-permute-start | bytes 491528 | tf_op jit(solution)/shard_map/ppermute | solution.py:704
  5.5 4.3 %collective-permute-start.1 = (f32[8,40,128]{2,1,0:T(8,128)S(1)}, f32[8,40,128]{2,1,0:T(8,128)S(1)}, u32[]{:S(2)}, u32[]{:S(2)}) collective-permute-start(f32[8,40,128]{2,1,0:T(8,128)S(1)} %get-tuple-element.51), channel_id=1, source_target_pairs={{0,15},{1,2},{2,1},{3,4},{4,3},{5,6},{6,5},{7,8},{8,7},{9,10},{10,... | collective-permute-start | bytes 491528 | tf_op jit(solution)/shard_map/ppermute | solution.py:704
  9.8 0.7 %pad_maximum_fusion.tab_ref = f32[16]{0:T(128)S(1)} fusion(f32[8]{0:T(128)} %param.5, f32[8]{0:T(128)} %param.6), kind=kLoop, calls=%fused_computation | loop fusion | flops 16 | bytes 128 | tf_op jit(solution)/shard_map/concatenate | solution.py:722
  10.6 0.0 collective-permute-done.swap_ref
  10.6 2.5 %collective-permute-done.1.other_ref = f32[8,40,128]{2,1,0:T(8,128)S(1)} collective-permute-done((f32[8,40,128]{2,1,0:T(8,128)S(1)}, f32[8,40,128]{2,1,0:T(8,128)S(1)}, u32[]{:S(2)}, u32[]{:S(2)}) %collective-permute-start.1) | collective-permute-done | bytes 163872 | tf_op jit(solution)/shard_map/ppermute | solution.py:704
  13.0 0.7 %widen.1 = (f32[16,4,16,128]{3,2,1,0:T(8,128)S(1)}, f32[10,4,16,128]{3,2,1,0:T(8,128)S(1)}, f32[10,4,16,128]{3,2,1,0:T(8,128)S(1)}) custom-call(s32[6]{0:T(128)S(1)} %stack.35.pos_ref, f32[16,4,8,128]{3,2,1,0:T(8,128)S(1)} %get-tuple-element.49.own_ref, f32[8,40,128]{2,1,0:T(8,128)S(1)} %collective-permute-done.swap_ref, ...), custom_call_target="tpu_custom_call" | custom-call | tf_op jit(solution)/shard_map/widen/pallas_call | solution.py:732
  13.7 4.1 %collective-permute-start.3 = (f32[10,4,16,128]{3,2,1,0:T(8,128)S(1)}, f32[10,4,16,128]{3,2,1,0:T(8,128)S(1)}, u32[]{:S(2)}, u32[]{:S(2)}) collective-permute-start(f32[10,4,16,128]{3,2,1,0:T(8,128)S(1)} %get-tuple-element.73), channel_id=1, source_target_pairs={{0,240},{16,32},{32,16},{48,64},{64,48},{80,96},{96,80},{112,128},... | collective-permute-start | bytes 983048 | tf_op jit(solution)/shard_map/ppermute | solution.py:704
  17.8 2.4 %inner.1 = (f32[33,2,16,128]{3,2,1,0:T(8,128)S(1)}, f32[33,2,16,128]{3,2,1,0:T(8,128)S(1)}, f32[33,2,16,128]{3,2,1,0:T(8,128)S(1)}, f32[33,16,128]{2,1,0:T(8,128...) custom-call(f32[16]{0:T(128)S(1)} %pad_maximum_fusion.tab_ref, ...), custom_call_target="tpu_custom_call" | custom-call | flops 20000000 | bytes 8000000 | tf_op jit(solution)/shard_map/inner/pallas_call | solution.py:750
  20.2 2.7 %collective-permute-start.2 = (f32[10,4,16,128]{3,2,1,0:T(8,128)S(1)}, f32[10,4,16,128]{3,2,1,0:T(8,128)S(1)}, u32[]{:S(2)}, u32[]{:S(2)}) collective-permute-start(f32[10,4,16,128]{3,2,1,0:T(8,128)S(1)} %get-tuple-element.72), channel_id=1, source_target_pairs={{0,16},{16,0},{32,48},{48,32},{64,80},{80,64},{96,112},{112,96},{1... | collective-permute-start | bytes 983048 | tf_op jit(solution)/shard_map/ppermute | solution.py:704
  22.9 0.0 collective-permute-done.3.other_ref
  22.9 1.3 %collective-permute-done.2.swap_ref = f32[10,4,16,128]{3,2,1,0:T(8,128)S(1)} collective-permute-done((f32[10,4,16,128]{3,2,1,0:T(8,128)S(1)}, f32[10,4,16,128]{3,2,1,0:T(8,128)S(1)}, u32[]{:S(2)}, u32[]{:S(2)}) %collective-permute-start.2) | collective-permute-done | bytes 327712 | tf_op jit(solution)/shard_map/ppermute | solution.py:704
  24.1 8.1 %levels.1 = (f32[16,16,128]{2,1,0:T(8,128)}, f32[8,8,64]{2,1,0:T(8,128)}, f32[64,128]{1,0:T(8,128)S(1)}, f32[33,2,16,128]{3,2,1,0:T(8,128)S(1)}, f32[33,2,16,128...) custom-call(f32[16]{0:T(128)S(1)} %pad_maximum_fusion.tab_ref, ...), custom_call_target="tpu_custom_call", output_to_operand_aliasing={{3}: (4, {}), {4}: (5, {}), {5}: (6, {}), {6}: (7, {}), {7}... | custom-call | tf_op jit(solution)/shard_map/levels/pallas_call | solution.py:761
  32.3 4.3 %collective-permute-start.5 = (f32[64,128]{1,0:T(8,128)S(1)}, f32[64,128]{1,0:T(8,128)S(1)}, u32[]{:S(2)}, u32[]{:S(2)}) collective-permute-start(f32[64,128]{1,0:T(8,128)S(1)} %get-tuple-element.94.own_ref), channel_id=1, source_target_pairs={{0,15},{1,2},{2,1},{3,4},{4,3},{5,6},{6,5},{7,8},{8,7},{9,10},{10,... | collective-permute-start | bytes 98312 | tf_op jit(solution)/shard_map/ppermute | solution.py:704
  36.5 0.0 collective-permute-start.4
  36.5 1.8 %collective-permute-done.5.other_ref = f32[64,128]{1,0:T(8,128)S(1)} collective-permute-done((f32[64,128]{1,0:T(8,128)S(1)}, f32[64,128]{1,0:T(8,128)S(1)}, u32[]{:S(2)}, u32[]{:S(2)}) %collective-permute-start.5) | collective-permute-done | bytes 32800 | tf_op jit(solution)/shard_map/ppermute | solution.py:704
  38.4 1.2 %collective-permute-done.4.swap_ref = f32[64,128]{1,0:T(8,128)S(1)} collective-permute-done((f32[64,128]{1,0:T(8,128)S(1)}, f32[64,128]{1,0:T(8,128)S(1)}, u32[]{:S(2)}, u32[]{:S(2)}) %collective-permute-start.4) | collective-permute-done | bytes 32800 | tf_op jit(solution)/shard_map/ppermute | solution.py:704
  39.6 0.6 %low_widen.1.own_ref = f32[15,16,128]{2,1,0:T(8,128)S(1)} custom-call(s32[6]{0:T(128)S(1)} %stack.35.pos_ref, f32[64,128]{1,0:T(8,128)S(1)} %get-tuple-element.94.own_ref, f32[64,128]{1,0:T(8,128)S(1)} %collective-permute-done.4.swap_ref, f32[64,128]{1,0:T(8,128)S(1)} %collective-permute-done.5.other_ref), custom_call_target="tpu_custom_call" | custom-call | tf_op jit(solution)/shard_map/low_widen/pallas_call | solution.py:781
  40.2 1.4 %collective-permute-start.7 = (f32[15,16,128]{2,1,0:T(8,128)S(1)}, f32[15,16,128]{2,1,0:T(8,128)S(1)}, u32[]{:S(2)}, u32[]{:S(2)}) collective-permute-start(f32[15,16,128]{2,1,0:T(8,128)S(1)} %low_widen.1.own_ref), channel_id=1, source_target_pairs={{0,240},{16,32},{32,16},{48,64},{64,48},{80,96},{96,80},{112,128},... | collective-permute-start | bytes 368648 | tf_op jit(solution)/shard_map/ppermute | solution.py:704
  41.5 2.6 %collective-permute-start.6 = (f32[15,16,128]{2,1,0:T(8,128)S(1)}, f32[15,16,128]{2,1,0:T(8,128)S(1)}, u32[]{:S(2)}, u32[]{:S(2)}) collective-permute-start(f32[15,16,128]{2,1,0:T(8,128)S(1)} %low_widen.1.own_ref), channel_id=1, source_target_pairs={{0,16},{16,0},{32,48},{48,32},{64,80},{80,64},{96,112},{112,96},{1... | collective-permute-start | bytes 368648 | tf_op jit(solution)/shard_map/ppermute | solution.py:704
  44.2 0.4 collective-permute-done.7.other_ref
  44.6 0.6 %collective-permute-done.6.swap_ref = f32[15,16,128]{2,1,0:T(8,128)S(1)} collective-permute-done((f32[15,16,128]{2,1,0:T(8,128)S(1)}, f32[15,16,128]{2,1,0:T(8,128)S(1)}, u32[]{:S(2)}, u32[]{:S(2)}) %collective-permute-start.6) | collective-permute-done | bytes 122912 | tf_op jit(solution)/shard_map/ppermute | solution.py:704
  45.1 1.8 %coarse.1 = f32[4,4,32]{2,1,0:T(4,128)} custom-call(s32[6]{0:T(128)S(1)} %stack.35.pos_ref, f32[15,16,128]{2,1,0:T(8,128)S(1)} %low_widen.1.own_ref, f32[15,16,128]{2,1,0:T(8,128)S(1)} %collective-permute-done.6.swap_ref, f32[15,16,128]{2,1,0:T(8,128)S(1)} %collective-permute-done.7.other_ref), custom_call_target="tpu_custom_call" | custom-call | tf_op jit(solution)/shard_map/coarse/pallas_call | solution.py:790
Async XLA Ops:
  1.7 0.9 %copy-start = (f32[16,16,128]{2,1,0:T(8,128)S(1)}, f32[16,16,128]{2,1,0:T(8,128)}, u32[]{:S(2)}) copy-start(f32[16,16,128]{2,1,0:T(8,128)} %rhs_ref.1) | copy-start | bytes 393220
  3.4 7.1 %collective-permute-start = (f32[8,40,128]{2,1,0:T(8,128)S(1)}, f32[8,40,128]{2,1,0:T(8,128)S(1)}, u32[]{:S(2)}, u32[]{:S(2)}) collective-permute-start(f32[8,40,128]{2,1,0:T(8,128)S(1)} %get-tuple-element.50), channel_id=1, source_target_pairs={{0,1},{1,0},{2,3},{3,2},{4,5},{5,4},{6,7},{7,6},{8,9},{9,8},{10,11... | collective-permute-start | bytes 491528 | tf_op jit(solution)/shard_map/ppermute | solution.py:704
  5.5 7.5 %collective-permute-start.1 = (f32[8,40,128]{2,1,0:T(8,128)S(1)}, f32[8,40,128]{2,1,0:T(8,128)S(1)}, u32[]{:S(2)}, u32[]{:S(2)}) collective-permute-start(f32[8,40,128]{2,1,0:T(8,128)S(1)} %get-tuple-element.51), channel_id=1, source_target_pairs={{0,15},{1,2},{2,1},{3,4},{4,3},{5,6},{6,5},{7,8},{8,7},{9,10},{10,... | collective-permute-start | bytes 491528 | tf_op jit(solution)/shard_map/ppermute | solution.py:704
  13.7 9.2 %collective-permute-start.3 = (f32[10,4,16,128]{3,2,1,0:T(8,128)S(1)}, f32[10,4,16,128]{3,2,1,0:T(8,128)S(1)}, u32[]{:S(2)}, u32[]{:S(2)}) collective-permute-start(f32[10,4,16,128]{3,2,1,0:T(8,128)S(1)} %get-tuple-element.73), channel_id=1, source_target_pairs={{0,240},{16,32},{32,16},{48,64},{64,48},{80,96},{96,80},{112,128},... | collective-permute-start | bytes 983048 | tf_op jit(solution)/shard_map/ppermute | solution.py:704
  20.2 3.9 %collective-permute-start.2 = (f32[10,4,16,128]{3,2,1,0:T(8,128)S(1)}, f32[10,4,16,128]{3,2,1,0:T(8,128)S(1)}, u32[]{:S(2)}, u32[]{:S(2)}) collective-permute-start(f32[10,4,16,128]{3,2,1,0:T(8,128)S(1)} %get-tuple-element.72), channel_id=1, source_target_pairs={{0,16},{16,0},{32,48},{48,32},{64,80},{80,64},{96,112},{112,96},{1... | collective-permute-start | bytes 983048 | tf_op jit(solution)/shard_map/ppermute | solution.py:704
  32.3 6.1 %collective-permute-start.5 = (f32[64,128]{1,0:T(8,128)S(1)}, f32[64,128]{1,0:T(8,128)S(1)}, u32[]{:S(2)}, u32[]{:S(2)}) collective-permute-start(f32[64,128]{1,0:T(8,128)S(1)} %get-tuple-element.94.own_ref), channel_id=1, source_target_pairs={{0,15},{1,2},{2,1},{3,4},{4,3},{5,6},{6,5},{7,8},{8,7},{9,10},{10,... | collective-permute-start | bytes 98312 | tf_op jit(solution)/shard_map/ppermute | solution.py:704
  36.5 3.1 %collective-permute-start.4 = (f32[64,128]{1,0:T(8,128)S(1)}, f32[64,128]{1,0:T(8,128)S(1)}, u32[]{:S(2)}, u32[]{:S(2)}) collective-permute-start(f32[64,128]{1,0:T(8,128)S(1)} %get-tuple-element.94.own_ref), channel_id=1, source_target_pairs={{0,1},{1,0},{2,3},{3,2},{4,5},{5,4},{6,7},{7,6},{8,9},{9,8},{10,11... | collective-permute-start | bytes 98312 | tf_op jit(solution)/shard_map/ppermute | solution.py:704
  40.2 4.4 %collective-permute-start.7 = (f32[15,16,128]{2,1,0:T(8,128)S(1)}, f32[15,16,128]{2,1,0:T(8,128)S(1)}, u32[]{:S(2)}, u32[]{:S(2)}) collective-permute-start(f32[15,16,128]{2,1,0:T(8,128)S(1)} %low_widen.1.own_ref), channel_id=1, source_target_pairs={{0,240},{16,32},{32,16},{48,64},{64,48},{80,96},{96,80},{112,128},... | collective-permute-start | bytes 368648 | tf_op jit(solution)/shard_map/ppermute | solution.py:704
  41.5 3.6 %collective-permute-start.6 = (f32[15,16,128]{2,1,0:T(8,128)S(1)}, f32[15,16,128]{2,1,0:T(8,128)S(1)}, u32[]{:S(2)}, u32[]{:S(2)}) collective-permute-start(f32[15,16,128]{2,1,0:T(8,128)S(1)} %low_widen.1.own_ref), channel_id=1, source_target_pairs={{0,16},{16,0},{32,48},{48,32},{64,80},{80,64},{96,112},{112,96},{1... | collective-permute-start | bytes 368648 | tf_op jit(solution)/shard_map/ppermute | solution.py:704

commit v5 on v4

--- a/solution.py
+++ b/solution.py
@@ -13,7 +13,7 @@
 HALF = ((0, 0), (0, 1), (1, -1), (1, 0), (1, 1))
 FULL = tuple((dy, dz) for dy in (-1, 0, 1) for dz in (-1, 0, 1))
 HI = lax.Precision.HIGHEST
-BY = (4, 3, 8, 6, 2, 2, 7, 5)
+BY = (5, 5, 8, 6, 2, 2, 7, 5)
 
 
 def neg(s):
@@ -428,11 +428,8 @@
         ]
 
     rows_loop(2, ROWS - 2, second, BY[2])
-    order = depth_order(True)
     for p in range(2):
-        part = U2[X0 : X0 + 16, p, 0:8].reshape(128, 128)
-        part = jnp.dot(part, order, precision=HI, preferred_element_type=F32)
-        fine_ref[:, pl.ds(p, 8, stride=2), :] = part.reshape(16, 8, 128)
+        fine_ref[:, p] = U2[X0 : X0 + 16, p, 0:8]
 
     def residual(r):
         around = neighbours(U2, r)
@@ -517,8 +514,8 @@
     UN[0] = r64(UN[6])
     UN[8] = r64(UN[2])
     for i in range(4):
-        mid_ref[i] = UN[i + 3, 0:8, 0:64]
-        mid_ref[i + 4] = r64(UN[i + 1])[0:8, 0:64]
+        mid_ref[i] = UN[i + 3, 0:8]
+        mid_ref[i + 4] = UN[i + 1, 0:8]
 
     def mid_residual(a):
         return [(UM, a + 1, MS[a] - a1(UN, a))]
@@ -631,6 +628,16 @@
     low_ref[60:64] = jnp.zeros((4, 128), F32)
 
 
+def finish_kernel(fine_in, mid_in, fine_ref, mid_ref):
+    order = depth_order(True)
+    for p in range(2):
+        part = jnp.dot(fine_in[:, p].reshape(128, 128), order, precision=HI, preferred_element_type=F32)
+        fine_ref[:, pl.ds(p, 8, stride=2), :] = part.reshape(16, 8, 128)
+    for i in range(4):
+        mid_ref[i] = mid_in[i, :, 0:64]
+        mid_ref[i + 4] = pltpu.roll(mid_in[i + 4], 64, 1)[:, 0:64]
+
+
 def low_widen_kernel(pos_ref, own_ref, swap_ref, other_ref, wide_ref):
     even = pos_ref[5] == 0
     for j in range(15):
@@ -701,7 +708,8 @@
     n = lax.axis_size(axis)
     swap = [(i, i ^ 1) for i in range(n)]
     other = [(i, (i - 1 if i % 2 == 0 else i + 1) % n) for i in range(n)]
-    return lax.ppermute(to_swap, axis, swap), lax.ppermute(to_other, axis, other)
+    far = lax.ppermute(to_other, axis, other)
+    return lax.ppermute(to_swap, axis, swap), far
 
 
 def per_device(material, velocity, density, right_side):
@@ -763,8 +771,8 @@
         in_specs=[smem, smem] + [vmem] * (2 + count),
         out_specs=[vmem] * (3 + count),
         out_shape=[
-            shape((16, 16, 128), F32),
-            shape((8, 8, 64), F32),
+            shape((16, 2, 8, 128), F32),
+            shape((8, 8, 128), F32),
             shape((64, 128), F32),
         ] + carried,
         input_output_aliases={4 + n: 3 + n for n in range(count)},
@@ -786,6 +794,14 @@
         compiler_params=params,
         name="low_widen",
     )(position, sent, *near)
+    fine, mid = pl.pallas_call(
+        finish_kernel,
+        in_specs=[vmem] * 2,
+        out_specs=[vmem] * 2,
+        out_shape=(shape((16, 16, 128), F32), shape((8, 8, 64), F32)),
+        compiler_params=params,
+        name="finish",
+    )(fine, mid)
     near = partners("gx", low, low)
     coarse = pl.pallas_call(
         low_kernel,

time: 47.7 us -> 47 us (0.985)
  waiting for transfers between devices: 7.76 us -> 6.84 us
    ppermute x8, waiting for transfers between devices: 7.76 us -> 6.84 us  [the longest x4 4.41 us: partners(): far = lax.ppermute(to_other, axis, other)]
    pallas_call x0 -> x1, Pallas kernels: none -> 0.92 us  [per_device(): pl.pallas_call(finish_kernel, in_specs=[vmem] * 2, out_specs=[vmem] * 2,...]
    pallas_call x1, Pallas kernels: 8.15 us -> 7.39 us  [per_device(): pl.pallas_call(main_kernel, in_specs=[smem, smem] + [vmem] * (2 + count),...]
  transfers between devices with their start and end apart: 8 -> 8, of which waited for: 6 -> 5; matrix products, arithmetic and copies ran while one was open for 2% -> 2% of each run, Pallas kernels for 5% -> 7%
where the time goes in v5:
time: 47 us; the launch traced here: 46.3 us
  starting transfers between devices  21.6 us (46%)
  Pallas kernels  14.5 us (31%)
  waiting for transfers between devices  6.84 us (15%)
  other arithmetic  1.66 us (4%)
  local copies, waits for them, and re-layouts  0.99 us (2%)
  between operations  0.71 us (2%)
    ppermute x4, starting transfers between devices, partners(): far = lax.ppermute(to_other, axis, other)  14.2 us
    ppermute x4, starting transfers between devices, partners(): return (lax.ppermute(to_swap, axis, swap), far)  7.44 us
    pallas_call x1, Pallas kernels, per_device(): pl.pallas_call(main_kernel, in_specs=[smem, smem] + [vmem] * (2 + count),...  7.39 us
    ppermute x4, waiting for transfers between devices, partners(): far = lax.ppermute(to_other, axis, other)  4.41 us
    ppermute x4, waiting for transfers between devices, partners(): return (lax.ppermute(to_swap, axis, swap), far)  2.43 us
    pallas_call x1, Pallas kernels, per_device(): pl.pallas_call(inner_kernel, in_specs=[smem, smem, vmem], out_specs=[vmem...  2.27 us
    pallas_call x1, Pallas kernels, per_device(): pl.pallas_call(low_kernel, in_specs=[smem] + [vmem] * 3, out_specs=vmem,...  1.85 us
  transfers between devices with their start and end apart: 8, of which 5 were waited for; matrix products, arithmetic and copies ran while one was open for 2% of the time, Pallas kernels for 7%

profile of v5, /device:TPU:1, one launch (start us, length us, event | category | flops | bytes accessed | tf_op | source)
XLA Modules:
  0.0 46.3 jit_solution(6350676794032835572)
XLA Ops:
  0.7 0.9 %convert_element_type.2.mat_ref = f32[16,16,128]{2,1,0:T(8,128)S(1)} convert(s32[16,16,128]{2,1,0:T(8,128)} %param.4) | non-fusion elementwise | flops 32768 | bytes 262144 | tf_op jit(solution)/shard_map/convert_element_type | solution.py:738
  1.6 0.1 stack.35.pos_ref
  1.7 0.0 copy-start
  1.7 0.9 %copy-done = f32[16,16,128]{2,1,0:T(8,128)S(1)} copy-done((f32[16,16,128]{2,1,0:T(8,128)S(1)}, f32[16,16,128]{2,1,0:T(8,128)}, u32[]{:S(2)}) %copy-start) | copy-done | bytes 131096
  2.6 0.8 %pack.1 = (f32[16,4,8,128]{3,2,1,0:T(8,128)S(1)}, f32[8,40,128]{2,1,0:T(8,128)S(1)}, f32[8,40,128]{2,1,0:T(8,128)S(1)}) custom-call(s32[6]{0:T(128)S(1)} %stack.35.pos_ref, f32[16,16,128]{2,1,0:T(8,128)S(1)} %convert_element_type.2.mat_ref, f32[16,16,128]{2,1,0:T(8,128)S(1)} %copy-done), custom_call_target="tpu_custom_call" | custom-call | tf_op jit(solution)/shard_map/pack/pallas_call | solution.py:731
  3.4 2.1 %collective-permute-start = (f32[8,40,128]{2,1,0:T(8,128)S(1)}, f32[8,40,128]{2,1,0:T(8,128)S(1)}, u32[]{:S(2)}, u32[]{:S(2)}) collective-permute-start(f32[8,40,128]{2,1,0:T(8,128)S(1)} %get-tuple-element.52), channel_id=1, source_target_pairs={{0,1},{1,0},{2,3},{3,2},{4,5},{5,4},{6,7},{7,6},{8,9},{9,8},{10,11... | collective-permute-start | bytes 491528 | tf_op jit(solution)/shard_map/ppermute | solution.py:712
  5.5 4.3 %collective-permute-start.1 = (f32[8,40,128]{2,1,0:T(8,128)S(1)}, f32[8,40,128]{2,1,0:T(8,128)S(1)}, u32[]{:S(2)}, u32[]{:S(2)}) collective-permute-start(f32[8,40,128]{2,1,0:T(8,128)S(1)} %get-tuple-element.53), channel_id=1, source_target_pairs={{0,15},{1,2},{2,1},{3,4},{4,3},{5,6},{6,5},{7,8},{8,7},{9,10},{10,... | collective-permute-start | bytes 491528 | tf_op jit(solution)/shard_map/ppermute | solution.py:711
  9.8 0.7 %pad_maximum_fusion.tab_ref = f32[16]{0:T(128)S(1)} fusion(f32[8]{0:T(128)} %param.5, f32[8]{0:T(128)} %param.6), kind=kLoop, calls=%fused_computation | loop fusion | flops 16 | bytes 128 | tf_op jit(solution)/shard_map/concatenate | solution.py:730
  10.6 0.0 collective-permute-done.swap_ref
  10.6 2.5 %collective-permute-done.1.other_ref = f32[8,40,128]{2,1,0:T(8,128)S(1)} collective-permute-done((f32[8,40,128]{2,1,0:T(8,128)S(1)}, f32[8,40,128]{2,1,0:T(8,128)S(1)}, u32[]{:S(2)}, u32[]{:S(2)}) %collective-permute-start.1) | collective-permute-done | bytes 163872 | tf_op jit(solution)/shard_map/ppermute | solution.py:711
  13.0 0.7 %widen.1 = (f32[16,4,16,128]{3,2,1,0:T(8,128)S(1)}, f32[10,4,16,128]{3,2,1,0:T(8,128)S(1)}, f32[10,4,16,128]{3,2,1,0:T(8,128)S(1)}) custom-call(s32[6]{0:T(128)S(1)} %stack.35.pos_ref, f32[16,4,8,128]{3,2,1,0:T(8,128)S(1)} %get-tuple-element.51.own_ref, f32[8,40,128]{2,1,0:T(8,128)S(1)} %collective-permute-done.swap_ref, ...), custom_call_target="tpu_custom_call" | custom-call | tf_op jit(solution)/shard_map/widen/pallas_call | solution.py:740
  13.7 4.1 %collective-permute-start.3 = (f32[10,4,16,128]{3,2,1,0:T(8,128)S(1)}, f32[10,4,16,128]{3,2,1,0:T(8,128)S(1)}, u32[]{:S(2)}, u32[]{:S(2)}) collective-permute-start(f32[10,4,16,128]{3,2,1,0:T(8,128)S(1)} %get-tuple-element.75), channel_id=1, source_target_pairs={{0,240},{16,32},{32,16},{48,64},{64,48},{80,96},{96,80},{112,128},... | collective-permute-start | bytes 983048 | tf_op jit(solution)/shard_map/ppermute | solution.py:711
  17.8 2.3 %inner.1 = (f32[33,2,16,128]{3,2,1,0:T(8,128)S(1)}, f32[33,2,16,128]{3,2,1,0:T(8,128)S(1)}, f32[33,2,16,128]{3,2,1,0:T(8,128)S(1)}, f32[33,16,128]{2,1,0:T(8,128...) custom-call(f32[16]{0:T(128)S(1)} %pad_maximum_fusion.tab_ref, ...), custom_call_target="tpu_custom_call" | custom-call | flops 20000000 | bytes 8000000 | tf_op jit(solution)/shard_map/inner/pallas_call | solution.py:758
  20.0 2.7 %collective-permute-start.2 = (f32[10,4,16,128]{3,2,1,0:T(8,128)S(1)}, f32[10,4,16,128]{3,2,1,0:T(8,128)S(1)}, u32[]{:S(2)}, u32[]{:S(2)}) collective-permute-start(f32[10,4,16,128]{3,2,1,0:T(8,128)S(1)} %get-tuple-element.74), channel_id=1, source_target_pairs={{0,16},{16,0},{32,48},{48,32},{64,80},{80,64},{96,112},{112,96},{1... | collective-permute-start | bytes 983048 | tf_op jit(solution)/shard_map/ppermute | solution.py:712
  22.7 0.1 collective-permute-done.3.other_ref
  22.8 1.1 %collective-permute-done.2.swap_ref = f32[10,4,16,128]{3,2,1,0:T(8,128)S(1)} collective-permute-done((f32[10,4,16,128]{3,2,1,0:T(8,128)S(1)}, f32[10,4,16,128]{3,2,1,0:T(8,128)S(1)}, u32[]{:S(2)}, u32[]{:S(2)}) %collective-permute-start.2) | collective-permute-done | bytes 327712 | tf_op jit(solution)/shard_map/ppermute | solution.py:712
  23.9 7.4 %levels.1 = (f32[16,2,8,128]{3,2,1,0:T(8,128)S(1)}, f32[8,8,128]{2,1,0:T(8,128)S(1)}, f32[64,128]{1,0:T(8,128)S(1)}, f32[33,2,16,128]{3,2,1,0:T(8,128)S(1)}, f32...) custom-call(f32[16]{0:T(128)S(1)} %pad_maximum_fusion.tab_ref, ...), custom_call_target="tpu_custom_call", output_to_operand_aliasing={{3}: (4, {}), {4}: (5, {}), {5}: (6, {}), {6}: (7, {}), {7}... | custom-call | tf_op jit(solution)/shard_map/levels/pallas_call | solution.py:769
  31.3 4.4 %collective-permute-start.5 = (f32[64,128]{1,0:T(8,128)S(1)}, f32[64,128]{1,0:T(8,128)S(1)}, u32[]{:S(2)}, u32[]{:S(2)}) collective-permute-start(f32[64,128]{1,0:T(8,128)S(1)} %get-tuple-element.98.own_ref), channel_id=1, source_target_pairs={{0,15},{1,2},{2,1},{3,4},{4,3},{5,6},{6,5},{7,8},{8,7},{9,10},{10,... | collective-permute-start | bytes 98312 | tf_op jit(solution)/shard_map/ppermute | solution.py:711
  35.7 0.0 collective-permute-start.4
  35.7 1.8 %collective-permute-done.5.other_ref = f32[64,128]{1,0:T(8,128)S(1)} collective-permute-done((f32[64,128]{1,0:T(8,128)S(1)}, f32[64,128]{1,0:T(8,128)S(1)}, u32[]{:S(2)}, u32[]{:S(2)}) %collective-permute-start.5) | collective-permute-done | bytes 32800 | tf_op jit(solution)/shard_map/ppermute | solution.py:711
  37.5 1.2 %collective-permute-done.4.swap_ref = f32[64,128]{1,0:T(8,128)S(1)} collective-permute-done((f32[64,128]{1,0:T(8,128)S(1)}, f32[64,128]{1,0:T(8,128)S(1)}, u32[]{:S(2)}, u32[]{:S(2)}) %collective-permute-start.4) | collective-permute-done | bytes 32800 | tf_op jit(solution)/shard_map/ppermute | solution.py:712
  38.8 0.6 %low_widen.1.own_ref = f32[15,16,128]{2,1,0:T(8,128)S(1)} custom-call(s32[6]{0:T(128)S(1)} %stack.35.pos_ref, f32[64,128]{1,0:T(8,128)S(1)} %get-tuple-element.98.own_ref, f32[64,128]{1,0:T(8,128)S(1)} %collective-permute-done.4.swap_ref, f32[64,128]{1,0:T(8,128)S(1)} %collective-permute-done.5.other_ref), custom_call_target="tpu_custom_call" | custom-call | tf_op jit(solution)/shard_map/low_widen/pallas_call | solution.py:789
  39.3 1.5 %collective-permute-start.7 = (f32[15,16,128]{2,1,0:T(8,128)S(1)}, f32[15,16,128]{2,1,0:T(8,128)S(1)}, u32[]{:S(2)}, u32[]{:S(2)}) collective-permute-start(f32[15,16,128]{2,1,0:T(8,128)S(1)} %low_widen.1.own_ref), channel_id=1, source_target_pairs={{0,240},{16,32},{32,16},{48,64},{64,48},{80,96},{96,80},{112,128},... | collective-permute-start | bytes 368648 | tf_op jit(solution)/shard_map/ppermute | solution.py:711
  40.9 2.6 %collective-permute-start.6 = (f32[15,16,128]{2,1,0:T(8,128)S(1)}, f32[15,16,128]{2,1,0:T(8,128)S(1)}, u32[]{:S(2)}, u32[]{:S(2)}) collective-permute-start(f32[15,16,128]{2,1,0:T(8,128)S(1)} %low_widen.1.own_ref), channel_id=1, source_target_pairs={{0,16},{16,0},{32,48},{48,32},{64,80},{80,64},{96,112},{112,96},{1... | collective-permute-start | bytes 368648 | tf_op jit(solution)/shard_map/ppermute | solution.py:712
  43.5 0.9 %finish.1 = (f32[16,16,128]{2,1,0:T(8,128)}, f32[8,8,64]{2,1,0:T(8,128)}) custom-call(f32[16,2,8,128]{3,2,1,0:T(8,128)S(1)} %get-tuple-element.94.fine_in, f32[8,8,128]{2,1,0:T(8,128)S(1)} %get-tuple-element.95.mid_in), custom_call_target="tpu_custom_call" | custom-call | tf_op jit(solution)/shard_map/finish/pallas_call | solution.py:797
  44.4 0.0 collective-permute-done.7.other_ref
  44.4 0.0 collective-permute-done.6.swap_ref
  44.5 1.8 %coarse.1 = f32[4,4,32]{2,1,0:T(4,128)} custom-call(s32[6]{0:T(128)S(1)} %stack.35.pos_ref, f32[15,16,128]{2,1,0:T(8,128)S(1)} %low_widen.1.own_ref, f32[15,16,128]{2,1,0:T(8,128)S(1)} %collective-permute-done.6.swap_ref, f32[15,16,128]{2,1,0:T(8,128)S(1)} %collective-permute-done.7.other_ref), custom_call_target="tpu_custom_call" | custom-call | tf_op jit(solution)/shard_map/coarse/pallas_call | solution.py:806
Async XLA Ops:
  1.7 0.9 %copy-start = (f32[16,16,128]{2,1,0:T(8,128)S(1)}, f32[16,16,128]{2,1,0:T(8,128)}, u32[]{:S(2)}) copy-start(f32[16,16,128]{2,1,0:T(8,128)} %rhs_ref.1) | copy-start | bytes 393220
  3.4 7.1 %collective-permute-start = (f32[8,40,128]{2,1,0:T(8,128)S(1)}, f32[8,40,128]{2,1,0:T(8,128)S(1)}, u32[]{:S(2)}, u32[]{:S(2)}) collective-permute-start(f32[8,40,128]{2,1,0:T(8,128)S(1)} %get-tuple-element.52), channel_id=1, source_target_pairs={{0,1},{1,0},{2,3},{3,2},{4,5},{5,4},{6,7},{7,6},{8,9},{9,8},{10,11... | collective-permute-start | bytes 491528 | tf_op jit(solution)/shard_map/ppermute | solution.py:712
  5.5 7.5 %collective-permute-start.1 = (f32[8,40,128]{2,1,0:T(8,128)S(1)}, f32[8,40,128]{2,1,0:T(8,128)S(1)}, u32[]{:S(2)}, u32[]{:S(2)}) collective-permute-start(f32[8,40,128]{2,1,0:T(8,128)S(1)} %get-tuple-element.53), channel_id=1, source_target_pairs={{0,15},{1,2},{2,1},{3,4},{4,3},{5,6},{6,5},{7,8},{8,7},{9,10},{10,... | collective-permute-start | bytes 491528 | tf_op jit(solution)/shard_map/ppermute | solution.py:711
  13.7 9.1 %collective-permute-start.3 = (f32[10,4,16,128]{3,2,1,0:T(8,128)S(1)}, f32[10,4,16,128]{3,2,1,0:T(8,128)S(1)}, u32[]{:S(2)}, u32[]{:S(2)}) collective-permute-start(f32[10,4,16,128]{3,2,1,0:T(8,128)S(1)} %get-tuple-element.75), channel_id=1, source_target_pairs={{0,240},{16,32},{32,16},{48,64},{64,48},{80,96},{96,80},{112,128},... | collective-permute-start | bytes 983048 | tf_op jit(solution)/shard_map/ppermute | solution.py:711
  20.0 3.9 %collective-permute-start.2 = (f32[10,4,16,128]{3,2,1,0:T(8,128)S(1)}, f32[10,4,16,128]{3,2,1,0:T(8,128)S(1)}, u32[]{:S(2)}, u32[]{:S(2)}) collective-permute-start(f32[10,4,16,128]{3,2,1,0:T(8,128)S(1)} %get-tuple-element.74), channel_id=1, source_target_pairs={{0,16},{16,0},{32,48},{48,32},{64,80},{80,64},{96,112},{112,96},{1... | collective-permute-start | bytes 983048 | tf_op jit(solution)/shard_map/ppermute | solution.py:712
  31.3 6.2 %collective-permute-start.5 = (f32[64,128]{1,0:T(8,128)S(1)}, f32[64,128]{1,0:T(8,128)S(1)}, u32[]{:S(2)}, u32[]{:S(2)}) collective-permute-start(f32[64,128]{1,0:T(8,128)S(1)} %get-tuple-element.98.own_ref), channel_id=1, source_target_pairs={{0,15},{1,2},{2,1},{3,4},{4,3},{5,6},{6,5},{7,8},{8,7},{9,10},{10,... | collective-permute-start | bytes 98312 | tf_op jit(solution)/shard_map/ppermute | solution.py:711
  35.7 3.1 %collective-permute-start.4 = (f32[64,128]{1,0:T(8,128)S(1)}, f32[64,128]{1,0:T(8,128)S(1)}, u32[]{:S(2)}, u32[]{:S(2)}) collective-permute-start(f32[64,128]{1,0:T(8,128)S(1)} %get-tuple-element.98.own_ref), channel_id=1, source_target_pairs={{0,1},{1,0},{2,3},{3,2},{4,5},{5,4},{6,7},{7,6},{8,9},{9,8},{10,11... | collective-permute-start | bytes 98312 | tf_op jit(solution)/shard_map/ppermute | solution.py:712
  39.3 5.1 %collective-permute-start.7 = (f32[15,16,128]{2,1,0:T(8,128)S(1)}, f32[15,16,128]{2,1,0:T(8,128)S(1)}, u32[]{:S(2)}, u32[]{:S(2)}) collective-permute-start(f32[15,16,128]{2,1,0:T(8,128)S(1)} %low_widen.1.own_ref), channel_id=1, source_target_pairs={{0,240},{16,32},{32,16},{48,64},{64,48},{80,96},{96,80},{112,128},... | collective-permute-start | bytes 368648 | tf_op jit(solution)/shard_map/ppermute | solution.py:711
  40.9 3.6 %collective-permute-start.6 = (f32[15,16,128]{2,1,0:T(8,128)S(1)}, f32[15,16,128]{2,1,0:T(8,128)S(1)}, u32[]{:S(2)}, u32[]{:S(2)}) collective-permute-start(f32[15,16,128]{2,1,0:T(8,128)S(1)} %low_widen.1.own_ref), channel_id=1, source_target_pairs={{0,16},{16,0},{32,48},{48,32},{64,80},{80,64},{96,112},{112,96},{1... | collective-permute-start | bytes 368648 | tf_op jit(solution)/shard_map/ppermute | solution.py:712

commit v6 on v5

--- a/solution.py
+++ b/solution.py
@@ -13,7 +13,7 @@
 HALF = ((0, 0), (0, 1), (1, -1), (1, 0), (1, 1))
 FULL = tuple((dy, dz) for dy in (-1, 0, 1) for dz in (-1, 0, 1))
 HI = lax.Precision.HIGHEST
-BY = (5, 5, 8, 6, 2, 2, 7, 5)
+BY = (5, 5, 15, 9, 2, 4, 7, 5)
 
 
 def neg(s):

time: 47 us -> 46.8 us (level)
  no operation moved by 1% of the time
where the time goes in v6:
time: 46.8 us; the launch traced here: 46.2 us
  starting transfers between devices  21.6 us (46%)
  Pallas kernels  14.3 us (31%)
  waiting for transfers between devices  6.83 us (15%)
  other arithmetic  1.66 us (4%)
  local copies, waits for them, and re-layouts  0.99 us (2%)
  between operations  0.71 us (2%)
    ppermute x4, starting transfers between devices, partners(): far = lax.ppermute(to_other, axis, other)  14.2 us
    ppermute x4, starting transfers between devices, partners(): return (lax.ppermute(to_swap, axis, swap), far)  7.44 us
    pallas_call x1, Pallas kernels, per_device(): pl.pallas_call(main_kernel, in_specs=[smem, smem] + [vmem] * (2 + count),...  7.22 us
    ppermute x4, waiting for transfers between devices, partners(): far = lax.ppermute(to_other, axis, other)  4.41 us
    ppermute x4, waiting for transfers between devices, partners(): return (lax.ppermute(to_swap, axis, swap), far)  2.42 us
    pallas_call x1, Pallas kernels, per_device(): pl.pallas_call(inner_kernel, in_specs=[smem, smem, vmem], out_specs=[vmem...  2.27 us
    pallas_call x1, Pallas kernels, per_device(): pl.pallas_call(low_kernel, in_specs=[smem] + [vmem] * 3, out_specs=vmem,...  1.85 us
  transfers between devices with their start and end apart: 8, of which 5 were waited for; matrix products, arithmetic and copies ran while one was open for 2% of the time, Pallas kernels for 7%

profile of v6, /device:TPU:1, one launch (start us, length us, event | category | flops | bytes accessed | tf_op | source)
XLA Modules:
  0.0 46.2 jit_solution(1577094397804743005)
XLA Ops:
  0.7 0.9 %convert_element_type.2.mat_ref = f32[16,16,128]{2,1,0:T(8,128)S(1)} convert(s32[16,16,128]{2,1,0:T(8,128)} %param.4) | non-fusion elementwise | flops 32768 | bytes 262144 | tf_op jit(solution)/shard_map/convert_element_type | solution.py:738
  1.6 0.1 stack.35.pos_ref
  1.7 0.0 copy-start
  1.7 0.9 %copy-done = f32[16,16,128]{2,1,0:T(8,128)S(1)} copy-done((f32[16,16,128]{2,1,0:T(8,128)S(1)}, f32[16,16,128]{2,1,0:T(8,128)}, u32[]{:S(2)}) %copy-start) | copy-done | bytes 131096
  2.6 0.8 %pack.1 = (f32[16,4,8,128]{3,2,1,0:T(8,128)S(1)}, f32[8,40,128]{2,1,0:T(8,128)S(1)}, f32[8,40,128]{2,1,0:T(8,128)S(1)}) custom-call(s32[6]{0:T(128)S(1)} %stack.35.pos_ref, f32[16,16,128]{2,1,0:T(8,128)S(1)} %convert_element_type.2.mat_ref, f32[16,16,128]{2,1,0:T(8,128)S(1)} %copy-done), custom_call_target="tpu_custom_call" | custom-call | tf_op jit(solution)/shard_map/pack/pallas_call | solution.py:731
  3.4 2.1 %collective-permute-start = (f32[8,40,128]{2,1,0:T(8,128)S(1)}, f32[8,40,128]{2,1,0:T(8,128)S(1)}, u32[]{:S(2)}, u32[]{:S(2)}) collective-permute-start(f32[8,40,128]{2,1,0:T(8,128)S(1)} %get-tuple-element.52), channel_id=1, source_target_pairs={{0,1},{1,0},{2,3},{3,2},{4,5},{5,4},{6,7},{7,6},{8,9},{9,8},{10,11... | collective-permute-start | bytes 491528 | tf_op jit(solution)/shard_map/ppermute | solution.py:712
  5.5 4.3 %collective-permute-start.1 = (f32[8,40,128]{2,1,0:T(8,128)S(1)}, f32[8,40,128]{2,1,0:T(8,128)S(1)}, u32[]{:S(2)}, u32[]{:S(2)}) collective-permute-start(f32[8,40,128]{2,1,0:T(8,128)S(1)} %get-tuple-element.53), channel_id=1, source_target_pairs={{0,15},{1,2},{2,1},{3,4},{4,3},{5,6},{6,5},{7,8},{8,7},{9,10},{10,... | collective-permute-start | bytes 491528 | tf_op jit(solution)/shard_map/ppermute | solution.py:711
  9.8 0.7 %pad_maximum_fusion.tab_ref = f32[16]{0:T(128)S(1)} fusion(f32[8]{0:T(128)} %param.5, f32[8]{0:T(128)} %param.6), kind=kLoop, calls=%fused_computation | loop fusion | flops 16 | bytes 128 | tf_op jit(solution)/shard_map/concatenate | solution.py:730
  10.6 0.0 collective-permute-done.swap_ref
  10.6 2.5 %collective-permute-done.1.other_ref = f32[8,40,128]{2,1,0:T(8,128)S(1)} collective-permute-done((f32[8,40,128]{2,1,0:T(8,128)S(1)}, f32[8,40,128]{2,1,0:T(8,128)S(1)}, u32[]{:S(2)}, u32[]{:S(2)}) %collective-permute-start.1) | collective-permute-done | bytes 163872 | tf_op jit(solution)/shard_map/ppermute | solution.py:711
  13.0 0.7 %widen.1 = (f32[16,4,16,128]{3,2,1,0:T(8,128)S(1)}, f32[10,4,16,128]{3,2,1,0:T(8,128)S(1)}, f32[10,4,16,128]{3,2,1,0:T(8,128)S(1)}) custom-call(s32[6]{0:T(128)S(1)} %stack.35.pos_ref, f32[16,4,8,128]{3,2,1,0:T(8,128)S(1)} %get-tuple-element.51.own_ref, f32[8,40,128]{2,1,0:T(8,128)S(1)} %collective-permute-done.swap_ref, ...), custom_call_target="tpu_custom_call" | custom-call | tf_op jit(solution)/shard_map/widen/pallas_call | solution.py:740
  13.7 4.1 %collective-permute-start.3 = (f32[10,4,16,128]{3,2,1,0:T(8,128)S(1)}, f32[10,4,16,128]{3,2,1,0:T(8,128)S(1)}, u32[]{:S(2)}, u32[]{:S(2)}) collective-permute-start(f32[10,4,16,128]{3,2,1,0:T(8,128)S(1)} %get-tuple-element.75), channel_id=1, source_target_pairs={{0,240},{16,32},{32,16},{48,64},{64,48},{80,96},{96,80},{112,128},... | collective-permute-start | bytes 983048 | tf_op jit(solution)/shard_map/ppermute | solution.py:711
  17.8 2.3 %inner.1 = (f32[33,2,16,128]{3,2,1,0:T(8,128)S(1)}, f32[33,2,16,128]{3,2,1,0:T(8,128)S(1)}, f32[33,2,16,128]{3,2,1,0:T(8,128)S(1)}, f32[33,16,128]{2,1,0:T(8,128...) custom-call(f32[16]{0:T(128)S(1)} %pad_maximum_fusion.tab_ref, ...), custom_call_target="tpu_custom_call" | custom-call | flops 20000000 | bytes 8000000 | tf_op jit(solution)/shard_map/inner/pallas_call | solution.py:758
  20.0 2.7 %collective-permute-start.2 = (f32[10,4,16,128]{3,2,1,0:T(8,128)S(1)}, f32[10,4,16,128]{3,2,1,0:T(8,128)S(1)}, u32[]{:S(2)}, u32[]{:S(2)}) collective-permute-start(f32[10,4,16,128]{3,2,1,0:T(8,128)S(1)} %get-tuple-element.74), channel_id=1, source_target_pairs={{0,16},{16,0},{32,48},{48,32},{64,80},{80,64},{96,112},{112,96},{1... | collective-permute-start | bytes 983048 | tf_op jit(solution)/shard_map/ppermute | solution.py:712
  22.7 0.1 collective-permute-done.3.other_ref
  22.8 1.1 %collective-permute-done.2.swap_ref = f32[10,4,16,128]{3,2,1,0:T(8,128)S(1)} collective-permute-done((f32[10,4,16,128]{3,2,1,0:T(8,128)S(1)}, f32[10,4,16,128]{3,2,1,0:T(8,128)S(1)}, u32[]{:S(2)}, u32[]{:S(2)}) %collective-permute-start.2) | collective-permute-done | bytes 327712 | tf_op jit(solution)/shard_map/ppermute | solution.py:712
  23.9 7.2 %levels.1 = (f32[16,2,8,128]{3,2,1,0:T(8,128)S(1)}, f32[8,8,128]{2,1,0:T(8,128)S(1)}, f32[64,128]{1,0:T(8,128)S(1)}, f32[33,2,16,128]{3,2,1,0:T(8,128)S(1)}, f32...) custom-call(f32[16]{0:T(128)S(1)} %pad_maximum_fusion.tab_ref, ...), custom_call_target="tpu_custom_call", output_to_operand_aliasing={{3}: (4, {}), {4}: (5, {}), {5}: (6, {}), {6}: (7, {}), {7}... | custom-call | tf_op jit(solution)/shard_map/levels/pallas_call | solution.py:769
  31.2 4.4 %collective-permute-start.5 = (f32[64,128]{1,0:T(8,128)S(1)}, f32[64,128]{1,0:T(8,128)S(1)}, u32[]{:S(2)}, u32[]{:S(2)}) collective-permute-start(f32[64,128]{1,0:T(8,128)S(1)} %get-tuple-element.98.own_ref), channel_id=1, source_target_pairs={{0,15},{1,2},{2,1},{3,4},{4,3},{5,6},{6,5},{7,8},{8,7},{9,10},{10,... | collective-permute-start | bytes 98312 | tf_op jit(solution)/shard_map/ppermute | solution.py:711
  35.5 0.0 collective-permute-start.4
  35.5 1.8 %collective-permute-done.5.other_ref = f32[64,128]{1,0:T(8,128)S(1)} collective-permute-done((f32[64,128]{1,0:T(8,128)S(1)}, f32[64,128]{1,0:T(8,128)S(1)}, u32[]{:S(2)}, u32[]{:S(2)}) %collective-permute-start.5) | collective-permute-done | bytes 32800 | tf_op jit(solution)/shard_map/ppermute | solution.py:711
  37.3 1.2 %collective-permute-done.4.swap_ref = f32[64,128]{1,0:T(8,128)S(1)} collective-permute-done((f32[64,128]{1,0:T(8,128)S(1)}, f32[64,128]{1,0:T(8,128)S(1)}, u32[]{:S(2)}, u32[]{:S(2)}) %collective-permute-start.4) | collective-permute-done | bytes 32800 | tf_op jit(solution)/shard_map/ppermute | solution.py:712
  38.6 0.6 %low_widen.1.own_ref = f32[15,16,128]{2,1,0:T(8,128)S(1)} custom-call(s32[6]{0:T(128)S(1)} %stack.35.pos_ref, f32[64,128]{1,0:T(8,128)S(1)} %get-tuple-element.98.own_ref, f32[64,128]{1,0:T(8,128)S(1)} %collective-permute-done.4.swap_ref, f32[64,128]{1,0:T(8,128)S(1)} %collective-permute-done.5.other_ref), custom_call_target="tpu_custom_call" | custom-call | tf_op jit(solution)/shard_map/low_widen/pallas_call | solution.py:789
  39.2 1.5 %collective-permute-start.7 = (f32[15,16,128]{2,1,0:T(8,128)S(1)}, f32[15,16,128]{2,1,0:T(8,128)S(1)}, u32[]{:S(2)}, u32[]{:S(2)}) collective-permute-start(f32[15,16,128]{2,1,0:T(8,128)S(1)} %low_widen.1.own_ref), channel_id=1, source_target_pairs={{0,240},{16,32},{32,16},{48,64},{64,48},{80,96},{96,80},{112,128},... | collective-permute-start | bytes 368648 | tf_op jit(solution)/shard_map/ppermute | solution.py:711
  40.7 2.6 %collective-permute-start.6 = (f32[15,16,128]{2,1,0:T(8,128)S(1)}, f32[15,16,128]{2,1,0:T(8,128)S(1)}, u32[]{:S(2)}, u32[]{:S(2)}) collective-permute-start(f32[15,16,128]{2,1,0:T(8,128)S(1)} %low_widen.1.own_ref), channel_id=1, source_target_pairs={{0,16},{16,0},{32,48},{48,32},{64,80},{80,64},{96,112},{112,96},{1... | collective-permute-start | bytes 368648 | tf_op jit(solution)/shard_map/ppermute | solution.py:712
  43.3 0.9 %finish.1 = (f32[16,16,128]{2,1,0:T(8,128)}, f32[8,8,64]{2,1,0:T(8,128)}) custom-call(f32[16,2,8,128]{3,2,1,0:T(8,128)S(1)} %get-tuple-element.94.fine_in, f32[8,8,128]{2,1,0:T(8,128)S(1)} %get-tuple-element.95.mid_in), custom_call_target="tpu_custom_call" | custom-call | tf_op jit(solution)/shard_map/finish/pallas_call | solution.py:797
  44.3 0.0 collective-permute-done.7.other_ref
  44.3 0.0 collective-permute-done.6.swap_ref
  44.3 1.8 %coarse.1 = f32[4,4,32]{2,1,0:T(4,128)} custom-call(s32[6]{0:T(128)S(1)} %stack.35.pos_ref, f32[15,16,128]{2,1,0:T(8,128)S(1)} %low_widen.1.own_ref, f32[15,16,128]{2,1,0:T(8,128)S(1)} %collective-permute-done.6.swap_ref, f32[15,16,128]{2,1,0:T(8,128)S(1)} %collective-permute-done.7.other_ref), custom_call_target="tpu_custom_call" | custom-call | tf_op jit(solution)/shard_map/coarse/pallas_call | solution.py:806
Async XLA Ops:
  1.7 0.9 %copy-start = (f32[16,16,128]{2,1,0:T(8,128)S(1)}, f32[16,16,128]{2,1,0:T(8,128)}, u32[]{:S(2)}) copy-start(f32[16,16,128]{2,1,0:T(8,128)} %rhs_ref.1) | copy-start | bytes 393220
  3.4 7.1 %collective-permute-start = (f32[8,40,128]{2,1,0:T(8,128)S(1)}, f32[8,40,128]{2,1,0:T(8,128)S(1)}, u32[]{:S(2)}, u32[]{:S(2)}) collective-permute-start(f32[8,40,128]{2,1,0:T(8,128)S(1)} %get-tuple-element.52), channel_id=1, source_target_pairs={{0,1},{1,0},{2,3},{3,2},{4,5},{5,4},{6,7},{7,6},{8,9},{9,8},{10,11... | collective-permute-start | bytes 491528 | tf_op jit(solution)/shard_map/ppermute | solution.py:712
  5.5 7.5 %collective-permute-start.1 = (f32[8,40,128]{2,1,0:T(8,128)S(1)}, f32[8,40,128]{2,1,0:T(8,128)S(1)}, u32[]{:S(2)}, u32[]{:S(2)}) collective-permute-start(f32[8,40,128]{2,1,0:T(8,128)S(1)} %get-tuple-element.53), channel_id=1, source_target_pairs={{0,15},{1,2},{2,1},{3,4},{4,3},{5,6},{6,5},{7,8},{8,7},{9,10},{10,... | collective-permute-start | bytes 491528 | tf_op jit(solution)/shard_map/ppermute | solution.py:711
  13.7 9.1 %collective-permute-start.3 = (f32[10,4,16,128]{3,2,1,0:T(8,128)S(1)}, f32[10,4,16,128]{3,2,1,0:T(8,128)S(1)}, u32[]{:S(2)}, u32[]{:S(2)}) collective-permute-start(f32[10,4,16,128]{3,2,1,0:T(8,128)S(1)} %get-tuple-element.75), channel_id=1, source_target_pairs={{0,240},{16,32},{32,16},{48,64},{64,48},{80,96},{96,80},{112,128},... | collective-permute-start | bytes 983048 | tf_op jit(solution)/shard_map/ppermute | solution.py:711
  20.0 3.9 %collective-permute-start.2 = (f32[10,4,16,128]{3,2,1,0:T(8,128)S(1)}, f32[10,4,16,128]{3,2,1,0:T(8,128)S(1)}, u32[]{:S(2)}, u32[]{:S(2)}) collective-permute-start(f32[10,4,16,128]{3,2,1,0:T(8,128)S(1)} %get-tuple-element.74), channel_id=1, source_target_pairs={{0,16},{16,0},{32,48},{48,32},{64,80},{80,64},{96,112},{112,96},{1... | collective-permute-start | bytes 983048 | tf_op jit(solution)/shard_map/ppermute | solution.py:712
  31.2 6.2 %collective-permute-start.5 = (f32[64,128]{1,0:T(8,128)S(1)}, f32[64,128]{1,0:T(8,128)S(1)}, u32[]{:S(2)}, u32[]{:S(2)}) collective-permute-start(f32[64,128]{1,0:T(8,128)S(1)} %get-tuple-element.98.own_ref), channel_id=1, source_target_pairs={{0,15},{1,2},{2,1},{3,4},{4,3},{5,6},{6,5},{7,8},{8,7},{9,10},{10,... | collective-permute-start | bytes 98312 | tf_op jit(solution)/shard_map/ppermute | solution.py:711
  35.5 3.1 %collective-permute-start.4 = (f32[64,128]{1,0:T(8,128)S(1)}, f32[64,128]{1,0:T(8,128)S(1)}, u32[]{:S(2)}, u32[]{:S(2)}) collective-permute-start(f32[64,128]{1,0:T(8,128)S(1)} %get-tuple-element.98.own_ref), channel_id=1, source_target_pairs={{0,1},{1,0},{2,3},{3,2},{4,5},{5,4},{6,7},{7,6},{8,9},{9,8},{10,11... | collective-permute-start | bytes 98312 | tf_op jit(solution)/shard_map/ppermute | solution.py:712
  39.2 5.1 %collective-permute-start.7 = (f32[15,16,128]{2,1,0:T(8,128)S(1)}, f32[15,16,128]{2,1,0:T(8,128)S(1)}, u32[]{:S(2)}, u32[]{:S(2)}) collective-permute-start(f32[15,16,128]{2,1,0:T(8,128)S(1)} %low_widen.1.own_ref), channel_id=1, source_target_pairs={{0,240},{16,32},{32,16},{48,64},{64,48},{80,96},{96,80},{112,128},... | collective-permute-start | bytes 368648 | tf_op jit(solution)/shard_map/ppermute | solution.py:711
  40.7 3.6 %collective-permute-start.6 = (f32[15,16,128]{2,1,0:T(8,128)S(1)}, f32[15,16,128]{2,1,0:T(8,128)S(1)}, u32[]{:S(2)}, u32[]{:S(2)}) collective-permute-start(f32[15,16,128]{2,1,0:T(8,128)S(1)} %low_widen.1.own_ref), channel_id=1, source_target_pairs={{0,16},{16,0},{32,48},{48,32},{64,80},{80,64},{96,112},{112,96},{1... | collective-permute-start | bytes 368648 | tf_op jit(solution)/shard_map/ppermute | solution.py:712
